TPU v7x, 256 devices: a whole 4x4x8 slice. The times are simulated.
256 devices in a mesh: gx: 2 (over y_hi), gy: 2 (over core), vert: 64 (over x, y_lo, z).
Axes of the slice: x: 4, y: 4 (y_hi: 2, y_lo: 2; y = y_hi * 2 + y_lo), z: 8, core: 2. Of those that a mesh axis runs over, the one named last changes fastest.
Arguments:
- distribution: float32 [8000, 64, 256], P('vert', 'gx', 'gy'), may hold values from 0 to 13, as said below
- collision_rate: float32 [64, 256], P('gx', 'gy'), may hold values from 0.05 to 0.9
Outputs:
- advanced: float32 [8000, 64, 256], P('vert', 'gx', 'gy')
Inputs may be any that keep to these rules, and one draw needn't show every extreme that they name: `distribution`: Nonnegative, of the shape of a local equilibrium with cell-to-cell variation.
All inputs are finite; a program needn't handle non-finite values.
Results may differ from a plain program's by a relative error of at most 0.0003.
Values sent between devices are 32-bit elements; how exact they have to be, the bound alone decides.
No kernel may reach another device: no remote copies, remote signals or barrier semaphores. Data moves between devices by JAX's collectives and lax.ppermute only.
A program may use at most 64 MiB of HBM per device.

v0:
```python
import math

import jax
import jax.numpy as jnp
from jax import lax
from jax.sharding import PartitionSpec as P

VG = 20
NZ = 2
STEPS = 2


speed_max = 4.5
time_step = 0.3 / 4.5


def with_halo(cells, sides, width):
    for axis, dim in sides:
        count = lax.axis_size(axis)
        head = lax.slice_in_dim(cells, 0, width, axis=dim)
        tail = lax.slice_in_dim(cells, cells.shape[dim] - width, cells.shape[dim], axis=dim)
        cells = jnp.concatenate(
            [
                lax.ppermute(tail, axis, [(i, (i + 1) % count) for i in range(count)]),
                cells,
                lax.ppermute(head, axis, [((i + 1) % count, i) for i in range(count)]),
            ],
            axis=dim,
        )
    return cells


def grid_speed(index):
    return speed_max * (2.0 * (index.astype(jnp.float32) + 0.5) / VG - 1.0)


def velocity_tables(first, count):
    labels = first + jnp.arange(count, dtype=jnp.int32)
    speed_x = grid_speed(labels // (VG * VG))
    speed_y = grid_speed(labels // VG % VG)
    speed_z = grid_speed(labels % VG)
    weight = (2.0 * speed_max / VG) ** 3 / (2.0 * math.pi) ** 1.5
    table = jnp.stack(
        [
            weight * jnp.ones_like(speed_x),
            weight * speed_x,
            weight * speed_y,
            weight * speed_z,
            weight * (speed_x * speed_x + speed_y * speed_y + speed_z * speed_z),
        ]
    )
    return (speed_x, speed_y, speed_z, table)


def running(center, xpad, ypad, speed_x, speed_y, speed_z):
    cols = center.shape[2]
    shaped = (-1, 1, 1)
    speed_x = speed_x.reshape(shaped)
    speed_y = speed_y.reshape(shaped)
    speed_z = speed_z.reshape(shaped)
    plane = lax.broadcasted_iota(jnp.int32, (1, 1, cols), 2) % NZ

    def below(offset):
        return jnp.where(
            plane >= offset, jnp.roll(center, offset, 2), jnp.roll(center, offset - NZ, 2)
        )

    def above(offset):
        return jnp.where(
            plane < NZ - offset, jnp.roll(center, -offset, 2), jnp.roll(center, NZ - offset, 2)
        )

    back_x = (3.0 * center - 4.0 * xpad[:, 1:-3] + xpad[:, :-4]) * 0.5
    ahead_x = (-3.0 * center + 4.0 * xpad[:, 3:-1] - xpad[:, 4:]) * 0.5
    back_y = (3.0 * center - 4.0 * ypad[:, :, NZ : NZ + cols] + ypad[:, :, :cols]) * 0.5
    ahead_y = (
        -3.0 * center
        + 4.0 * ypad[:, :, 3 * NZ : 3 * NZ + cols]
        - ypad[:, :, 4 * NZ : 4 * NZ + cols]
    ) * 0.5
    back_z = (3.0 * center - 4.0 * below(1) + below(2)) * 0.5
    ahead_z = (-3.0 * center + 4.0 * above(1) - above(2)) * 0.5
    flux = jnp.maximum(speed_x, 0.0) * back_x + jnp.minimum(speed_x, 0.0) * ahead_x
    flux = flux + jnp.maximum(speed_y, 0.0) * back_y + jnp.minimum(speed_y, 0.0) * ahead_y
    flux = flux + jnp.maximum(speed_z, 0.0) * back_z + jnp.minimum(speed_z, 0.0) * ahead_z
    return center - time_step * flux


def parameters(moments):
    density = moments[0]
    flow_x = moments[1] / density
    flow_y = moments[2] / density
    flow_z = moments[3] / density
    temper = (moments[4] / density - (flow_x * flow_x + flow_y * flow_y + flow_z * flow_z)) / 3.0
    return jnp.stack([density / (temper * jnp.sqrt(temper)), flow_x, flow_y, flow_z, 0.5 / temper])


def relax(moved, speed_x, speed_y, speed_z, params, rate):
    diff_x = speed_x[:, None] - params[1][None]
    diff_y = speed_y[:, None] - params[2][None]
    diff_z = speed_z[:, None] - params[3][None]
    maxwell = params[0][None] * jnp.exp(
        -params[4][None] * (diff_x * diff_x + diff_y * diff_y + diff_z * diff_z)
    )
    return moved + rate[None] * (maxwell - moved)


def body(distribution, collision_rate):
    vel_local, rows_x, cols_yz = distribution.shape
    first = lax.axis_index("vert") * vel_local
    speed_x, speed_y, speed_z, table = velocity_tables(first, vel_local)
    rate = collision_rate.reshape(-1)
    state = distribution
    for step in range(STEPS):
        xpad = with_halo(state, (("gx", 1),), 2)
        ypad = with_halo(state, (("gy", 2),), 2 * NZ)
        moved = running(state, xpad, ypad, speed_x, speed_y, speed_z)
        moved = moved.reshape(vel_local, -1)
        partial_sum = jnp.dot(table, moved, precision=lax.Precision.HIGHEST)
        params = parameters(lax.psum(partial_sum, "vert"))
        state = relax(moved, speed_x, speed_y, speed_z, params, rate).reshape(
            vel_local, rows_x, cols_yz
        )
    return state


def solution(mesh):
    placed = (P("vert", "gx", "gy"), P("gx", "gy"))
    return jax.shard_map(
        body, mesh=mesh, in_specs=placed, out_specs=P("vert", "gx", "gy"), check_vma=False
    )
```

profile of v0, /device:TPU:16, one launch (start us, length us, event | category | flops | bytes accessed | tf_op | source)
XLA Modules:
  0.0 1144.8 jit_solution(8993777181403356462)
XLA Ops:
  6.5 2.0 copy.58
  8.6 2.2 collective-permute-start
  10.8 1.5 collective-permute-start.1
  12.2 4.8 fusion.103
  17.1 2.7 copy.65
  19.7 0.1 collective-permute-start.3
  19.8 2.7 copy.64
  22.5 0.6 collective-permute-start.2
  23.3 2.4 fusion.99
  25.7 2.4 fusion.100
  28.3 8.9 fusion.40
  37.2 1.3 copy-done
  38.5 2.5 fusion.104
  41.0 0.0 all-reduce.3.cloned.1.call-update
  41.0 0.0 all-reduce.5.cloned.1.call-start
  41.1 532.4 %all-reduce.3.cloned.1.call-done = f32[5,4096]{1,0:T(8,128)} async-done(((f32[5,4096]{1,0:T(8,128)}), f32[5,4096]{1,0:T(8,128)}) %all-reduce.3.cloned.1.call-update) | async-done | bytes 81936 | tf_op jit(solution)/shard_map/psum | solution.py:120
  573.5 1.5 fusion.62
  575.0 6.3 multiply_add_fusion.3
  581.4 0.5 fusion.93
  582.0 0.5 fusion.94
  582.5 0.3 collective-permute-start.7
  582.8 0.5 collective-permute-start.6
  583.3 0.8 collective-permute-start.4
  584.1 2.8 collective-permute-start.5
  587.0 4.2 collective-permute-done.4
  591.2 2.0 collective-permute-done.5
  593.1 7.5 fusion.9
  600.6 2.5 fusion.105
  603.1 525.0 %all-reduce.5.cloned.1.call-done = f32[5,4096]{1,0:T(8,128)} async-done(((f32[5,4096]{1,0:T(8,128)}), f32[5,4096]{1,0:T(8,128)}) %all-reduce.5.cloned.1.call-update) | async-done | bytes 81936 | tf_op jit(solution)/shard_map/psum | solution.py:120
  1128.1 1.5 fusion.63
  1129.6 5.3 multiply_add_fusion.2
  1134.9 3.1 copy.63
  (37 shorter events, 0.7 us)
Async XLA Ops:
  6.5 567.0 %all-reduce.3.cloned.1.call-start = ((), (), s32[]{:S(2)}) async-start(), calls=%async_computation | async-start | bytes 262144 | tf_op jit(solution)/shard_map/psum | solution.py:120
  8.6 19.7 %collective-permute-start = (f32[125,2,128]{0,2,1:T(8,128)S(1)}, f32[125,2,128]{0,2,1:T(8,128)S(1)}, u32[]{:S(2)}, u32[]{:S(2)}) collective-permute-start(f32[125,2,128]{0,2,1:T(8,128)S(1)} %get-tuple-element.35), channel_id=1, source_target_pairs={{0,128},{128,0},{1,129},{129,1},{2,130},{130,2},{3,131},{131,3},{4... | collective-permute-start | bytes 384008 | tf_op jit(solution)/shard_map/ppermute | solution.py:24
  10.8 17.5 %collective-permute-start.1 = (f32[125,2,128]{0,2,1:T(8,128)S(1)}, f32[125,2,128]{0,2,1:T(8,128)S(1)}, u32[]{:S(2)}, u32[]{:S(2)}) collective-permute-start(f32[125,2,128]{0,2,1:T(8,128)S(1)} %get-tuple-element.36), channel_id=1, source_target_pairs={{128,0},{0,128},{129,1},{1,129},{130,2},{2,130},{131,3},{3,131},{1... | collective-permute-start | bytes 384008 | tf_op jit(solution)/shard_map/ppermute | solution.py:26
  19.7 8.4 collective-permute-start.3
  22.5 5.7 collective-permute-start.2
  37.2 1.4 copy-start
  37.2 537.8 %copy-start.1 = (f32[32,128]{1,0:T(8,128)S(1)}, f32[32,128]{1,0:T(8,128)}, u32[]{:S(2)}) copy-start(f32[32,128]{1,0:T(8,128)} %param.3) | copy-start | bytes 49156
  41.0 1087.1 %all-reduce.5.cloned.1.call-start = ((), (), s32[]{:S(2)}) async-start(), calls=%async_computation.1 | async-start | bytes 262144 | tf_op jit(solution)/shard_map/psum | solution.py:120
  582.5 4.3 collective-permute-start.7
  582.8 4.1 collective-permute-start.6
  583.3 7.9 collective-permute-start.4
  584.1 9.0 collective-permute-start.5
Sparse Core Ops, SparseCore 0:
  41.1 532.3 all-reduce.2
  603.2 524.8 all-reduce.4
where the time goes:
time: 1150 us; the launch traced here: 1140 us
  waiting for transfers between devices  1060 us (92%)
  other arithmetic  31.1 us (3%)
  local copies, waits for them, and re-layouts  22.9 us (2%)
  between operations  13.7 us (1%)
    psum x2, waiting for transfers between devices, body(): params = parameters(lax.psum(partial_sum, 'vert'))  1060 us
  transfers between devices with their start and end apart: 10, of which 4 were waited for; matrix products, arithmetic and copies ran while one was open for 1% of the time, Pallas kernels for 0%

commit v1 on v0

--- a/solution.py
+++ b/solution.py
@@ -105,6 +105,16 @@
     return moved + rate[None] * (maxwell - moved)
 
 
+def sum_over_vert(partial):
+    count = lax.axis_size("vert")
+    rows, cells = partial.shape
+    share = cells // count
+    parts = jnp.transpose(partial.reshape(rows, count, share), (1, 0, 2)).reshape(count, -1)
+    total = jnp.sum(lax.all_to_all(parts, "vert", 0, 0), axis=0)
+    spread = lax.all_to_all(jnp.broadcast_to(total[None], parts.shape), "vert", 0, 0)
+    return jnp.transpose(spread.reshape(count, rows, share), (1, 0, 2)).reshape(rows, cells)
+
+
 def body(distribution, collision_rate):
     vel_local, rows_x, cols_yz = distribution.shape
     first = lax.axis_index("vert") * vel_local
@@ -117,7 +127,7 @@
         moved = running(state, xpad, ypad, speed_x, speed_y, speed_z)
         moved = moved.reshape(vel_local, -1)
         partial_sum = jnp.dot(table, moved, precision=lax.Precision.HIGHEST)
-        params = parameters(lax.psum(partial_sum, "vert"))
+        params = parameters(sum_over_vert(partial_sum))
         state = relax(moved, speed_x, speed_y, speed_z, params, rate).reshape(
             vel_local, rows_x, cols_yz
         )

time: 1150 us -> 145 us (0.13)
  the two profiles are of different devices: /device:TPU:16 before, /device:TPU:1 now
where the time goes in v1:
time: 145 us; the launch traced here: 143 us
  blocking collectives  47.8 us (33%)
  local copies, waits for them, and re-layouts  26 us (18%)
  other arithmetic  25.7 us (18%)
  starting transfers between devices  17.9 us (12%)
  waiting for transfers between devices  15.5 us (11%)
  matrix products  9.89 us (7%)
    all_to_all x2, blocking collectives, sum_over_vert(): total = jnp.sum(lax.all_to_all(parts, 'vert', 0, 0), axis=0)  34.2 us
    sub x2, other arithmetic, running(): return center - time_step * flux  16.4 us
    all_to_all x1, blocking collectives, sum_over_vert(): lax.all_to_all(jnp.broadcast_to(total[None], parts.shape), 'vert', 0, 0)  13.6 us
    dot_general x2, matrix products, body(): partial_sum = jnp.dot(table, moved, precision=lax.Precision.HIGHEST)  9.89 us
    all_to_all x1, waiting for transfers between devices, sum_over_vert(): lax.all_to_all(jnp.broadcast_to(total[None], parts.shape), 'vert', 0, 0)  9.72 us
    add x2, other arithmetic, relax(): return moved + rate[None] * (maxwell - moved)  8.83 us
    unnamed x9, local copies, waits for them, and re-layouts  8.73 us
    ppermute x4, starting transfers between devices, with_halo(): lax.ppermute(tail, axis, [(i, (i + 1) % count) for i in range(count)])  6.64 us
  transfers between devices with their start and end apart: 9, of which 3 were waited for; matrix products, arithmetic and copies ran while one was open for 11% of the time, Pallas kernels for 0%

profile of v1, /device:TPU:1, one launch (start us, length us, event | category | flops | bytes accessed | tf_op | source)
XLA Modules:
  0.0 143.1 jit_solution(2616429555806681225)
XLA Ops:
  0.0 2.0 %copy.94 = f32[125,32,128]{0,2,1:T(8,128)S(1)} copy(f32[125,32,128]{2,1,0:T(8,128)} %param.2) | data formatting | bytes 4096000 | tf_op args[0]
  2.1 3.8 %collective-permute-start = (f32[125,2,128]{0,2,1:T(8,128)S(1)}, f32[125,2,128]{0,2,1:T(8,128)S(1)}, u32[]{:S(2)}, u32[]{:S(2)}) collective-permute-start(f32[125,2,128]{0,2,1:T(8,128)S(1)} %get-tuple-element.35), channel_id=1, source_target_pairs={{0,128},{128,0},{1,129},{129,1},{2,130},{130,2},{3,131},{131,3},{4... | collective-permute-start | bytes 384008 | tf_op jit(solution)/shard_map/ppermute | solution.py:24
  6.0 4.8 %fusion.99 = (f32[125,32,4]{2,1,0:T(8,128)}, f32[125,32,4]{2,1,0:T(8,128)}) fusion(f32[125,32,128]{2,1,0:T(8,128)} %param.2), kind=kLoop, calls=%fused_computation.172 | loop fusion | bytes 256000 | tf_op jit(solution)/shard_map/slice | solution.py:21
  10.8 2.7 %copy.117 = f32[125,32,4]{0,1,2:T(8,128)S(1)} copy(f32[125,32,4]{2,1,0:T(8,128)} %get-tuple-element.38) | data formatting | bytes 128000
  13.5 3.0 %collective-permute-start.3 = (f32[125,32,4]{0,1,2:T(8,128)S(1)}, f32[125,32,4]{0,1,2:T(8,128)S(1)}, u32[]{:S(2)}, u32[]{:S(2)}) collective-permute-start(f32[125,32,4]{0,1,2:T(8,128)S(1)} %copy.117), channel_id=1, source_target_pairs={{64,0},{0,64},{65,1},{1,65},{66,2},{2,66},{67,3},{3,67},{68,4},{4,... | collective-permute-start | bytes 192008 | tf_op jit(solution)/shard_map/ppermute | solution.py:26
  16.5 2.7 %copy.116 = f32[125,32,4]{0,1,2:T(8,128)S(1)} copy(f32[125,32,4]{2,1,0:T(8,128)} %get-tuple-element.37) | data formatting | bytes 128000
  19.5 2.4 %fusion.95 = (f32[125,32,127]{0,2,1:T(8,128)}, f32[125,32,127]{0,2,1:T(8,128)}) fusion(f32[125,32,128]{0,2,1:T(8,128)S(1)} %copy.94), kind=kLoop, calls=%fused_computation.168 | loop fusion | bytes 8128000 | tf_op jit(solution)/shard_map/jit(_roll_static)/slice | solution.py:65
  21.9 2.4 %fusion.96 = (f32[125,32,126]{0,2,1:T(8,128)}, f32[125,32,126]{0,2,1:T(8,128)}) fusion(f32[125,32,128]{0,2,1:T(8,128)S(1)} %copy.94), kind=kLoop, calls=%fused_computation.169 | loop fusion | bytes 8064000 | tf_op jit(solution)/shard_map/jit(_roll_static)/slice | solution.py:70
  24.5 8.9 %fusion.40 = f32[125,32,128]{0,2,1:T(8,128)S(1)} fusion(f32[125,32,128]{0,2,1:T(8,128)S(1)} %copy.94, f32[125,32,4]{0,2,1:T(4,128)S(1)} %copy.83, f32[125,32,4]{0,2,1:T(4,128)S(1)} %copy.79, f32[125,2,128]{0,2,1:T(8,128)S(1)} %collective-permute-done.1, f32[125,2,128]{0,2,1:T(8,128)S(1)} %collective-permute-done, f32[125,32,126]{0,2,1:T(8,128)} %get-tuple-element.32, ...), kind=kLoop, calls=%fused_computation.58 | loop fusion | flops 25088000 | bytes 12675512 | tf_op jit(solution)/shard_map/sub | solution.py:86
  33.4 1.3 copy-done
  34.7 4.9 %convolution_bitcast_fusion.1 = f32[64,5,64]{2,1,0:T(8,128)S(1)} fusion(f32[64,64,125]{2,1,0:T(8,128)S(1)} %bitcast.30, f32[5,125]{1,0:T(8,128)S(1)} %stack.5), kind=kOutput, calls=%fused_computation.101 | convolution fusion | flops 30720000 | bytes 2132420 | tf_op jit(solution)/shard_map/dot_general | solution.py:129
  39.7 0.2 copy.95
  40.0 20.6 %all_to_all.30 = f32[64,1,320]{2,1,0:T(1,128)S(1)} all-to-all(f32[64,1,320]{2,1,0:T(1,128)S(1)} %copy.96), channel_id=1, replica_groups=mesh['gx'=2,'gy'=2,'vert'=64] {'vert'}, dimensions={0} | all-to-all | bytes 163840 | tf_op jit(solution)/shard_map/all_to_all | solution.py:113
  60.7 0.7 broadcast_in_dim.65
  61.4 4.6 %all-to-all-start.1 = ((f32[64,1,320]{2,1,0:T(1,128)}), f32[64,1,320]{2,1,0:T(1,128)S(1)}, u32[]{:S(2)}, u32[]{:S(2)}) async-start(f32[64,1,320]{2,1,0:T(1,128)} %broadcast_in_dim.65), calls=%async_computation.1 | async-start | bytes 196608 | tf_op jit(solution)/shard_map/all_to_all | solution.py:114
  66.1 9.7 %all-to-all-done.1 = f32[64,1,320]{2,1,0:T(1,128)S(1)} async-done(((f32[64,1,320]{2,1,0:T(1,128)}), f32[64,1,320]{2,1,0:T(1,128)S(1)}, u32[]{:S(2)}, u32[]{:S(2)}) %all-to-all-start.1) | async-done | bytes 81952 | tf_op jit(solution)/shard_map/all_to_all | solution.py:114
  76.8 3.6 %multiply_add_fusion.3 = f32[125,32,128]{0,2,1:T(8,128)S(1)} fusion(f32[125,32,128]{0,2,1:T(8,128)S(1)} %copy-done.1, f32[32,128]{1,0:T(8,128)S(1)} %get-tuple-element.14, f32[125]{0:T(128)S(1)} %get-tuple-element.50, f32[32,128]{1,0:T(8,128)S(1)} %get-tuple-element.13, f32[125]{0:T(128)S(1)} %get-tuple-element.49, f32[32,128]{1,0:T(8,128)S(1)} %get-tuple-element.12, ...), kind=kLoop, calls=%fused_computation.99 | loop fusion | flops 6656000 | bytes 4195804 | tf_op jit(solution)/shard_map/add | solution.py:105
  80.5 0.5 fusion.89
  81.0 0.5 fusion.90
  81.6 3.2 %collective-permute-start.7 = (f32[125,32,4]{0,1,2:T(8,128)S(1)}, f32[125,32,4]{0,1,2:T(8,128)S(1)}, u32[]{:S(2)}, u32[]{:S(2)}) collective-permute-start(f32[125,32,4]{0,1,2:T(8,128)S(1)} %copy.105), channel_id=1, source_target_pairs={{64,0},{0,64},{65,1},{1,65},{66,2},{2,66},{67,3},{3,67},{68,4},{4,... | collective-permute-start | bytes 192008 | tf_op jit(solution)/shard_map/ppermute | solution.py:26
  84.8 2.6 %collective-permute-start.4 = (f32[125,2,128]{0,2,1:T(8,128)S(1)}, f32[125,2,128]{0,2,1:T(8,128)S(1)}, u32[]{:S(2)}, u32[]{:S(2)}) collective-permute-start(f32[125,2,128]{0,2,1:T(8,128)S(1)} %get-tuple-element.23), channel_id=1, source_target_pairs={{0,128},{128,0},{1,129},{129,1},{2,130},{130,2},{3,131},{131,3},{4... | collective-permute-start | bytes 384008 | tf_op jit(solution)/shard_map/ppermute | solution.py:24
  87.5 0.3 collective-permute-start.5
  88.0 3.0 %collective-permute-done.4 = f32[125,2,128]{0,2,1:T(8,128)S(1)} collective-permute-done((f32[125,2,128]{0,2,1:T(8,128)S(1)}, f32[125,2,128]{0,2,1:T(8,128)S(1)}, u32[]{:S(2)}, u32[]{:S(2)}) %collective-permute-start.4) | collective-permute-done | bytes 128032 | tf_op jit(solution)/shard_map/ppermute | solution.py:24
  91.0 2.7 %collective-permute-done.5 = f32[125,2,128]{0,2,1:T(8,128)S(1)} collective-permute-done((f32[125,2,128]{0,2,1:T(8,128)S(1)}, f32[125,2,128]{0,2,1:T(8,128)S(1)}, u32[]{:S(2)}, u32[]{:S(2)}) %collective-permute-start.5) | collective-permute-done | bytes 128032 | tf_op jit(solution)/shard_map/ppermute | solution.py:26
  93.7 7.5 %fusion.9 = f32[125,32,128]{0,2,1:T(8,128)S(1)} fusion(f32[125,32,128]{0,2,1:T(8,128)S(1)} %multiply_add_fusion.3, f32[125,32,4]{0,2,1:T(4,128)S(1)} %copy.106, f32[125,32,4]{0,2,1:T(4,128)S(1)} %copy.104, f32[125,2,128]{0,2,1:T(8,128)S(1)} %collective-permute-done.5, f32[125,2,128]{0,2,1:T(8,128)S(1)} %collective-permute-done.4, ...), kind=kLoop, calls=%fused_computation.25 | loop fusion | flops 25088000 | bytes 12675512 | tf_op jit(solution)/shard_map/sub | solution.py:86
  101.2 4.9 %convolution_bitcast_fusion = f32[64,5,64]{2,1,0:T(8,128)S(1)} fusion(f32[64,64,125]{2,1,0:T(8,128)S(1)} %bitcast.29, f32[5,125]{1,0:T(8,128)S(1)} %stack.5), kind=kOutput, calls=%fused_computation.100 | convolution fusion | flops 30720000 | bytes 2132420 | tf_op jit(solution)/shard_map/dot_general | solution.py:129
  106.1 0.2 copy.107
  106.3 0.1 copy.108
  106.4 13.5 %all_to_all.31 = f32[64,1,320]{2,1,0:T(1,128)S(1)} all-to-all(f32[64,1,320]{2,1,0:T(1,128)S(1)} %copy.108), channel_id=1, replica_groups=mesh['gx'=2,'gy'=2,'vert'=64] {'vert'}, dimensions={0} | all-to-all | bytes 163840 | tf_op jit(solution)/shard_map/all_to_all | solution.py:113
  120.1 13.6 %all_to_all.32 = f32[64,1,320]{2,1,0:T(1,128)S(1)} all-to-all(f32[64,1,320]{2,1,0:T(1,128)S(1)} %broadcast_in_dim.66), channel_id=1, replica_groups=mesh['gx'=2,'gy'=2,'vert'=64] {'vert'}, dimensions={0} | all-to-all | bytes 163840 | tf_op jit(solution)/shard_map/all_to_all | solution.py:114
  134.8 5.3 %multiply_add_fusion.2 = f32[125,32,128]{0,2,1:T(8,128)} fusion(f32[125,32,128]{0,2,1:T(8,128)S(1)} %fusion.9, f32[32,128]{1,0:T(8,128)S(1)} %get-tuple-element.9, f32[32,128]{1,0:T(8,128)S(1)} %get-tuple-element.8, f32[32,128]{1,0:T(8,128)S(1)} %get-tuple-element.7, f32[32,128]{1,0:T(8,128)S(1)} %divide_negate_fusion, f32[32,128]{1,0:T(8,128)S(1)} %get-tuple-element.5, ...), kind=kLoop, calls=%fused_computation.98 | loop fusion | flops 6656000 | bytes 4195804 | tf_op jit(solution)/shard_map/add | solution.py:105
  140.0 3.1 %copy.115 = f32[125,32,128]{2,1,0:T(8,128)} copy(f32[125,32,128]{0,2,1:T(8,128)} %multiply_add_fusion.2) | data formatting | bytes 4096000 | tf_op jit(solution)/shard_map/add | solution.py:105
  (70 shorter events, 3.2 us)
Async XLA Ops:
  2.1 22.4 %collective-permute-start = (f32[125,2,128]{0,2,1:T(8,128)S(1)}, f32[125,2,128]{0,2,1:T(8,128)S(1)}, u32[]{:S(2)}, u32[]{:S(2)}) collective-permute-start(f32[125,2,128]{0,2,1:T(8,128)S(1)} %get-tuple-element.35), channel_id=1, source_target_pairs={{0,128},{128,0},{1,129},{129,1},{2,130},{130,2},{3,131},{131,3},{4... | collective-permute-start | bytes 384008 | tf_op jit(solution)/shard_map/ppermute | solution.py:24
  5.9 18.6 %collective-permute-start.1 = (f32[125,2,128]{0,2,1:T(8,128)S(1)}, f32[125,2,128]{0,2,1:T(8,128)S(1)}, u32[]{:S(2)}, u32[]{:S(2)}) collective-permute-start(f32[125,2,128]{0,2,1:T(8,128)S(1)} %get-tuple-element.36), channel_id=1, source_target_pairs={{128,0},{0,128},{129,1},{1,129},{130,2},{2,130},{131,3},{3,131},{1... | collective-permute-start | bytes 384008 | tf_op jit(solution)/shard_map/ppermute | solution.py:26
  13.5 10.8 %collective-permute-start.3 = (f32[125,32,4]{0,1,2:T(8,128)S(1)}, f32[125,32,4]{0,1,2:T(8,128)S(1)}, u32[]{:S(2)}, u32[]{:S(2)}) collective-permute-start(f32[125,32,4]{0,1,2:T(8,128)S(1)} %copy.117), channel_id=1, source_target_pairs={{64,0},{0,64},{65,1},{1,65},{66,2},{2,66},{67,3},{3,67},{68,4},{4,... | collective-permute-start | bytes 192008 | tf_op jit(solution)/shard_map/ppermute | solution.py:26
  19.2 5.2 %collective-permute-start.2 = (f32[125,32,4]{0,1,2:T(8,128)S(1)}, f32[125,32,4]{0,1,2:T(8,128)S(1)}, u32[]{:S(2)}, u32[]{:S(2)}) collective-permute-start(f32[125,32,4]{0,1,2:T(8,128)S(1)} %copy.116), channel_id=1, source_target_pairs={{0,64},{64,0},{1,65},{65,1},{2,66},{66,2},{3,67},{67,3},{4,68},{68... | collective-permute-start | bytes 192008 | tf_op jit(solution)/shard_map/ppermute | solution.py:24
  33.4 1.3 copy-start
  34.7 42.1 %copy-start.2 = (f32[32,128]{1,0:T(8,128)S(1)}, f32[32,128]{1,0:T(8,128)}, u32[]{:S(2)}) copy-start(f32[32,128]{1,0:T(8,128)} %param.3) | copy-start | bytes 49156
  39.7 37.1 %copy-start.1 = (f32[125,32,128]{0,2,1:T(8,128)S(1)}, f32[125,32,128]{0,2,1:T(8,128)}, u32[]{:S(2)}) copy-start(f32[125,32,128]{0,2,1:T(8,128)} %copy-done) | copy-start | bytes 6144004
  61.4 14.4 %all-to-all-start.1 = ((f32[64,1,320]{2,1,0:T(1,128)}), f32[64,1,320]{2,1,0:T(1,128)S(1)}, u32[]{:S(2)}, u32[]{:S(2)}) async-start(f32[64,1,320]{2,1,0:T(1,128)} %broadcast_in_dim.65), calls=%async_computation.1 | async-start | bytes 196608 | tf_op jit(solution)/shard_map/all_to_all | solution.py:114
  81.6 6.3 %collective-permute-start.7 = (f32[125,32,4]{0,1,2:T(8,128)S(1)}, f32[125,32,4]{0,1,2:T(8,128)S(1)}, u32[]{:S(2)}, u32[]{:S(2)}) collective-permute-start(f32[125,32,4]{0,1,2:T(8,128)S(1)} %copy.105), channel_id=1, source_target_pairs={{64,0},{0,64},{65,1},{1,65},{66,2},{2,66},{67,3},{3,67},{68,4},{4,... | collective-permute-start | bytes 192008 | tf_op jit(solution)/shard_map/ppermute | solution.py:26
  84.7 3.2 %collective-permute-start.6 = (f32[125,32,4]{0,1,2:T(8,128)S(1)}, f32[125,32,4]{0,1,2:T(8,128)S(1)}, u32[]{:S(2)}, u32[]{:S(2)}) collective-permute-start(f32[125,32,4]{0,1,2:T(8,128)S(1)} %copy.103), channel_id=1, source_target_pairs={{0,64},{64,0},{1,65},{65,1},{2,66},{66,2},{3,67},{67,3},{4,68},{68... | collective-permute-start | bytes 192008 | tf_op jit(solution)/shard_map/ppermute | solution.py:24
  84.8 6.2 %collective-permute-start.4 = (f32[125,2,128]{0,2,1:T(8,128)S(1)}, f32[125,2,128]{0,2,1:T(8,128)S(1)}, u32[]{:S(2)}, u32[]{:S(2)}) collective-permute-start(f32[125,2,128]{0,2,1:T(8,128)S(1)} %get-tuple-element.23), channel_id=1, source_target_pairs={{0,128},{128,0},{1,129},{129,1},{2,130},{130,2},{3,131},{131,3},{4... | collective-permute-start | bytes 384008 | tf_op jit(solution)/shard_map/ppermute | solution.py:24
  87.5 6.2 %collective-permute-start.5 = (f32[125,2,128]{0,2,1:T(8,128)S(1)}, f32[125,2,128]{0,2,1:T(8,128)S(1)}, u32[]{:S(2)}, u32[]{:S(2)}) collective-permute-start(f32[125,2,128]{0,2,1:T(8,128)S(1)} %get-tuple-element.24), channel_id=1, source_target_pairs={{128,0},{0,128},{129,1},{1,129},{130,2},{2,130},{131,3},{3,131},{1... | collective-permute-start | bytes 384008 | tf_op jit(solution)/shard_map/ppermute | solution.py:26

commit v2 on v0

v2 whole, which is shorter than its diff:
```python
import math

import jax
import jax.numpy as jnp
from jax import lax
from jax.experimental import pallas as pl
from jax.experimental.pallas import tpu as pltpu
from jax.sharding import Mesh
from jax.sharding import PartitionSpec as P

VG = 20
VEL_LOCAL = 125
CHUNK = 5
CHUNKS = VEL_LOCAL // CHUNK
GROUPS = 7
ROWS = 32
LANES = 128

SPACING = 9.0 / VG
LOWEST = 4.5 * (1.0 / VG - 1.0)
DT = 0.3 / 4.5
WEIGHT = (9.0 / VG) ** 3 / (2.0 * math.pi) ** 1.5
SPEEDS = [LOWEST + SPACING * n for n in range(VG)]

VERT = ("x", "yl", "z")
PLANE = ("x", "yl")

ROW_SECOND = 5 * ROWS
ROW_SPILL_Y = 10 * ROWS
ROW_SPILL_X = 11 * ROWS
ROW_EDGE = 12 * ROWS
ROW_COUNT = 16 * ROWS

STACK = 72
NEAR_Y = 32
NEAR_X = 64


def speed_of(index):
    return index.astype(jnp.float32) * SPACING + LOWEST


def lane_index():
    return lax.broadcasted_iota(jnp.int32, (ROWS, LANES), 1)


def other_plane(tile, even):
    return jnp.where(even, pltpu.roll(tile, LANES - 1, 1), pltpu.roll(tile, 1, 1))


def chunk_place(first, chunk):
    slot = lax.rem(first, VG) + chunk * CHUNK
    group = lax.div(slot, VG)
    whole = lax.div(first, VG) + group
    index_x = lax.div(whole, VG)
    return group, index_x, whole - index_x * VG, slot - group * VG


def y_sides(lane, positive):
    shift = jnp.where(positive, 2, LANES - 2)
    one = ((lane + jnp.where(positive, 2, 0)) & (LANES - 1)) < 2
    two = ((lane + jnp.where(positive, 4, 0)) & (LANES - 1)) < 4
    return shift, one, two


def y_part(center, near, sides):
    shift, one, two = sides
    far = pltpu.roll(jnp.where(two, near, center), shift, 1)
    return pltpu.roll(jnp.where(one, near, center) - 0.25 * far, shift, 1)


def upwind(center, back, x_one, x_two, even, coef_x, coef_y, coef_z):
    return (
        center * (1.0 - 1.5 * (coef_x + coef_y) - 2.0 * coef_z)
        + (2.0 * coef_x) * (x_one - 0.25 * x_two)
        + (2.0 * coef_y) * back
        + (2.0 * coef_z) * other_plane(center, even)
    )


def first_kernel(place, f, f_near, f_edge, rate, kept, sums, groups, buf):
    device = place[0]
    first = device * VEL_LOCAL
    sign = jnp.where(device >= 32, 1, -1)
    lane = lane_index()
    even = lax.rem(lane, 2) == 0
    keep = 1.0 - rate[...]
    groups[...] = jnp.zeros_like(groups)

    def chunk(c, carry):
        group, index_x, index_y, index_z = chunk_place(first, c)
        coef_x = DT * jnp.abs(speed_of(index_x))
        coef_y = DT * jnp.abs(speed_of(index_y))
        positive = index_y >= VG // 2
        sides = y_sides(lane, positive)
        side = jnp.where(index_z >= VG // 2, 1.0, -1.0)
        acc = [None] * 4
        for t in range(CHUNK):
            v = c * CHUNK + t
            center = f[v]
            halo = f_edge[v]
            buf[t, 8:40] = center
            buf[t, 6:8] = halo
            buf[t, 40:42] = halo
            x_one = buf[t, pl.ds(8 - sign, ROWS)]
            x_two = buf[t, pl.ds(8 - 2 * sign, ROWS)]
            speed_z = speed_of(index_z + t)
            back = y_part(center, f_near[v], sides)
            moved = upwind(
                center, back, x_one, x_two, even, coef_x, coef_y, DT * speed_z * side
            )
            kept[v] = keep * moved
            power = moved
            for k in range(4):
                acc[k] = power if acc[k] is None else acc[k] + power
                if k < 3:
                    power = power * speed_z
        for k in range(3):
            groups[group, k] += acc[k]
            groups[group, 3 + k] += side * acc[k + 1]
        return carry

    lax.fori_loop(0, CHUNKS, chunk, 0)
    sums[...] = jnp.zeros_like(sums)

    def spread(group, carry):
        whole = lax.div(first, VG) + group
        index_x = lax.div(whole, VG)
        index_y = whole - index_x * VG
        speed_x = speed_of(index_x)
        speed_y = speed_of(index_y)
        coef_x = DT * jnp.abs(speed_x)
        coef_y = DT * jnp.abs(speed_y)
        positive = index_y >= VG // 2
        sides = y_sides(lane, positive)
        zero_rows = jnp.zeros((2, LANES), jnp.float32)

        def put(row, parts):
            squares = speed_x * speed_x + speed_y * speed_y
            count = parts[0].shape[0]
            for m, value in enumerate(
                (
                    parts[0],
                    speed_x * parts[0],
                    speed_y * parts[0],
                    parts[1],
                    squares * parts[0] + parts[2],
                )
            ):
                at = row + m * (ROWS if count == ROWS else 4)
                sums[at : at + count] += value

        level = [WEIGHT * groups[group, k] for k in range(6)]
        put(0, level[:3])
        second, near_y, near_x = [], [], []
        for k in range(3):
            center = keep * level[k]
            absolute = keep * level[3 + k]
            buf[k, 8:40] = center
            buf[k, 6:8] = zero_rows
            buf[k, 40:42] = zero_rows
            x_one = buf[k, pl.ds(8 - sign, ROWS)]
            x_two = buf[k, pl.ds(8 - 2 * sign, ROWS)]
            second.append(
                center * (1.0 - 1.5 * (coef_x + coef_y))
                - (2.0 * DT) * (absolute - other_plane(absolute, even))
                + (2.0 * coef_x) * (x_one - 0.25 * x_two)
                + (2.0 * coef_y) * y_part(center, 0.0, sides)
            )
            near_y.append(coef_y * jnp.where(sides[2], center, 0.0))
            tail = coef_x * jnp.maximum(sign, 0).astype(jnp.float32)
            head = coef_x * jnp.maximum(-sign, 0).astype(jnp.float32)
            near_x.append(
                jnp.concatenate([tail * buf[k, 38:40], head * buf[k, 8:10]], axis=0)
            )
        put(ROW_SECOND, second)
        put(ROW_SPILL_X, near_x)
        squares = speed_x * speed_x + speed_y * speed_y
        packed = sums[ROW_SPILL_Y : ROW_SPILL_Y + ROWS]
        for m, value in enumerate(
            (
                near_y[0],
                speed_x * near_y[0],
                speed_y * near_y[0],
                near_y[1],
                squares * near_y[0] + near_y[2],
            )
        ):
            packed = packed + (pltpu.roll(value, 8 * m, 1) if m else value)
        sums[ROW_SPILL_Y : ROW_SPILL_Y + ROWS] = packed
        return carry

    lax.fori_loop(0, GROUPS, spread, 0)
    for m in range(5):
        sums[ROW_EDGE + 4 * m : ROW_EDGE + 4 * m + 2] = sums[ROWS * m + 30 : ROWS * m + 32]
        sums[ROW_EDGE + 4 * m + 2 : ROW_EDGE + 4 * m + 4] = sums[ROWS * m : ROWS * m + 2]


def parameters(moments):
    density = moments[0]
    share = 1.0 / density
    flow_x = moments[1] * share
    flow_y = moments[2] * share
    flow_z = moments[3] * share
    temper = (moments[4] * share - (flow_x * flow_x + flow_y * flow_y + flow_z * flow_z)) / 3.0
    return density / (temper * jnp.sqrt(temper)), flow_x, flow_y, flow_z, 0.5 / temper


def products(part_x, part_y, part_z):
    yz = part_y[0] * part_z[0]
    return (
        part_x[0] * yz,
        part_x[1] * yz,
        part_x[0] * (part_y[1] * part_z[0]),
        part_x[0] * (part_y[0] * part_z[1]),
        part_x[2] * yz + part_x[0] * (part_y[2] * part_z[0] + part_y[0] * part_z[2]),
    )


def second_kernel(
    place, kept, kept_near, kept_edge, total, total_near, total_edge, rate, rate_near, rate_edge,
    out, first_mom, stack_rate, tables, kinds, table_two, base, buf,
):
    device = place[0]
    first = device * VEL_LOCAL
    sign = jnp.where(device >= 32, 1, -1)
    lane = lane_index()
    even = lax.rem(lane, 2) == 0
    rising = (2, lane >= LANES - 2, lane >= LANES - 4)
    falling = (LANES - 2, lane < 2, lane < 4)

    for m in range(5):
        first_mom[m, 0:32] = total[ROWS * m : ROWS * (m + 1)]
        first_mom[m, 32:64] = total_near[ROWS * m : ROWS * (m + 1)]
        first_mom[m, 64:72] = total[ROWS * m : ROWS * m + 8]
        first_mom[m, 64:68] = total_edge[ROWS + 4 * m : ROWS + 4 * m + 4]
    stack_rate[0:32] = rate[...]
    stack_rate[32:64] = rate_near[...]
    stack_rate[64:72] = rate[0:8]
    stack_rate[64:68] = rate_edge[...]

    def block(b, carry):
        at = pl.ds(pl.multiple_of(b * 8, 8), 8)
        amp, flow_x, flow_y, flow_z, inv = parameters([first_mom[m, at] for m in range(5)])
        scale = amp * stack_rate[at]
        base[at] = scale
        full, plus, minus = [], [], []
        for d, flow in enumerate((flow_x, flow_y, flow_z)):
            halves = []
            for half in range(2):
                level = [None] * 4
                for n in range(half * 10, half * 10 + 10):
                    gap = SPEEDS[n] - flow
                    value = jnp.exp(-(inv * gap * gap))
                    tables[d, n, at] = value
                    for k in range(4):
                        term = value if k == 0 else value * (SPEEDS[n] ** k)
                        level[k] = term if level[k] is None else level[k] + term
                halves.append(level)
            full.append([halves[0][k] + halves[1][k] for k in range(3)])
            plus.append([halves[1][k + 1] for k in range(3)])
            minus.append([-halves[0][k + 1] for k in range(3)])
        scale = scale * WEIGHT
        x, y, z = ([scale * part for part in full[0]]), full[1], full[2]
        sets = [
            products([scale * part for part in plus[0]], y, z),
            products([scale * part for part in minus[0]], y, z),
            products(x, plus[1], z),
            products(x, minus[1], z),
            products(x, y, [plus[2][k] + minus[2][k] for k in range(3)]),
        ]
        whole = products(x, y, z)
        for m in range(5):
            for s in range(5):
                kinds[s, m, at] = sets[s][m]
            kinds[5, m, at] = (
                whole[m]
                - (1.5 * DT) * ((sets[0][m] + sets[1][m]) + (sets[2][m] + sets[3][m]))
                - (2.0 * DT) * sets[4][m]
            )
        return carry

    lax.fori_loop(0, STACK // 8, block, 0)

    spill_y = total_near[ROW_SPILL_Y : ROW_SPILL_Y + ROWS]
    moments = []
    for m in range(5):
        own = slice(0, ROWS)
        near = slice(NEAR_Y, NEAR_Y + ROWS)
        result = total[ROW_SECOND + ROWS * m : ROW_SECOND + ROWS * (m + 1)] + kinds[5, m, own]
        result = result + (2.0 * DT) * other_plane(kinds[4, m, own], even)
        buf[0, 8:40] = kinds[0, m, own]
        buf[0, 6:8] = kinds[0, m, NEAR_X : NEAR_X + 2] + (1.0 / DT) * total_edge[4 * m : 4 * m + 2]
        result = result + (2.0 * DT) * (buf[0, 7:39] - 0.25 * buf[0, 6:38])
        buf[1, 8:40] = kinds[1, m, own]
        buf[1, 40:42] = (
            kinds[1, m, NEAR_X + 2 : NEAR_X + 4] + (1.0 / DT) * total_edge[4 * m + 2 : 4 * m + 4]
        )
        result = result + (2.0 * DT) * (buf[1, 9:41] - 0.25 * buf[1, 10:42])
        spill = pltpu.roll(spill_y, LANES - 8 * m, 1) if m else spill_y
        spill = (1.0 / DT) * spill
        result = result + (2.0 * DT) * y_part(kinds[2, m, own], kinds[2, m, near] + spill, rising)
        back = y_part(kinds[3, m, own], kinds[3, m, near] + spill, falling)
        moments.append(result + (2.0 * DT) * back)

    amp, flow_x, flow_y, flow_z, inv = parameters(moments)
    scale_two = amp * rate[...]
    keep = 1.0 - rate[...]
    for n in range(VG):
        gap = SPEEDS[n] - flow_z
        table_two[n] = jnp.exp(-(inv * gap * gap))
    table_two[VG] = scale_two
    table_two[VG + 1] = flow_x
    table_two[VG + 2] = flow_y
    table_two[VG + 3] = inv
    edge_at = NEAR_X + jnp.where(sign > 0, 0, 2)

    def chunk(c, carry):
        group, index_x, index_y, index_z = chunk_place(first, c)
        speed_x = speed_of(index_x)
        speed_y = speed_of(index_y)
        coef_x = DT * jnp.abs(speed_x)
        coef_y = DT * jnp.abs(speed_y)
        positive = index_y >= VG // 2
        sides = y_sides(lane, positive)
        side = jnp.where(index_z >= VG // 2, 1.0, -1.0)
        front = base[...] * tables[0, index_x] * tables[1, index_y]
        front_edge = (
            base[pl.ds(edge_at, 2)]
            * tables[0, index_x, pl.ds(edge_at, 2)]
            * tables[1, index_y, pl.ds(edge_at, 2)]
        )
        gap_x = speed_x - table_two[VG + 1]
        gap_y = speed_y - table_two[VG + 2]
        front_two = table_two[VG] * jnp.exp(
            -(table_two[VG + 3] * (gap_x * gap_x + gap_y * gap_y))
        )
        for t in range(CHUNK):
            v = c * CHUNK + t
            speed_z = speed_of(index_z + t)
            center = kept[v] + front[0:32] * tables[2, index_z + t, 0:32]
            near = kept_near[v] + front[32:64] * tables[2, index_z + t, 32:64]
            halo = kept_edge[v] + front_edge * tables[2, index_z + t, pl.ds(edge_at, 2)]
            buf[t, 8:40] = center
            buf[t, 6:8] = halo
            buf[t, 40:42] = halo
            x_one = buf[t, pl.ds(8 - sign, ROWS)]
            x_two = buf[t, pl.ds(8 - 2 * sign, ROWS)]
            moved = upwind(
                center, y_part(center, near, sides), x_one, x_two, even, coef_x, coef_y,
                DT * speed_z * side,
            )
            out[v] = keep * moved + front_two * table_two[index_z + t]
        return carry

    lax.fori_loop(0, CHUNKS, chunk, 0)


def vmem():
    return pl.BlockSpec(memory_space=pltpu.VMEM)


def smem():
    return pl.BlockSpec(memory_space=pltpu.SMEM)


SWAP = [(0, 1), (1, 0)]


def sum_over_vert(partial):
    parts = partial.reshape(8, 8, 8, LANES)
    share = jnp.sum(lax.all_to_all(parts, PLANE, 0, 0), axis=0)
    share = jnp.sum(lax.all_to_all(jnp.broadcast_to(share[None], parts.shape), "z", 0, 0), axis=0)
    whole = lax.all_to_all(jnp.broadcast_to(share[None], parts.shape), PLANE, 0, 0)
    return whole.reshape(ROW_COUNT, LANES)


def edge_rows(cells, forward):
    start = jnp.where(forward, ROWS - 2, 0)
    return lax.dynamic_slice_in_dim(cells, start, 2, axis=1)


def body(distribution, collision_rate):
    device = lax.axis_index(VERT)
    place = device.astype(jnp.int32).reshape(1)
    forward = device >= 32
    tile = jax.ShapeDtypeStruct((VEL_LOCAL, ROWS, LANES), jnp.float32)
    f_edge = lax.ppermute(edge_rows(distribution, forward), "gx", SWAP)
    f_near = lax.ppermute(distribution, "gy", SWAP)
    rate_near = lax.ppermute(collision_rate, "gy", SWAP)
    rate_edge = lax.ppermute(
        jnp.concatenate([collision_rate[ROWS - 2 :], collision_rate[:2]], axis=0), "gx", SWAP
    )
    kept, partial = pl.pallas_call(
        first_kernel,
        out_shape=(tile, jax.ShapeDtypeStruct((ROW_COUNT, LANES), jnp.float32)),
        in_specs=[smem(), vmem(), vmem(), vmem(), vmem()],
        out_specs=(vmem(), vmem()),
        scratch_shapes=[
            pltpu.VMEM((GROUPS, 6, ROWS, LANES), jnp.float32),
            pltpu.VMEM((CHUNK, 48, LANES), jnp.float32),
        ],
        compiler_params=pltpu.CompilerParams(vmem_limit_bytes=24 * 2**20),
        name="move_and_sum",
    )(place, distribution, f_near, f_edge, collision_rate)
    kept_edge = lax.ppermute(edge_rows(kept, forward), "gx", SWAP)
    kept_near = lax.ppermute(kept, "gy", SWAP)
    total = sum_over_vert(partial)
    total_near = lax.ppermute(total, "gy", SWAP)
    total_edge = lax.ppermute(total[ROW_SPILL_X : ROW_EDGE + ROWS], "gx", SWAP)
    return pl.pallas_call(
        second_kernel,
        out_shape=tile,
        in_specs=[smem()] + [vmem()] * 9,
        out_specs=vmem(),
        scratch_shapes=[
            pltpu.VMEM((5, STACK, LANES), jnp.float32),
            pltpu.VMEM((STACK, LANES), jnp.float32),
            pltpu.VMEM((3, VG, STACK, LANES), jnp.float32),
            pltpu.VMEM((6, 5, STACK, LANES), jnp.float32),
            pltpu.VMEM((VG + 4, ROWS, LANES), jnp.float32),
            pltpu.VMEM((STACK, LANES), jnp.float32),
            pltpu.VMEM((CHUNK, 48, LANES), jnp.float32),
        ],
        compiler_params=pltpu.CompilerParams(vmem_limit_bytes=32 * 2**20),
        name="collide_move_collide",
    )(
        place, kept, kept_near, kept_edge, total, total_near, total_edge,
        collision_rate, rate_near, rate_edge,
    )


def solution(mesh):
    split = Mesh(mesh.devices.reshape(2, 2, 4, 2, 8), ("gx", "gy", "x", "yl", "z"))
    placed = (P(VERT, "gx", "gy"), P("gx", "gy"))
    return jax.shard_map(
        body, mesh=split, in_specs=placed, out_specs=P(VERT, "gx", "gy"), check_vma=False
    )
```

time: 1150 us -> 83.6 us (0.07)
  the two profiles are of different devices: /device:TPU:16 before, /device:TPU:1 now
where the time goes in v2:
time: 83.6 us; the launch traced here: 83.2 us
  blocking collectives  36.5 us (44%)
  starting transfers between devices  16.7 us (20%)
  Pallas kernels  15.9 us (19%)
  waiting for transfers between devices  7.67 us (9%)
  local copies, waits for them, and re-layouts  6.37 us (8%)
    all_to_all x1, blocking collectives, sum_over_vert(): lax.all_to_all(jnp.broadcast_to(share[None], parts.shape), 'z', 0, 0)  18.1 us
    all_to_all x1, blocking collectives, sum_over_vert(): share = jnp.sum(lax.all_to_all(parts, PLANE, 0, 0), axis=0)  9.86 us
    pallas_call x1, Pallas kernels, body(): pl.pallas_call(second_kernel, out_shape=tile, in_specs=[smem()] + [vmem()...  9.65 us
    all_to_all x1, blocking collectives, sum_over_vert(): lax.all_to_all(jnp.broadcast_to(share[None], parts.shape), PLANE, 0, 0)  8.56 us
    pallas_call x1, Pallas kernels, body(): pl.pallas_call(first_kernel, out_shape=(tile, jax.ShapeDtypeStruct((ROW_C...  6.22 us
    ppermute x1, waiting for transfers between devices, body(): f_edge = lax.ppermute(edge_rows(distribution, forward), 'gx', SWAP)  5.39 us
    unnamed x10, local copies, waits for them, and re-layouts  5.17 us
    ppermute x1, starting transfers between devices, body(): total_near = lax.ppermute(total, 'gy', SWAP)  4.01 us
  transfers between devices with their start and end apart: 8, of which 3 were waited for; matrix products, arithmetic and copies ran while one was open for 1% of the time, Pallas kernels for 0%

profile of v2, /device:TPU:1, one launch (start us, length us, event | category | flops | bytes accessed | tf_op | source)
XLA Modules:
  0.0 83.2 jit_solution(10238505448806427610)
XLA Ops:
  0.0 3.2 %collective-permute-start = (f32[125,32,128]{2,1,0:T(8,128)}, f32[125,32,128]{2,1,0:T(8,128)S(1)}, u32[]{:S(2)}, u32[]{:S(2)}) collective-permute-start(f32[125,32,128]{2,1,0:T(8,128)} %f.1), channel_id=1, source_target_pairs={{0,64},{64,0},{1,65},{65,1},{2,66},{66,2},{3,67},{67,3},{4,68},{68... | collective-permute-start | bytes 6144008 | tf_op jit(solution)/shard_map/ppermute | solution.py:389
  3.2 1.1 %constant_dynamic-slice_fusion.1 = f32[125,2,128]{2,1,0:T(2,128)S(1)} fusion(f32[125,32,128]{2,1,0:T(8,128)} %f.1, s32[]{:T(128)S(6)} %select_n.7), kind=kLoop, calls=%fused_computation.2 | loop fusion | bytes 256004 | tf_op jit(solution)/shard_map/dynamic_slice | solution.py:380
  4.3 1.3 %collective-permute-start.1 = (f32[125,2,128]{2,1,0:T(2,128)S(1)}, f32[125,2,128]{2,1,0:T(2,128)S(1)}, u32[]{:S(2)}, u32[]{:S(2)}) collective-permute-start(f32[125,2,128]{2,1,0:T(2,128)S(1)} %constant_dynamic-slice_fusion.1), channel_id=1, source_target_pairs={{0,128},{128,0},{1,129},{129,1},{2,130},{130,2},{3,131},{131,3},{4... | collective-permute-start | bytes 384008 | tf_op jit(solution)/shard_map/ppermute | solution.py:388
  5.6 5.4 %collective-permute-done.1.f_edge = f32[125,2,128]{2,1,0:T(2,128)S(1)} collective-permute-done((f32[125,2,128]{2,1,0:T(2,128)S(1)}, f32[125,2,128]{2,1,0:T(2,128)S(1)}, u32[]{:S(2)}, u32[]{:S(2)}) %collective-permute-start.1) | collective-permute-done | bytes 128032 | tf_op jit(solution)/shard_map/ppermute | solution.py:388
  11.0 0.0 collective-permute-done.f_near
  11.0 0.0 copy-start.1
  11.0 1.3 %copy-done.1 = f32[125,32,128]{2,1,0:T(8,128)} copy-done((f32[125,32,128]{2,1,0:T(8,128)}, f32[125,32,128]{2,1,0:T(8,128)S(1)}, u32[]{:S(2)}) %copy-start.1) | copy-done | bytes 2048024
  12.3 0.0 copy-start
  12.3 1.6 %copy-done = f32[125,32,128]{2,1,0:T(8,128)S(1)} copy-done((f32[125,32,128]{2,1,0:T(8,128)S(1)}, f32[125,32,128]{2,1,0:T(8,128)}, u32[]{:S(2)}) %copy-start) | copy-done | bytes 2048024
  13.9 0.0 copy-start.2
  13.9 1.6 %copy-done.2 = f32[125,32,128]{2,1,0:T(8,128)S(1)} copy-done((f32[125,32,128]{2,1,0:T(8,128)S(1)}, f32[125,32,128]{2,1,0:T(8,128)}, u32[]{:S(2)}) %copy-start.2) | copy-done | bytes 2048024
  15.4 0.7 copy-done.3
  16.2 6.2 %move_and_sum.1 = (f32[125,32,128]{2,1,0:T(8,128)S(1)}, f32[512,128]{1,0:T(8,128)S(1)}) custom-call(s32[1]{0:T(128)} %bitcast.place, f32[125,32,128]{2,1,0:T(8,128)S(1)} %copy-done, f32[125,32,128]{2,1,0:T(8,128)S(1)} %copy-done.2, f32[125,2,128]{2,1,0:T(2,128)S(1)} %collective-permute-done.1.f_edge, f32[32,128]{1,0:T(8,128)S(1)} %copy-done.3), custom_call_target="tpu_custom_call" | custom-call | tf_op jit(solution)/shard_map/move_and_sum/pallas_call | solution.py:394
  22.4 0.0 copy-start.4
  22.4 0.9 %collective-permute-start.2 = (f32[125,32,128]{2,1,0:T(8,128)S(1)}, f32[125,32,128]{2,1,0:T(8,128)}, u32[]{:S(2)}, u32[]{:S(2)}) collective-permute-start(f32[125,32,128]{2,1,0:T(8,128)S(1)} %get-tuple-element.7.kept), channel_id=1, source_target_pairs={{0,64},{64,0},{1,65},{65,1},{2,66},{66,2},{3,67},{67,3},{4,68},{68... | collective-permute-start | bytes 6144008 | tf_op jit(solution)/shard_map/ppermute | solution.py:407
  23.3 9.9 %all_to_all.15 = f32[8,8,8,128]{3,2,1,0:T(8,128)S(1)} all-to-all(f32[8,8,8,128]{3,2,1,0:T(8,128)S(1)} %bitcast.6), channel_id=1, replica_groups=mesh['gx'=2,'gy'=2,'x'=4,'yl'=2,'z'=8] {'x','yl'}, dimensions={0} | all-to-all | bytes 524288 | tf_op jit(solution)/shard_map/all_to_all | solution.py:372
  33.2 18.1 %all_to_all.16 = f32[8,8,8,128]{3,2,1,0:T(8,128)S(1)} all-to-all(f32[8,8,8,128]{3,2,1,0:T(8,128)S(1)} %broadcast_in_dim.4), channel_id=1, replica_groups=mesh['gx'=2,'gy'=2,'x'=4,'yl'=2,'z'=8] {'z'}, dimensions={0} | all-to-all | bytes 524288 | tf_op jit(solution)/shard_map/all_to_all | solution.py:373
  51.3 8.6 %all_to_all.17 = f32[8,8,8,128]{3,2,1,0:T(8,128)S(1)} all-to-all(f32[8,8,8,128]{3,2,1,0:T(8,128)S(1)} %broadcast_in_dim.5), channel_id=1, replica_groups=mesh['gx'=2,'gy'=2,'x'=4,'yl'=2,'z'=8] {'x','yl'}, dimensions={0} | all-to-all | bytes 524288 | tf_op jit(solution)/shard_map/all_to_all | solution.py:374
  59.8 4.0 %collective-permute-start.4 = (f32[512,128]{1,0:T(8,128)S(1)}, f32[512,128]{1,0:T(8,128)S(1)}, u32[]{:S(2)}, u32[]{:S(2)}) collective-permute-start(f32[512,128]{1,0:T(8,128)S(1)} %bitcast.3), channel_id=1, source_target_pairs={{0,64},{64,0},{1,65},{65,1},{2,66},{66,2},{3,67},{67,3},{4,68},{68... | collective-permute-start | bytes 786440 | tf_op jit(solution)/shard_map/ppermute | solution.py:409
  63.9 0.0 copy-done.4
  63.9 0.1 constant_dynamic-slice_fusion
  63.9 2.7 %collective-permute-start.3 = (f32[125,2,128]{2,1,0:T(2,128)S(1)}, f32[125,2,128]{2,1,0:T(2,128)S(1)}, u32[]{:S(2)}, u32[]{:S(2)}) collective-permute-start(f32[125,2,128]{2,1,0:T(2,128)S(1)} %constant_dynamic-slice_fusion), channel_id=1, source_target_pairs={{0,128},{128,0},{1,129},{129,1},{2,130},{130,2},{3,131},{131,3},{4... | collective-permute-start | bytes 384008 | tf_op jit(solution)/shard_map/ppermute | solution.py:406
  66.6 0.3 collective-permute-start.5
  67.0 2.6 %collective-permute-start.7 = (f32[4,128]{1,0:T(4,128)S(1)}, f32[4,128]{1,0:T(4,128)S(1)}, u32[]{:S(2)}, u32[]{:S(2)}) collective-permute-start(f32[4,128]{1,0:T(4,128)S(1)} %pad_maximum_fusion), channel_id=1, source_target_pairs={{0,128},{128,0},{1,129},{129,1},{2,130},{130,2},{3,131},{131,3},{4... | collective-permute-start | bytes 6152 | tf_op jit(solution)/shard_map/ppermute | solution.py:391
  69.6 1.4 %collective-permute-done.7.rate_edge = f32[4,128]{1,0:T(4,128)S(1)} collective-permute-done((f32[4,128]{1,0:T(4,128)S(1)}, f32[4,128]{1,0:T(4,128)S(1)}, u32[]{:S(2)}, u32[]{:S(2)}) %collective-permute-start.7) | collective-permute-done | bytes 2080 | tf_op jit(solution)/shard_map/ppermute | solution.py:391
  71.1 1.6 %collective-permute-start.6 = (f32[32,128]{1,0:T(8,128)S(1)}, f32[32,128]{1,0:T(8,128)S(1)}, u32[]{:S(2)}, u32[]{:S(2)}) collective-permute-start(f32[32,128]{1,0:T(8,128)S(1)} %copy-done.4), channel_id=1, source_target_pairs={{0,64},{64,0},{1,65},{65,1},{2,66},{66,2},{3,67},{67,3},{4,68},{68... | collective-permute-start | bytes 49160 | tf_op jit(solution)/shard_map/ppermute | solution.py:390
  72.7 0.8 %collective-permute-done.6.rate_near = f32[32,128]{1,0:T(8,128)S(1)} collective-permute-done((f32[32,128]{1,0:T(8,128)S(1)}, f32[32,128]{1,0:T(8,128)S(1)}, u32[]{:S(2)}, u32[]{:S(2)}) %collective-permute-start.6) | collective-permute-done | bytes 16416 | tf_op jit(solution)/shard_map/ppermute | solution.py:390
  73.5 0.0 collective-permute-done.3.kept_edge
  73.5 0.0 collective-permute-done.5.total_edge
  73.5 0.0 collective-permute-done.4.total_near
  73.5 0.0 collective-permute-done.2.kept_near
  73.5 9.6 %collide_move_collide.1 = f32[125,32,128]{2,1,0:T(8,128)} custom-call(s32[1]{0:T(128)} %bitcast.place, f32[125,32,128]{2,1,0:T(8,128)S(1)} %get-tuple-element.7.kept, f32[125,32,128]{2,1,0:T(8,128)} %collective-permute-done.2.kept_near, f32[125,2,128]{2,1,0:T(2,128)S(1)} %collective-permute-done.3.kept_edge, f32[512,128]{1,0:T(8,128)S(1)} %bitcast.5, ...), custom_call_target="tpu_custom_call" | custom-call | tf_op jit(solution)/shard_map/collide_move_collide/pallas_call | solution.py:411
  (8 shorter events, 0.1 us)
Async XLA Ops:
  0.0 11.0 %collective-permute-start = (f32[125,32,128]{2,1,0:T(8,128)}, f32[125,32,128]{2,1,0:T(8,128)S(1)}, u32[]{:S(2)}, u32[]{:S(2)}) collective-permute-start(f32[125,32,128]{2,1,0:T(8,128)} %f.1), channel_id=1, source_target_pairs={{0,64},{64,0},{1,65},{65,1},{2,66},{66,2},{3,67},{67,3},{4,68},{68... | collective-permute-start | bytes 6144008 | tf_op jit(solution)/shard_map/ppermute | solution.py:389
  4.3 6.7 %collective-permute-start.1 = (f32[125,2,128]{2,1,0:T(2,128)S(1)}, f32[125,2,128]{2,1,0:T(2,128)S(1)}, u32[]{:S(2)}, u32[]{:S(2)}) collective-permute-start(f32[125,2,128]{2,1,0:T(2,128)S(1)} %constant_dynamic-slice_fusion.1), channel_id=1, source_target_pairs={{0,128},{128,0},{1,129},{129,1},{2,130},{130,2},{3,131},{131,3},{4... | collective-permute-start | bytes 384008 | tf_op jit(solution)/shard_map/ppermute | solution.py:388
  11.0 1.3 %copy-start.1 = (f32[125,32,128]{2,1,0:T(8,128)}, f32[125,32,128]{2,1,0:T(8,128)S(1)}, u32[]{:S(2)}) copy-start(f32[125,32,128]{2,1,0:T(8,128)S(1)} %collective-permute-done.f_near) | copy-start | bytes 6144004
  12.3 1.6 %copy-start = (f32[125,32,128]{2,1,0:T(8,128)S(1)}, f32[125,32,128]{2,1,0:T(8,128)}, u32[]{:S(2)}) copy-start(f32[125,32,128]{2,1,0:T(8,128)} %f.1) | copy-start | bytes 6144004
  13.9 1.6 %copy-start.2 = (f32[125,32,128]{2,1,0:T(8,128)S(1)}, f32[125,32,128]{2,1,0:T(8,128)}, u32[]{:S(2)}) copy-start(f32[125,32,128]{2,1,0:T(8,128)} %copy-done.1) | copy-start | bytes 6144004
  15.4 0.7 copy-start.3
  22.4 41.5 %copy-start.4 = (f32[32,128]{1,0:T(8,128)S(1)}, f32[32,128]{1,0:T(8,128)}, u32[]{:S(2)}) copy-start(f32[32,128]{1,0:T(8,128)} %rate.3) | copy-start | bytes 49156
  22.4 51.1 %collective-permute-start.2 = (f32[125,32,128]{2,1,0:T(8,128)S(1)}, f32[125,32,128]{2,1,0:T(8,128)}, u32[]{:S(2)}, u32[]{:S(2)}) collective-permute-start(f32[125,32,128]{2,1,0:T(8,128)S(1)} %get-tuple-element.7.kept), channel_id=1, source_target_pairs={{0,64},{64,0},{1,65},{65,1},{2,66},{66,2},{3,67},{67,3},{4,68},{68... | collective-permute-start | bytes 6144008 | tf_op jit(solution)/shard_map/ppermute | solution.py:407
  59.8 13.7 %collective-permute-start.4 = (f32[512,128]{1,0:T(8,128)S(1)}, f32[512,128]{1,0:T(8,128)S(1)}, u32[]{:S(2)}, u32[]{:S(2)}) collective-permute-start(f32[512,128]{1,0:T(8,128)S(1)} %bitcast.3), channel_id=1, source_target_pairs={{0,64},{64,0},{1,65},{65,1},{2,66},{66,2},{3,67},{67,3},{4,68},{68... | collective-permute-start | bytes 786440 | tf_op jit(solution)/shard_map/ppermute | solution.py:409
  63.9 9.6 %collective-permute-start.3 = (f32[125,2,128]{2,1,0:T(2,128)S(1)}, f32[125,2,128]{2,1,0:T(2,128)S(1)}, u32[]{:S(2)}, u32[]{:S(2)}) collective-permute-start(f32[125,2,128]{2,1,0:T(2,128)S(1)} %constant_dynamic-slice_fusion), channel_id=1, source_target_pairs={{0,128},{128,0},{1,129},{129,1},{2,130},{130,2},{3,131},{131,3},{4... | collective-permute-start | bytes 384008 | tf_op jit(solution)/shard_map/ppermute | solution.py:406
  66.6 6.9 %collective-permute-start.5 = (f32[64,128]{1,0:T(8,128)S(1)}, f32[64,128]{1,0:T(8,128)S(1)}, u32[]{:S(2)}, u32[]{:S(2)}) collective-permute-start(f32[64,128]{1,0:T(8,128)S(1)} %slice.12), channel_id=1, source_target_pairs={{0,128},{128,0},{1,129},{129,1},{2,130},{130,2},{3,131},{131,3},{4... | collective-permute-start | bytes 98312 | tf_op jit(solution)/shard_map/ppermute | solution.py:410
  67.0 4.1 %collective-permute-start.7 = (f32[4,128]{1,0:T(4,128)S(1)}, f32[4,128]{1,0:T(4,128)S(1)}, u32[]{:S(2)}, u32[]{:S(2)}) collective-permute-start(f32[4,128]{1,0:T(4,128)S(1)} %pad_maximum_fusion), channel_id=1, source_target_pairs={{0,128},{128,0},{1,129},{129,1},{2,130},{130,2},{3,131},{131,3},{4... | collective-permute-start | bytes 6152 | tf_op jit(solution)/shard_map/ppermute | solution.py:391
  71.1 2.5 %collective-permute-start.6 = (f32[32,128]{1,0:T(8,128)S(1)}, f32[32,128]{1,0:T(8,128)S(1)}, u32[]{:S(2)}, u32[]{:S(2)}) collective-permute-start(f32[32,128]{1,0:T(8,128)S(1)} %copy-done.4), channel_id=1, source_target_pairs={{0,64},{64,0},{1,65},{65,1},{2,66},{66,2},{3,67},{67,3},{4,68},{68... | collective-permute-start | bytes 49160 | tf_op jit(solution)/shard_map/ppermute | solution.py:390

commit v3 on v0

v3 whole, which is shorter than its diff:
```python
import functools
import math

import jax
import jax.numpy as jnp
from jax import lax
from jax.experimental import pallas as pl
from jax.experimental.pallas import tpu as pltpu
from jax.sharding import Mesh
from jax.sharding import PartitionSpec as P

VG = 20
VEL_LOCAL = 125
CHUNK = 5
CHUNKS = VEL_LOCAL // CHUNK
STEPS = 5
STEP_CHUNKS = CHUNKS // STEPS
PIECE = VEL_LOCAL // STEPS
GROUPS = 7
ROWS = 32
LANES = 128

SPACING = 9.0 / VG
LOWEST = 4.5 * (1.0 / VG - 1.0)
DT = 0.3 / 4.5
WEIGHT = (9.0 / VG) ** 3 / (2.0 * math.pi) ** 1.5
SPEEDS = [LOWEST + SPACING * n for n in range(VG)]

VERT = ("x", "yl", "z")
PLANE = ("x", "yl")

ROW_SECOND = 5 * ROWS
ROW_SPILL_Y = 10 * ROWS
ROW_SPILL_X = 11 * ROWS
ROW_EDGE = 12 * ROWS
ROW_RATE = 13 * ROWS
ROW_COUNT = 14 * ROWS


def speed_of(index):
    return index.astype(jnp.float32) * SPACING + LOWEST


def lane_index():
    return lax.broadcasted_iota(jnp.int32, (ROWS, LANES), 1)


def other_plane(tile, even):
    return jnp.where(even, pltpu.roll(tile, LANES - 1, 1), pltpu.roll(tile, 1, 1))


def chunk_place(first, chunk):
    slot = lax.rem(first, VG) + chunk * CHUNK
    group = lax.div(slot, VG)
    whole = lax.div(first, VG) + group
    index_x = lax.div(whole, VG)
    return group, index_x, whole - index_x * VG, slot - group * VG


def y_part(center, near, sides):
    shift, one, two = sides
    far = pltpu.roll(jnp.where(two, near, center), shift, 1)
    return pltpu.roll(jnp.where(one, near, center) - 0.25 * far, shift, 1)


def upwind(center, back, x_one, x_two, even, coef_x, coef_y, coef_z):
    return (
        center * (1.0 - 1.5 * (coef_x + coef_y) - 2.0 * coef_z)
        + (2.0 * coef_x) * (x_one - 0.25 * x_two)
        + (2.0 * coef_y) * back
        + (2.0 * coef_z) * other_plane(center, even)
    )


def static_sides(positive):
    lane = lane_index()
    if positive:
        return 2, lane >= LANES - 2, lane >= LANES - 4
    return LANES - 2, lane < 2, lane < 4


def each_sign(positive, run):
    for value in (True, False):
        pl.when(positive if value else jnp.logical_not(positive))(functools.partial(run, value))


def x_steps(buf, slot, center, halo, forward):
    buf[slot, 8:40] = center
    if forward:
        buf[slot, 6:8] = halo
        return buf[slot, 7:39], buf[slot, 6:38]
    buf[slot, 40:42] = halo
    return buf[slot, 9:41], buf[slot, 10:42]


def load_piece(f, held, sem, piece):
    rows = pl.ds(piece * PIECE, PIECE)
    return pltpu.make_async_copy(f.at[rows], held.at[rows], sem.at[piece])


def send_kernel(place, f, out, band, sem):
    def take(forward):
        copy = pltpu.make_async_copy(f.at[:, pl.ds(24 if forward else 0, 8)], band, sem)
        copy.start()
        copy.wait()
        out[...] = band[:, 6:8] if forward else band[:, 0:2]

    each_sign(place[0] >= 32, take)


def inside_kernel(
    place, f, f_near, rate, kept, kept_edge, groups, held, held_near, held_rate, buf, sem, sem_near,
    sem_rate,
):
    rate_copy = pltpu.make_async_copy(rate, held_rate, sem_rate)
    rate_copy.start()
    for piece in range(STEPS):
        load_piece(f, held, sem, piece).start()
        load_piece(f_near, held_near, sem_near, piece).start()
    rate_copy.wait()
    device = place[0]
    first = device * VEL_LOCAL
    even = lax.rem(lane_index(), 2) == 0
    keep = 1.0 - held_rate[...]
    groups[...] = jnp.zeros_like(groups)

    def move(forward):
        def chunk(c, carry):
            group, index_x, index_y, index_z = chunk_place(first, c)
            coef_x = DT * jnp.abs(speed_of(index_x))
            coef_y = DT * jnp.abs(speed_of(index_y))
            side = jnp.where(index_z >= VG // 2, 1.0, -1.0)

            def run(rising):
                sides = static_sides(rising)
                acc = [None] * 4
                for t in range(CHUNK):
                    v = c * CHUNK + t
                    center = held[v]
                    x_one, x_two = x_steps(
                        buf, t, center, jnp.zeros((2, LANES), jnp.float32), forward
                    )
                    speed_z = speed_of(index_z + t)
                    back = y_part(center, held_near[v], sides)
                    moved = upwind(
                        center, back, x_one, x_two, even, coef_x, coef_y, DT * speed_z * side
                    )
                    left = keep * moved
                    kept[v] = left
                    kept_edge[v] = left[30:32] if forward else left[0:2]
                    power = moved
                    for k in range(4):
                        acc[k] = power if acc[k] is None else acc[k] + power
                        if k < 3:
                            power = power * speed_z
                for k in range(3):
                    groups[group, k] += acc[k]
                    groups[group, 3 + k] += side * acc[k + 1]

            each_sign(index_y >= VG // 2, run)
            return carry

        def piece(p, carry):
            load_piece(f, held, sem, p).wait()
            load_piece(f_near, held_near, sem_near, p).wait()
            return lax.fori_loop(p * STEP_CHUNKS, (p + 1) * STEP_CHUNKS, chunk, carry)

        lax.fori_loop(0, STEPS, piece, 0)

    each_sign(device >= 32, move)


def edge_kernel(
    place, kept_in, groups_in, f_edge, rate, kept, sums, groups, edge, buf, sem
):
    del kept_in
    device = place[0]
    first = device * VEL_LOCAL
    groups[...] = groups_in[...]
    even = lax.rem(lane_index(), 2) == 0
    keep = 1.0 - rate[...]

    def enter(forward):
        rows = slice(0, 2) if forward else slice(30, 32)
        inner = slice(0, 2) if forward else slice(6, 8)
        none = jnp.zeros((1, LANES), jnp.float32)
        band = kept.at[:, pl.ds(0 if forward else 24, 8)]
        load = pltpu.make_async_copy(band, edge, sem)
        load.start()
        load.wait()

        def chunk(c, carry):
            group, index_x, _, index_z = chunk_place(first, c)
            coef = (2.0 * DT) * jnp.abs(speed_of(index_x))
            side = jnp.where(index_z >= VG // 2, 1.0, -1.0)
            acc = [None] * 4
            for t in range(CHUNK):
                v = c * CHUNK + t
                halo = f_edge[v]
                one = [halo[1:2], none] if forward else [none, halo[0:1]]
                power = coef * (jnp.concatenate(one, axis=0) - 0.25 * halo)
                edge[v, inner] += keep[rows] * power
                speed_z = speed_of(index_z + t)
                for k in range(4):
                    acc[k] = power if acc[k] is None else acc[k] + power
                    if k < 3:
                        power = power * speed_z
            for k in range(3):
                groups[group, k, rows] += acc[k]
                groups[group, 3 + k, rows] += side * acc[k + 1]
            return carry

        lax.fori_loop(0, CHUNKS, chunk, 0)
        store = pltpu.make_async_copy(edge, band, sem)
        store.start()
        return store

    def spread(forward):
        def one(group, carry):
            whole = lax.div(first, VG) + group
            index_x = lax.div(whole, VG)
            index_y = whole - index_x * VG
            speed_x = speed_of(index_x)
            speed_y = speed_of(index_y)
            coef_x = DT * jnp.abs(speed_x)
            coef_y = DT * jnp.abs(speed_y)
            squares = speed_x * speed_x + speed_y * speed_y

            def five(parts):
                return (
                    parts[0],
                    speed_x * parts[0],
                    speed_y * parts[0],
                    parts[1],
                    squares * parts[0] + parts[2],
                )

            def run(rising):
                sides = static_sides(rising)
                level = [WEIGHT * groups[group, k] for k in range(6)]
                for m, value in enumerate(five(level)):
                    sums[ROWS * m : ROWS * (m + 1)] += value
                second, near_y, near_x = [], [], []
                for k in range(3):
                    center = keep * level[k]
                    absolute = keep * level[3 + k]
                    x_one, x_two = x_steps(
                        buf, k, center, jnp.zeros((2, LANES), jnp.float32), forward
                    )
                    second.append(
                        center * (1.0 - 1.5 * (coef_x + coef_y))
                        - (2.0 * DT) * (absolute - other_plane(absolute, even))
                        + (2.0 * coef_x) * (x_one - 0.25 * x_two)
                        + (2.0 * coef_y) * y_part(center, 0.0, sides)
                    )
                    near_y.append(coef_y * jnp.where(sides[2], center, 0.0))
                    near_x.append(coef_x * (center[30:32] if forward else center[0:2]))
                for m, value in enumerate(five(second)):
                    sums[ROW_SECOND + ROWS * m : ROW_SECOND + ROWS * (m + 1)] += value
                for m, value in enumerate(five(near_x)):
                    at = ROW_SPILL_X + 4 * m + (0 if forward else 2)
                    sums[at : at + 2] += value
                packed = sums[ROW_SPILL_Y : ROW_SPILL_Y + ROWS]
                for m, value in enumerate(five(near_y)):
                    packed = packed + (pltpu.roll(value, 8 * m, 1) if m else value)
                sums[ROW_SPILL_Y : ROW_SPILL_Y + ROWS] = packed

            each_sign(index_y >= VG // 2, run)
            return carry

        lax.fori_loop(0, GROUPS, one, 0)

    sums[...] = jnp.zeros_like(sums)

    def both(forward):
        store = enter(forward)
        spread(forward)
        store.wait()

    each_sign(device >= 32, both)
    for m in range(5):
        at = ROW_EDGE + 4 * m
        sums[at : at + 2] = sums[ROWS * m + 30 : ROWS * m + 32]
        sums[at + 2 : at + 4] = sums[ROWS * m : ROWS * m + 2]

    @pl.when(device == 0)
    def _():
        at = ROW_EDGE + 20
        sums[at : at + 2] = rate[30:32]
        sums[at + 2 : at + 4] = rate[0:2]
        sums[ROW_RATE : ROW_RATE + ROWS] = rate[...]


def parameters(moments):
    density = moments[0]
    share = 1.0 / density
    flow_x = moments[1] * share
    flow_y = moments[2] * share
    flow_z = moments[3] * share
    temper = (moments[4] * share - (flow_x * flow_x + flow_y * flow_y + flow_z * flow_z)) / 3.0
    return density / (temper * jnp.sqrt(temper)), flow_x, flow_y, flow_z, 0.5 / temper


def products(part_x, part_y, part_z):
    yz = part_y[0] * part_z[0]
    return (
        part_x[0] * yz,
        part_x[1] * yz,
        part_x[0] * (part_y[1] * part_z[0]),
        part_x[0] * (part_y[0] * part_z[1]),
        part_x[2] * yz + part_x[0] * (part_y[2] * part_z[0] + part_y[0] * part_z[2]),
    )


def one_block(at, moments, rate, base, tables, kinds, wanted):
    amp, flow_x, flow_y, flow_z, inv = parameters(moments)
    scale = amp * rate
    base[at] = scale
    full, plus, minus = [], [], []
    for d, flow in enumerate((flow_x, flow_y, flow_z)):
        halves = []
        for half in range(2):
            level = [None] * 4
            for n in range(half * 10, half * 10 + 10):
                gap = SPEEDS[n] - flow
                value = jnp.exp(-(inv * gap * gap))
                tables[d, n, at] = value
                for k in range(4):
                    term = value if k == 0 else value * (SPEEDS[n] ** k)
                    level[k] = term if level[k] is None else level[k] + term
            halves.append(level)
        full.append([halves[0][k] + halves[1][k] for k in range(3)])
        plus.append([halves[1][k + 1] for k in range(3)])
        minus.append([-halves[0][k + 1] for k in range(3)])
    scale = scale * WEIGHT
    x, y, z = [scale * part for part in full[0]], full[1], full[2]
    sets = {}
    if "x" in wanted:
        sets[0] = products([scale * part for part in plus[0]], y, z)
        sets[1] = products([scale * part for part in minus[0]], y, z)
    if "y" in wanted:
        sets[2] = products(x, plus[1], z)
        sets[3] = products(x, minus[1], z)
    if "z" in wanted:
        sets[4] = products(x, y, [plus[2][k] + minus[2][k] for k in range(3)])
        whole = products(x, y, z)
        sets[5] = [
            whole[m]
            - (1.5 * DT) * ((sets[0][m] + sets[1][m]) + (sets[2][m] + sets[3][m]))
            - (2.0 * DT) * sets[4][m]
            for m in range(5)
        ]
    for s, values in sets.items():
        for m in range(5):
            kinds[s, m, at] = values[m]


def table_kernel(wanted, total, rate, base, tables, kinds):
    def block(b, carry):
        def rows(start):
            return pl.ds(pl.multiple_of(start + b * 8, 8), 8)

        one_block(
            rows(0), [total[rows(ROWS * m)] for m in range(5)], rate[rows(0)], base, tables, kinds,
            wanted,
        )
        return carry

    lax.fori_loop(0, ROWS // 8, block, 0)


def second_kernel(
    place, kept, kept_near, kept_edge, total, total_near, total_edge, rate,
    base, tables, kinds, base_near, tables_near, kinds_near,
    out, base_edge, tables_edge, kinds_edge, table_two, done, buf, sem,
):
    device = place[0]
    first = device * VEL_LOCAL
    even = lax.rem(lane_index(), 2) == 0
    keep = 1.0 - rate[...]

    def edge(row):
        rows = total_edge[row : row + 4]
        return jnp.concatenate([rows, rows], axis=0)

    one_block(
        slice(0, 8), [edge(ROWS + 4 * m) for m in range(5)], edge(ROWS + 20), base_edge,
        tables_edge, kinds_edge, "x",
    )
    spill_y = total_near[ROW_SPILL_Y : ROW_SPILL_Y + ROWS]
    moments = []
    for m in range(5):
        result = total[ROW_SECOND + ROWS * m : ROW_SECOND + ROWS * (m + 1)] + kinds[5, m]
        x_one, x_two = x_steps(
            buf, 0, kinds[0, m],
            kinds_edge[0, m, 0:2] + (1.0 / DT) * total_edge[4 * m : 4 * m + 2], True,
        )
        x_low, x_lower = x_steps(
            buf, 1, kinds[1, m],
            kinds_edge[1, m, 2:4] + (1.0 / DT) * total_edge[4 * m + 2 : 4 * m + 4], False,
        )
        spill = pltpu.roll(spill_y, LANES - 8 * m, 1) if m else spill_y
        spill = (1.0 / DT) * spill
        moments.append(
            result
            + (2.0 * DT)
            * (
                other_plane(kinds[4, m], even)
                + (x_one - 0.25 * x_two)
                + (x_low - 0.25 * x_lower)
                + y_part(kinds[2, m], kinds_near[2, m] + spill, static_sides(True))
                + y_part(kinds[3, m], kinds_near[3, m] + spill, static_sides(False))
            )
        )
    amp, flow_x, flow_y, flow_z, inv = parameters(moments)
    for n in range(VG):
        gap = SPEEDS[n] - flow_z
        table_two[n] = jnp.exp(-(inv * gap * gap))
    table_two[VG] = amp * rate[...]
    table_two[VG + 1] = flow_x
    table_two[VG + 2] = flow_y
    table_two[VG + 3] = inv


    def move(forward):
        row = 0 if forward else 2

        def chunk(c, carry):
            group, index_x, index_y, index_z = chunk_place(first, c)
            speed_x = speed_of(index_x)
            speed_y = speed_of(index_y)
            coef_x = DT * jnp.abs(speed_x)
            coef_y = DT * jnp.abs(speed_y)
            side = jnp.where(index_z >= VG // 2, 1.0, -1.0)

            def run(rising):
                sides = static_sides(rising)
                front = base[...] * tables[0, index_x] * tables[1, index_y]
                front_near = base_near[...] * tables_near[0, index_x] * tables_near[1, index_y]
                front_edge = base_edge[...] * tables_edge[0, index_x] * tables_edge[1, index_y]
                gap_x = speed_x - table_two[VG + 1]
                gap_y = speed_y - table_two[VG + 2]
                front_two = table_two[VG] * jnp.exp(
                    -(table_two[VG + 3] * (gap_x * gap_x + gap_y * gap_y))
                )
                for t in range(CHUNK):
                    v = c * CHUNK + t
                    n = index_z + t
                    center = kept[v] + front * tables[2, n]
                    near = kept_near[v] + front_near * tables_near[2, n]
                    halo = kept_edge[v] + (front_edge * tables_edge[2, n])[row : row + 2]
                    x_one, x_two = x_steps(buf, t, center, halo, forward)
                    moved = upwind(
                        center, y_part(center, near, sides), x_one, x_two, even, coef_x, coef_y,
                        DT * speed_of(n) * side,
                    )
                    done[v] = keep * moved + front_two * table_two[n]

            each_sign(index_y >= VG // 2, run)
            return carry

        def piece(p, carry):
            lax.fori_loop(p * STEP_CHUNKS, (p + 1) * STEP_CHUNKS, chunk, 0)
            load_piece(done, out, sem, p).start()
            return carry

        lax.fori_loop(0, STEPS, piece, 0)

    each_sign(device >= 32, move)
    for piece in range(STEPS):
        load_piece(done, out, sem, piece).wait()


def vmem():
    return pl.BlockSpec(memory_space=pltpu.VMEM)


def in_hbm(x):
    return pltpu.with_memory_space_constraint(x, pltpu.HBM)


def hbm():
    return pl.BlockSpec(memory_space=pltpu.HBM)


def anywhere():
    return pl.BlockSpec(memory_space=pl.ANY)


def smem():
    return pl.BlockSpec(memory_space=pltpu.SMEM)


SWAP = [(0, 1), (1, 0)]


def sum_over_vert(partial, beside):
    parts = partial.reshape(8, -1, 8, LANES)
    share = jnp.sum(lax.all_to_all(parts, PLANE, 0, 0), axis=0)
    share = jnp.sum(lax.all_to_all(jnp.broadcast_to(share[None], parts.shape), "z", 0, 0), axis=0)
    share, beside = lax.optimization_barrier((share, beside))
    whole = lax.all_to_all(jnp.broadcast_to(share[None], parts.shape), PLANE, 0, 0)
    return whole.reshape(ROW_COUNT, LANES), beside


def f32(*shape):
    return jax.ShapeDtypeStruct(shape, jnp.float32)


def tables_of(total, rate, wanted, name):
    return pl.pallas_call(
        functools.partial(table_kernel, wanted),
        out_shape=(
            f32(ROWS, LANES), f32(3, VG, ROWS, LANES), f32(6, 5, ROWS, LANES)
        ),
        in_specs=[vmem(), vmem()],
        out_specs=(vmem(), vmem(), vmem()),
        compiler_params=pltpu.CompilerParams(vmem_limit_bytes=16 * 2**20),
        cost_estimate=pl.CostEstimate(flops=8000000, bytes_accessed=3000000, transcendentals=250000),
        name=name,
    )(total, rate)


def body(distribution, collision_rate):
    device = lax.axis_index(VERT)
    place = device.astype(jnp.int32).reshape(1)
    f_edge = pl.pallas_call(
        send_kernel,
        out_shape=f32(VEL_LOCAL, 2, LANES),
        in_specs=[smem(), hbm()],
        out_specs=vmem(),
        scratch_shapes=[pltpu.VMEM((VEL_LOCAL, 8, LANES), jnp.float32), pltpu.SemaphoreType.DMA],
        compiler_params=pltpu.CompilerParams(vmem_limit_bytes=24 * 2**20),
        cost_estimate=pl.CostEstimate(flops=0, bytes_accessed=600000, transcendentals=0),
        name="send_rows",
    )(place, in_hbm(distribution))
    f_edge = lax.ppermute(f_edge, "gx", SWAP)
    f_near = lax.ppermute(distribution, "gy", SWAP)
    kept, kept_edge, groups = pl.pallas_call(
        inside_kernel,
        out_shape=(
            f32(VEL_LOCAL, ROWS, LANES), f32(VEL_LOCAL, 2, LANES), f32(GROUPS, 6, ROWS, LANES)
        ),
        in_specs=[smem(), hbm(), hbm(), hbm()],
        out_specs=(vmem(), vmem(), vmem()),
        scratch_shapes=[
            pltpu.VMEM((VEL_LOCAL, ROWS, LANES), jnp.float32),
            pltpu.VMEM((VEL_LOCAL, ROWS, LANES), jnp.float32),
            pltpu.VMEM((ROWS, LANES), jnp.float32),
            pltpu.VMEM((CHUNK, 48, LANES), jnp.float32),
            pltpu.SemaphoreType.DMA((STEPS,)),
            pltpu.SemaphoreType.DMA((STEPS,)),
            pltpu.SemaphoreType.DMA,
        ],
        compiler_params=pltpu.CompilerParams(vmem_limit_bytes=16 * 2**20),
        cost_estimate=pl.CostEstimate(flops=50000000, bytes_accessed=6000000, transcendentals=0),
        name="move_inside",
    )(place, in_hbm(distribution), in_hbm(f_near), in_hbm(collision_rate))
    kept_edge = lax.ppermute(kept_edge, "gx", SWAP)
    kept, partial = pl.pallas_call(
        edge_kernel,
        out_shape=(f32(VEL_LOCAL, ROWS, LANES), f32(ROW_COUNT, LANES)),
        in_specs=[smem(), anywhere()] + [vmem()] * 3,
        out_specs=(anywhere(), vmem()),
        scratch_shapes=[
            pltpu.VMEM((GROUPS, 6, ROWS, LANES), jnp.float32),
            pltpu.VMEM((VEL_LOCAL, 8, LANES), jnp.float32),
            pltpu.VMEM((CHUNK, 48, LANES), jnp.float32),
            pltpu.SemaphoreType.DMA,
        ],
        input_output_aliases={1: 0},
        compiler_params=pltpu.CompilerParams(vmem_limit_bytes=16 * 2**20),
        name="enter_and_sum",
    )(place, kept, groups, f_edge, collision_rate)
    kept_near = lax.ppermute(kept, "gy", SWAP)
    total, kept_edge = sum_over_vert(partial, kept_edge)
    total_near = lax.ppermute(total, "gy", SWAP)
    total_edge = lax.ppermute(total[ROW_SPILL_X : ROW_EDGE + ROWS], "gx", SWAP)
    own = tables_of(total, collision_rate, "xyz", "tables_own")
    near = tables_of(total_near, total_near[ROW_RATE : ROW_RATE + ROWS], "y", "tables_near")
    return pl.pallas_call(
        second_kernel,
        out_shape=f32(VEL_LOCAL, ROWS, LANES),
        in_specs=[smem()] + [vmem()] * 13,
        out_specs=anywhere(),
        scratch_shapes=[
            pltpu.VMEM((8, LANES), jnp.float32),
            pltpu.VMEM((3, VG, 8, LANES), jnp.float32),
            pltpu.VMEM((2, 5, 8, LANES), jnp.float32),
            pltpu.VMEM((VG + 4, ROWS, LANES), jnp.float32),
            pltpu.VMEM((VEL_LOCAL, ROWS, LANES), jnp.float32),
            pltpu.VMEM((CHUNK, 48, LANES), jnp.float32),
            pltpu.SemaphoreType.DMA((STEPS,)),
        ],
        compiler_params=pltpu.CompilerParams(vmem_limit_bytes=24 * 2**20),
        name="collide_move_collide",
    )(
        place, kept, kept_near, kept_edge, total, total_near, total_edge, collision_rate, *own,
        *near,
    )


def solution(mesh):
    split = Mesh(mesh.devices.reshape(2, 2, 4, 2, 8), ("gx", "gy", "x", "yl", "z"))
    placed = (P(VERT, "gx", "gy"), P("gx", "gy"))
    return jax.shard_map(
        body, mesh=split, in_specs=placed, out_specs=P(VERT, "gx", "gy"), check_vma=False
    )
```

time: 1150 us -> 70.2 us (0.06)
  the two profiles are of different devices: /device:TPU:16 before, /device:TPU:1 now
where the time goes in v3:
time: 70.2 us; the launch traced here: 69.9 us
  starting transfers between devices  22.1 us (31%)
  Pallas kernels  19.7 us (28%)
  blocking collectives  18.7 us (27%)
  waiting for transfers between devices  8.51 us (12%)
  local copies, waits for them, and re-layouts  0.73 us (1%)
    all_to_all x1, blocking collectives, sum_over_vert(): lax.all_to_all(jnp.broadcast_to(share[None], parts.shape), PLANE, 0, 0)  9.56 us
    all_to_all x1, blocking collectives, sum_over_vert(): share = jnp.sum(lax.all_to_all(parts, PLANE, 0, 0), axis=0)  9.12 us
    all_to_all x1, starting transfers between devices, sum_over_vert(): lax.all_to_all(jnp.broadcast_to(share[None], parts.shape), 'z', 0, 0)  8.17 us
    pallas_call x1, Pallas kernels, body(): pl.pallas_call(second_kernel, out_shape=f32(VEL_LOCAL, ROWS, LANES), in_s...  8.02 us
    pallas_call x1, Pallas kernels, body(): pl.pallas_call(inside_kernel, out_shape=(f32(VEL_LOCAL, ROWS, LANES), f32...  7.19 us
    all_to_all x1, waiting for transfers between devices, sum_over_vert(): lax.all_to_all(jnp.broadcast_to(share[None], parts.shape), 'z', 0, 0)  6.26 us
    ppermute x1, starting transfers between devices, body(): total_near = lax.ppermute(total, 'gy', SWAP)  3.73 us
    ppermute x1, starting transfers between devices, body(): f_near = lax.ppermute(distribution, 'gy', SWAP)  3.24 us
  transfers between devices with their start and end apart: 7, of which 3 were waited for; matrix products, arithmetic and copies ran while one was open for 1% of the time, Pallas kernels for 13%

profile of v3, /device:TPU:1, one launch (start us, length us, event | category | flops | bytes accessed | tf_op | source)
XLA Modules:
  0.0 69.9 jit_solution(6666943729068953852)
XLA Ops:
  0.0 3.2 %collective-permute-start = (f32[125,32,128]{2,1,0:T(8,128)}, f32[125,32,128]{2,1,0:T(8,128)}, u32[]{:S(2)}, u32[]{:S(2)}) collective-permute-start(f32[125,32,128]{2,1,0:T(8,128)} %f.3), channel_id=1, source_target_pairs={{0,64},{64,0},{1,65},{65,1},{2,66},{66,2},{3,67},{67,3},{4,68},{68... | collective-permute-start | bytes 6144008 | tf_op jit(solution)/shard_map/ppermute | solution.py:538
  3.2 1.1 %send_rows.1 = f32[125,2,128]{2,1,0:T(2,128)S(1)} custom-call(s32[1]{0:T(128)} %bitcast.place, f32[125,32,128]{2,1,0:T(8,128)} %f.3), custom_call_target="tpu_custom_call" | custom-call | bytes 600000 | tf_op jit(solution)/shard_map/send_rows/pallas_call | solution.py:527
  4.3 0.0 copy-start
  4.3 1.3 %collective-permute-start.1 = (f32[125,2,128]{2,1,0:T(2,128)S(1)}, f32[125,2,128]{2,1,0:T(2,128)S(1)}, u32[]{:S(2)}, u32[]{:S(2)}) collective-permute-start(f32[125,2,128]{2,1,0:T(2,128)S(1)} %send_rows.1), channel_id=1, source_target_pairs={{0,128},{128,0},{1,129},{129,1},{2,130},{130,2},{3,131},{131,3},{4... | collective-permute-start | bytes 384008 | tf_op jit(solution)/shard_map/ppermute | solution.py:537
  5.6 1.7 %collective-permute-done.f_near = f32[125,32,128]{2,1,0:T(8,128)} collective-permute-done((f32[125,32,128]{2,1,0:T(8,128)}, f32[125,32,128]{2,1,0:T(8,128)}, u32[]{:S(2)}, u32[]{:S(2)}) %collective-permute-start) | collective-permute-done | bytes 2048032 | tf_op jit(solution)/shard_map/ppermute | solution.py:538
  7.3 7.2 %move_inside.1 = (f32[125,32,128]{2,1,0:T(8,128)S(1)}, f32[125,2,128]{2,1,0:T(2,128)S(1)}, f32[7,6,32,128]{3,2,1,0:T(8,128)S(1)}) custom-call(s32[1]{0:T(128)} %bitcast.place, f32[125,32,128]{2,1,0:T(8,128)} %f.3, f32[125,32,128]{2,1,0:T(8,128)} %collective-permute-done.f_near, f32[32,128]{1,0:T(8,128)} %rate.7), custom_call_target="tpu_custom_call" | custom-call | flops 50000000 | bytes 6000000 | tf_op jit(solution)/shard_map/move_inside/pallas_call | solution.py:539
  14.5 0.0 collective-permute-done.1.f_edge
  14.5 0.0 copy-done
  14.5 2.3 %enter_and_sum.1 = (f32[125,32,128]{2,1,0:T(8,128)S(1)}, f32[448,128]{1,0:T(8,128)S(1)}) custom-call(s32[1]{0:T(128)} %bitcast.place, f32[125,32,128]{2,1,0:T(8,128)S(1)} %get-tuple-element.18.kept_in, f32[7,6,32,128]{3,2,1,0:T(8,128)S(1)} %get-tuple-element.19.groups_in, ...), custom_call_target="tpu_custom_call", output_to_operand_aliasing={{0}: (1, {})} | custom-call | tf_op jit(solution)/shard_map/enter_and_sum/pallas_call | solution.py:560
  16.8 0.5 collective-permute-start.2
  17.3 9.1 %all_to_all.15 = f32[8,7,8,128]{3,2,1,0:T(8,128)S(1)} all-to-all(f32[8,7,8,128]{3,2,1,0:T(8,128)S(1)} %bitcast.7), channel_id=1, replica_groups=mesh['gx'=2,'gy'=2,'x'=4,'yl'=2,'z'=8] {'x','yl'}, dimensions={0} | all-to-all | bytes 458752 | tf_op jit(solution)/shard_map/all_to_all | solution.py:499
  26.4 0.7 %broadcast_in_dim.4 = f32[8,7,8,128]{3,2,1,0:T(8,128)} broadcast(f32[7,8,128]{2,1,0:T(8,128)S(1)} %reduce_sum.18), dimensions={1,2,3} | broadcast | bytes 258048 | tf_op jit(solution)/shard_map/broadcast_in_dim | solution.py:500
  27.1 8.2 %all-to-all-start.1 = ((f32[8,7,8,128]{3,2,1,0:T(8,128)}), f32[8,7,8,128]{3,2,1,0:T(8,128)S(1)}, u32[]{:S(2)}, u32[]{:S(2)}) async-start(f32[8,7,8,128]{3,2,1,0:T(8,128)} %broadcast_in_dim.4), calls=%async_computation.1 | async-start | bytes 458752 | tf_op jit(solution)/shard_map/all_to_all | solution.py:500
  35.3 2.6 %collective-permute-start.3 = (f32[125,2,128]{2,1,0:T(2,128)S(1)}, f32[125,2,128]{2,1,0:T(2,128)S(1)}, u32[]{:S(2)}, u32[]{:S(2)}) collective-permute-start(f32[125,2,128]{2,1,0:T(2,128)S(1)} %get-tuple-element.22), channel_id=1, source_target_pairs={{0,128},{128,0},{1,129},{129,1},{2,130},{130,2},{3,131},{131,3},{4... | collective-permute-start | bytes 384008 | tf_op jit(solution)/shard_map/ppermute | solution.py:559
  37.9 6.3 %all-to-all-done.1 = f32[8,7,8,128]{3,2,1,0:T(8,128)S(1)} async-done(((f32[8,7,8,128]{3,2,1,0:T(8,128)}), f32[8,7,8,128]{3,2,1,0:T(8,128)S(1)}, u32[]{:S(2)}, u32[]{:S(2)}) %all-to-all-start.1) | async-done | bytes 229408 | tf_op jit(solution)/shard_map/all_to_all | solution.py:500
  44.2 0.0 collective-permute-done.3.kept_edge
  44.3 9.6 %all_to_all.16 = f32[8,7,8,128]{3,2,1,0:T(8,128)S(1)} all-to-all(f32[8,7,8,128]{3,2,1,0:T(8,128)S(1)} %broadcast_in_dim.5), channel_id=1, replica_groups=mesh['gx'=2,'gy'=2,'x'=4,'yl'=2,'z'=8] {'x','yl'}, dimensions={0} | all-to-all | bytes 458752 | tf_op jit(solution)/shard_map/all_to_all | solution.py:502
  53.8 3.7 %collective-permute-start.4 = (f32[448,128]{1,0:T(8,128)S(1)}, f32[448,128]{1,0:T(8,128)S(1)}, u32[]{:S(2)}, u32[]{:S(2)}) collective-permute-start(f32[448,128]{1,0:T(8,128)S(1)} %bitcast.3), channel_id=1, source_target_pairs={{0,64},{64,0},{1,65},{65,1},{2,66},{66,2},{3,67},{67,3},{4,68},{68... | collective-permute-start | bytes 688136 | tf_op jit(solution)/shard_map/ppermute | solution.py:577
  57.6 2.6 %collective-permute-start.5 = (f32[64,128]{1,0:T(8,128)S(1)}, f32[64,128]{1,0:T(8,128)S(1)}, u32[]{:S(2)}, u32[]{:S(2)}) collective-permute-start(f32[64,128]{1,0:T(8,128)S(1)} %slice.8), channel_id=1, source_target_pairs={{0,128},{128,0},{1,129},{129,1},{2,130},{130,2},{3,131},{131,3},{4... | collective-permute-start | bytes 98312 | tf_op jit(solution)/shard_map/ppermute | solution.py:578
  60.2 0.6 tables_own.1
  60.8 0.0 collective-permute-done.4.total.total_near
  60.8 0.5 tables_near.1
  61.3 0.5 collective-permute-done.5.total_edge
  61.8 0.0 collective-permute-done.2.kept_near
  61.8 8.0 %collide_move_collide.1 = f32[125,32,128]{2,1,0:T(8,128)} custom-call(s32[1]{0:T(128)} %bitcast.place, f32[125,32,128]{2,1,0:T(8,128)S(1)} %get-tuple-element.20.kept, f32[125,32,128]{2,1,0:T(8,128)} %collective-permute-done.2.kept_near, f32[125,2,128]{2,1,0:T(2,128)S(1)} %collective-permute-done.3.kept_edge, f32[448,128]{1,0:T(8,128)S(1)} %bitcast.6, ...), custom_call_target="tpu_custom_call" | custom-call | tf_op jit(solution)/shard_map/collide_move_collide/pallas_call | solution.py:581
  (5 shorter events, 0.1 us)
Async XLA Ops:
  0.0 7.3 %collective-permute-start = (f32[125,32,128]{2,1,0:T(8,128)}, f32[125,32,128]{2,1,0:T(8,128)}, u32[]{:S(2)}, u32[]{:S(2)}) collective-permute-start(f32[125,32,128]{2,1,0:T(8,128)} %f.3), channel_id=1, source_target_pairs={{0,64},{64,0},{1,65},{65,1},{2,66},{66,2},{3,67},{67,3},{4,68},{68... | collective-permute-start | bytes 6144008 | tf_op jit(solution)/shard_map/ppermute | solution.py:538
  4.3 10.2 %copy-start = (f32[32,128]{1,0:T(8,128)S(1)}, f32[32,128]{1,0:T(8,128)}, u32[]{:S(2)}) copy-start(f32[32,128]{1,0:T(8,128)} %rate.7) | copy-start | bytes 49156
  4.3 10.2 %collective-permute-start.1 = (f32[125,2,128]{2,1,0:T(2,128)S(1)}, f32[125,2,128]{2,1,0:T(2,128)S(1)}, u32[]{:S(2)}, u32[]{:S(2)}) collective-permute-start(f32[125,2,128]{2,1,0:T(2,128)S(1)} %send_rows.1), channel_id=1, source_target_pairs={{0,128},{128,0},{1,129},{129,1},{2,130},{130,2},{3,131},{131,3},{4... | collective-permute-start | bytes 384008 | tf_op jit(solution)/shard_map/ppermute | solution.py:537
  16.8 45.0 %collective-permute-start.2 = (f32[125,32,128]{2,1,0:T(8,128)S(1)}, f32[125,32,128]{2,1,0:T(8,128)}, u32[]{:S(2)}, u32[]{:S(2)}) collective-permute-start(f32[125,32,128]{2,1,0:T(8,128)S(1)} %get-tuple-element.20.kept), channel_id=1, source_target_pairs={{0,64},{64,0},{1,65},{65,1},{2,66},{66,2},{3,67},{67,3},{4,68},{68... | collective-permute-start | bytes 6144008 | tf_op jit(solution)/shard_map/ppermute | solution.py:575
  27.1 17.1 %all-to-all-start.1 = ((f32[8,7,8,128]{3,2,1,0:T(8,128)}), f32[8,7,8,128]{3,2,1,0:T(8,128)S(1)}, u32[]{:S(2)}, u32[]{:S(2)}) async-start(f32[8,7,8,128]{3,2,1,0:T(8,128)} %broadcast_in_dim.4), calls=%async_computation.1 | async-start | bytes 458752 | tf_op jit(solution)/shard_map/all_to_all | solution.py:500
  35.3 8.9 %collective-permute-start.3 = (f32[125,2,128]{2,1,0:T(2,128)S(1)}, f32[125,2,128]{2,1,0:T(2,128)S(1)}, u32[]{:S(2)}, u32[]{:S(2)}) collective-permute-start(f32[125,2,128]{2,1,0:T(2,128)S(1)} %get-tuple-element.22), channel_id=1, source_target_pairs={{0,128},{128,0},{1,129},{129,1},{2,130},{130,2},{3,131},{131,3},{4... | collective-permute-start | bytes 384008 | tf_op jit(solution)/shard_map/ppermute | solution.py:559
  53.8 7.0 %collective-permute-start.4 = (f32[448,128]{1,0:T(8,128)S(1)}, f32[448,128]{1,0:T(8,128)S(1)}, u32[]{:S(2)}, u32[]{:S(2)}) collective-permute-start(f32[448,128]{1,0:T(8,128)S(1)} %bitcast.3), channel_id=1, source_target_pairs={{0,64},{64,0},{1,65},{65,1},{2,66},{66,2},{3,67},{67,3},{4,68},{68... | collective-permute-start | bytes 688136 | tf_op jit(solution)/shard_map/ppermute | solution.py:577
  57.6 4.3 %collective-permute-start.5 = (f32[64,128]{1,0:T(8,128)S(1)}, f32[64,128]{1,0:T(8,128)S(1)}, u32[]{:S(2)}, u32[]{:S(2)}) collective-permute-start(f32[64,128]{1,0:T(8,128)S(1)} %slice.8), channel_id=1, source_target_pairs={{0,128},{128,0},{1,129},{129,1},{2,130},{130,2},{3,131},{131,3},{4... | collective-permute-start | bytes 98312 | tf_op jit(solution)/shard_map/ppermute | solution.py:578

commit v4 on v3

--- a/solution.py
+++ b/solution.py
@@ -57,10 +57,22 @@
     return group, index_x, whole - index_x * VG, slot - group * VG
 
 
+def y_sides(positive):
+    lane = lane_index()
+    if positive is True:
+        return 2, 4, lane >= LANES - 2, lane >= LANES - 4
+    if positive is False:
+        return LANES - 2, LANES - 4, lane < 2, lane < 4
+    one = ((lane + jnp.where(positive, 2, 0)) & (LANES - 1)) < 2
+    two = ((lane + jnp.where(positive, 4, 0)) & (LANES - 1)) < 4
+    return jnp.where(positive, 2, LANES - 2), jnp.where(positive, 4, LANES - 4), one, two
+
+
 def y_part(center, near, sides):
-    shift, one, two = sides
-    far = pltpu.roll(jnp.where(two, near, center), shift, 1)
-    return pltpu.roll(jnp.where(one, near, center) - 0.25 * far, shift, 1)
+    shift_one, shift_two, one, two = sides
+    return pltpu.roll(jnp.where(one, near, center), shift_one, 1) - 0.25 * pltpu.roll(
+        jnp.where(two, near, center), shift_two, 1
+    )
 
 
 def upwind(center, back, x_one, x_two, even, coef_x, coef_y, coef_z):
@@ -70,13 +82,6 @@
         + (2.0 * coef_y) * back
         + (2.0 * coef_z) * other_plane(center, even)
     )
-
-
-def static_sides(positive):
-    lane = lane_index()
-    if positive:
-        return 2, lane >= LANES - 2, lane >= LANES - 4
-    return LANES - 2, lane < 2, lane < 4
 
 
 def each_sign(positive, run):
@@ -131,33 +136,31 @@
             coef_y = DT * jnp.abs(speed_of(index_y))
             side = jnp.where(index_z >= VG // 2, 1.0, -1.0)
 
-            def run(rising):
-                sides = static_sides(rising)
-                acc = [None] * 4
-                for t in range(CHUNK):
-                    v = c * CHUNK + t
-                    center = held[v]
-                    x_one, x_two = x_steps(
-                        buf, t, center, jnp.zeros((2, LANES), jnp.float32), forward
-                    )
-                    speed_z = speed_of(index_z + t)
-                    back = y_part(center, held_near[v], sides)
-                    moved = upwind(
-                        center, back, x_one, x_two, even, coef_x, coef_y, DT * speed_z * side
-                    )
-                    left = keep * moved
-                    kept[v] = left
-                    kept_edge[v] = left[30:32] if forward else left[0:2]
-                    power = moved
-                    for k in range(4):
-                        acc[k] = power if acc[k] is None else acc[k] + power
-                        if k < 3:
-                            power = power * speed_z
-                for k in range(3):
-                    groups[group, k] += acc[k]
-                    groups[group, 3 + k] += side * acc[k + 1]
-
-            each_sign(index_y >= VG // 2, run)
+            sides = y_sides(index_y >= VG // 2)
+            acc = [None] * 4
+            for t in range(CHUNK):
+                v = c * CHUNK + t
+                center = held[v]
+                x_one, x_two = x_steps(
+                    buf, t, center, jnp.zeros((2, LANES), jnp.float32), forward
+                )
+                speed_z = speed_of(index_z + t)
+                back = y_part(center, held_near[v], sides)
+                moved = upwind(
+                    center, back, x_one, x_two, even, coef_x, coef_y, DT * speed_z * side
+                )
+                left = keep * moved
+                kept[v] = left
+                kept_edge[v] = left[30:32] if forward else left[0:2]
+                power = moved
+                for k in range(4):
+                    acc[k] = power if acc[k] is None else acc[k] + power
+                    if k < 3:
+                        power = power * speed_z
+            for k in range(3):
+                groups[group, k] += acc[k]
+                groups[group, 3 + k] += side * acc[k + 1]
+
             return carry
 
         def piece(p, carry):
@@ -235,37 +238,35 @@
                     squares * parts[0] + parts[2],
                 )
 
-            def run(rising):
-                sides = static_sides(rising)
-                level = [WEIGHT * groups[group, k] for k in range(6)]
-                for m, value in enumerate(five(level)):
-                    sums[ROWS * m : ROWS * (m + 1)] += value
-                second, near_y, near_x = [], [], []
-                for k in range(3):
-                    center = keep * level[k]
-                    absolute = keep * level[3 + k]
-                    x_one, x_two = x_steps(
-                        buf, k, center, jnp.zeros((2, LANES), jnp.float32), forward
-                    )
-                    second.append(
-                        center * (1.0 - 1.5 * (coef_x + coef_y))
-                        - (2.0 * DT) * (absolute - other_plane(absolute, even))
-                        + (2.0 * coef_x) * (x_one - 0.25 * x_two)
-                        + (2.0 * coef_y) * y_part(center, 0.0, sides)
-                    )
-                    near_y.append(coef_y * jnp.where(sides[2], center, 0.0))
-                    near_x.append(coef_x * (center[30:32] if forward else center[0:2]))
-                for m, value in enumerate(five(second)):
-                    sums[ROW_SECOND + ROWS * m : ROW_SECOND + ROWS * (m + 1)] += value
-                for m, value in enumerate(five(near_x)):
-                    at = ROW_SPILL_X + 4 * m + (0 if forward else 2)
-                    sums[at : at + 2] += value
-                packed = sums[ROW_SPILL_Y : ROW_SPILL_Y + ROWS]
-                for m, value in enumerate(five(near_y)):
-                    packed = packed + (pltpu.roll(value, 8 * m, 1) if m else value)
-                sums[ROW_SPILL_Y : ROW_SPILL_Y + ROWS] = packed
-
-            each_sign(index_y >= VG // 2, run)
+            sides = y_sides(index_y >= VG // 2)
+            level = [WEIGHT * groups[group, k] for k in range(6)]
+            for m, value in enumerate(five(level)):
+                sums[ROWS * m : ROWS * (m + 1)] += value
+            second, near_y, near_x = [], [], []
+            for k in range(3):
+                center = keep * level[k]
+                absolute = keep * level[3 + k]
+                x_one, x_two = x_steps(
+                    buf, k, center, jnp.zeros((2, LANES), jnp.float32), forward
+                )
+                second.append(
+                    center * (1.0 - 1.5 * (coef_x + coef_y))
+                    - (2.0 * DT) * (absolute - other_plane(absolute, even))
+                    + (2.0 * coef_x) * (x_one - 0.25 * x_two)
+                    + (2.0 * coef_y) * y_part(center, 0.0, sides)
+                )
+                near_y.append(coef_y * jnp.where(sides[3], center, 0.0))
+                near_x.append(coef_x * (center[30:32] if forward else center[0:2]))
+            for m, value in enumerate(five(second)):
+                sums[ROW_SECOND + ROWS * m : ROW_SECOND + ROWS * (m + 1)] += value
+            for m, value in enumerate(five(near_x)):
+                at = ROW_SPILL_X + 4 * m + (0 if forward else 2)
+                sums[at : at + 2] += value
+            packed = sums[ROW_SPILL_Y : ROW_SPILL_Y + ROWS]
+            for m, value in enumerate(five(near_y)):
+                packed = packed + (pltpu.roll(value, 8 * m, 1) if m else value)
+            sums[ROW_SPILL_Y : ROW_SPILL_Y + ROWS] = packed
+
             return carry
 
         lax.fori_loop(0, GROUPS, one, 0)
@@ -369,9 +370,43 @@
     lax.fori_loop(0, ROWS // 8, block, 0)
 
 
+def second_inside_kernel(
+    place, kept, kept_near, rate, base, tables, base_near, tables_near, moved_part, buf
+):
+    device = place[0]
+    first = device * VEL_LOCAL
+    even = lax.rem(lane_index(), 2) == 0
+
+    def move(forward):
+        def chunk(c, carry):
+            group, index_x, index_y, index_z = chunk_place(first, c)
+            coef_x = DT * jnp.abs(speed_of(index_x))
+            coef_y = DT * jnp.abs(speed_of(index_y))
+            side = jnp.where(index_z >= VG // 2, 1.0, -1.0)
+            sides = y_sides(index_y >= VG // 2)
+            front = base[...] * tables[0, index_x] * tables[1, index_y]
+            front_near = base_near[...] * tables_near[0, index_x] * tables_near[1, index_y]
+            for t in range(CHUNK):
+                v = c * CHUNK + t
+                n = index_z + t
+                center = kept[v] + front * tables[2, n]
+                near = kept_near[v] + front_near * tables_near[2, n]
+                x_one, x_two = x_steps(
+                    buf, t, center, jnp.zeros((2, LANES), jnp.float32), forward
+                )
+                moved_part[v] = upwind(
+                    center, y_part(center, near, sides), x_one, x_two, even, coef_x, coef_y,
+                    DT * speed_of(n) * side,
+                )
+            return carry
+
+        lax.fori_loop(0, CHUNKS, chunk, 0)
+
+    each_sign(device >= 32, move)
+
+
 def second_kernel(
-    place, kept, kept_near, kept_edge, total, total_near, total_edge, rate,
-    base, tables, kinds, base_near, tables_near, kinds_near,
+    place, moved_part, kept_edge, total, total_near, total_edge, rate, kinds, kinds_near,
     out, base_edge, tables_edge, kinds_edge, table_two, done, buf, sem,
 ):
     device = place[0]
@@ -408,8 +443,8 @@
                 other_plane(kinds[4, m], even)
                 + (x_one - 0.25 * x_two)
                 + (x_low - 0.25 * x_lower)
-                + y_part(kinds[2, m], kinds_near[2, m] + spill, static_sides(True))
-                + y_part(kinds[3, m], kinds_near[3, m] + spill, static_sides(False))
+                + y_part(kinds[2, m], kinds_near[2, m] + spill, y_sides(True))
+                + y_part(kinds[3, m], kinds_near[3, m] + spill, y_sides(False))
             )
         )
     amp, flow_x, flow_y, flow_z, inv = parameters(moments)
@@ -424,39 +459,27 @@
 
     def move(forward):
         row = 0 if forward else 2
+        rows = slice(0, 2) if forward else slice(30, 32)
+        none = jnp.zeros((1, LANES), jnp.float32)
 
         def chunk(c, carry):
             group, index_x, index_y, index_z = chunk_place(first, c)
             speed_x = speed_of(index_x)
-            speed_y = speed_of(index_y)
-            coef_x = DT * jnp.abs(speed_x)
-            coef_y = DT * jnp.abs(speed_y)
-            side = jnp.where(index_z >= VG // 2, 1.0, -1.0)
-
-            def run(rising):
-                sides = static_sides(rising)
-                front = base[...] * tables[0, index_x] * tables[1, index_y]
-                front_near = base_near[...] * tables_near[0, index_x] * tables_near[1, index_y]
-                front_edge = base_edge[...] * tables_edge[0, index_x] * tables_edge[1, index_y]
-                gap_x = speed_x - table_two[VG + 1]
-                gap_y = speed_y - table_two[VG + 2]
-                front_two = table_two[VG] * jnp.exp(
-                    -(table_two[VG + 3] * (gap_x * gap_x + gap_y * gap_y))
-                )
-                for t in range(CHUNK):
-                    v = c * CHUNK + t
-                    n = index_z + t
-                    center = kept[v] + front * tables[2, n]
-                    near = kept_near[v] + front_near * tables_near[2, n]
-                    halo = kept_edge[v] + (front_edge * tables_edge[2, n])[row : row + 2]
-                    x_one, x_two = x_steps(buf, t, center, halo, forward)
-                    moved = upwind(
-                        center, y_part(center, near, sides), x_one, x_two, even, coef_x, coef_y,
-                        DT * speed_of(n) * side,
-                    )
-                    done[v] = keep * moved + front_two * table_two[n]
-
-            each_sign(index_y >= VG // 2, run)
+            coef = (2.0 * DT) * jnp.abs(speed_x)
+            gap_x = speed_x - table_two[VG + 1]
+            gap_y = speed_of(index_y) - table_two[VG + 2]
+            front_two = table_two[VG] * jnp.exp(
+                -(table_two[VG + 3] * (gap_x * gap_x + gap_y * gap_y))
+            )
+            front_edge = base_edge[...] * tables_edge[0, index_x] * tables_edge[1, index_y]
+            for t in range(CHUNK):
+                v = c * CHUNK + t
+                n = index_z + t
+                halo = kept_edge[v] + (front_edge * tables_edge[2, n])[row : row + 2]
+                one = [halo[1:2], none] if forward else [none, halo[0:1]]
+                entered = coef * (jnp.concatenate(one, axis=0) - 0.25 * halo)
+                done[v] = keep * moved_part[v] + front_two * table_two[n]
+                done[v, rows] += keep[rows] * entered
             return carry
 
         def piece(p, carry):
@@ -578,10 +601,20 @@
     total_edge = lax.ppermute(total[ROW_SPILL_X : ROW_EDGE + ROWS], "gx", SWAP)
     own = tables_of(total, collision_rate, "xyz", "tables_own")
     near = tables_of(total_near, total_near[ROW_RATE : ROW_RATE + ROWS], "y", "tables_near")
+    moved_part = pl.pallas_call(
+        second_inside_kernel,
+        out_shape=f32(VEL_LOCAL, ROWS, LANES),
+        in_specs=[smem()] + [vmem()] * 7,
+        out_specs=vmem(),
+        scratch_shapes=[pltpu.VMEM((CHUNK, 48, LANES), jnp.float32)],
+        compiler_params=pltpu.CompilerParams(vmem_limit_bytes=16 * 2**20),
+        cost_estimate=pl.CostEstimate(flops=50000000, bytes_accessed=6000000, transcendentals=0),
+        name="move_inside_two",
+    )(place, kept, kept_near, collision_rate, *own[:2], *near[:2])
     return pl.pallas_call(
         second_kernel,
         out_shape=f32(VEL_LOCAL, ROWS, LANES),
-        in_specs=[smem()] + [vmem()] * 13,
+        in_specs=[smem()] + [vmem()] * 8,
         out_specs=anywhere(),
         scratch_shapes=[
             pltpu.VMEM((8, LANES), jnp.float32),
@@ -593,10 +626,10 @@
             pltpu.SemaphoreType.DMA((STEPS,)),
         ],
         compiler_params=pltpu.CompilerParams(vmem_limit_bytes=24 * 2**20),
-        name="collide_move_collide",
+        name="collide_two",
     )(
-        place, kept, kept_near, kept_edge, total, total_near, total_edge, collision_rate, *own,
-        *near,
+        place, moved_part, kept_edge, total, total_near, total_edge, collision_rate, own[2],
+        near[2],
     )
 
 

time: 70.2 us -> 68.9 us (0.981)
  Pallas kernels: 19.7 us -> 18.9 us
    pallas_call x0 -> x1, Pallas kernels: none -> 5.94 us  [body(): pl.pallas_call(second_inside_kernel, out_shape=f32(VEL_LOCAL, ROWS, LANES...]
    pallas_call x1, Pallas kernels: 8.02 us -> 2.4 us  [body(): pl.pallas_call(second_kernel, out_shape=f32(VEL_LOCAL, ROWS, LANES), in_s...]
    pallas_call x1, Pallas kernels: 7.19 us -> 6.37 us  [body(): pl.pallas_call(inside_kernel, out_shape=(f32(VEL_LOCAL, ROWS, LANES), f32...]
  transfers between devices with their start and end apart: 7 -> 7, of which waited for: 3 -> 2; matrix products, arithmetic and copies ran while one was open for 1% -> 1% of each run, Pallas kernels for 13% -> 21%
where the time goes in v4:
time: 68.9 us; the launch traced here: 68.5 us
  starting transfers between devices  22.1 us (32%)
  Pallas kernels  18.9 us (27%)
  blocking collectives  18.6 us (27%)
  waiting for transfers between devices  7.96 us (12%)
  local copies, waits for them, and re-layouts  0.73 us (1%)
    all_to_all x1, blocking collectives, sum_over_vert(): lax.all_to_all(jnp.broadcast_to(share[None], parts.shape), PLANE, 0, 0)  9.56 us
    all_to_all x1, blocking collectives, sum_over_vert(): share = jnp.sum(lax.all_to_all(parts, PLANE, 0, 0), axis=0)  9.05 us
    all_to_all x1, starting transfers between devices, sum_over_vert(): lax.all_to_all(jnp.broadcast_to(share[None], parts.shape), 'z', 0, 0)  8.19 us
    pallas_call x1, Pallas kernels, body(): pl.pallas_call(inside_kernel, out_shape=(f32(VEL_LOCAL, ROWS, LANES), f32...  6.37 us
    all_to_all x1, waiting for transfers between devices, sum_over_vert(): lax.all_to_all(jnp.broadcast_to(share[None], parts.shape), 'z', 0, 0)  6.26 us
    pallas_call x1, Pallas kernels, body(): pl.pallas_call(second_inside_kernel, out_shape=f32(VEL_LOCAL, ROWS, LANES...  5.94 us
    ppermute x1, starting transfers between devices, body(): total_near = lax.ppermute(total, 'gy', SWAP)  3.73 us
    ppermute x1, starting transfers between devices, body(): f_near = lax.ppermute(distribution, 'gy', SWAP)  3.24 us
  transfers between devices with their start and end apart: 7, of which 2 were waited for; matrix products, arithmetic and copies ran while one was open for 1% of the time, Pallas kernels for 21%

profile of v4, /device:TPU:1, one launch (start us, length us, event | category | flops | bytes accessed | tf_op | source)
XLA Modules:
  0.0 68.5 jit_solution(17349187516723775783)
XLA Ops:
  0.0 3.2 %collective-permute-start = (f32[125,32,128]{2,1,0:T(8,128)}, f32[125,32,128]{2,1,0:T(8,128)}, u32[]{:S(2)}, u32[]{:S(2)}) collective-permute-start(f32[125,32,128]{2,1,0:T(8,128)} %f.3), channel_id=1, source_target_pairs={{0,64},{64,0},{1,65},{65,1},{2,66},{66,2},{3,67},{67,3},{4,68},{68... | collective-permute-start | bytes 6144008 | tf_op jit(solution)/shard_map/ppermute | solution.py:561
  3.2 1.1 %send_rows.1 = f32[125,2,128]{2,1,0:T(2,128)S(1)} custom-call(s32[1]{0:T(128)} %bitcast.place, f32[125,32,128]{2,1,0:T(8,128)} %f.3), custom_call_target="tpu_custom_call" | custom-call | bytes 600000 | tf_op jit(solution)/shard_map/send_rows/pallas_call | solution.py:550
  4.3 0.0 copy-start
  4.3 1.3 %collective-permute-start.1 = (f32[125,2,128]{2,1,0:T(2,128)S(1)}, f32[125,2,128]{2,1,0:T(2,128)S(1)}, u32[]{:S(2)}, u32[]{:S(2)}) collective-permute-start(f32[125,2,128]{2,1,0:T(2,128)S(1)} %send_rows.1), channel_id=1, source_target_pairs={{0,128},{128,0},{1,129},{129,1},{2,130},{130,2},{3,131},{131,3},{4... | collective-permute-start | bytes 384008 | tf_op jit(solution)/shard_map/ppermute | solution.py:560
  5.6 1.7 %collective-permute-done.f_near = f32[125,32,128]{2,1,0:T(8,128)} collective-permute-done((f32[125,32,128]{2,1,0:T(8,128)}, f32[125,32,128]{2,1,0:T(8,128)}, u32[]{:S(2)}, u32[]{:S(2)}) %collective-permute-start) | collective-permute-done | bytes 2048032 | tf_op jit(solution)/shard_map/ppermute | solution.py:561
  7.3 6.4 %move_inside.1 = (f32[125,32,128]{2,1,0:T(8,128)S(1)}, f32[125,2,128]{2,1,0:T(2,128)S(1)}, f32[7,6,32,128]{3,2,1,0:T(8,128)S(1)}) custom-call(s32[1]{0:T(128)} %bitcast.place, f32[125,32,128]{2,1,0:T(8,128)} %f.3, f32[125,32,128]{2,1,0:T(8,128)} %collective-permute-done.f_near, f32[32,128]{1,0:T(8,128)} %rate.9), custom_call_target="tpu_custom_call" | custom-call | flops 50000000 | bytes 6000000 | tf_op jit(solution)/shard_map/move_inside/pallas_call | solution.py:562
  13.7 0.0 collective-permute-done.1.f_edge
  13.7 0.0 copy-done
  13.7 2.1 %enter_and_sum.1 = (f32[125,32,128]{2,1,0:T(8,128)S(1)}, f32[448,128]{1,0:T(8,128)S(1)}) custom-call(s32[1]{0:T(128)} %bitcast.place, f32[125,32,128]{2,1,0:T(8,128)S(1)} %get-tuple-element.18.kept_in, f32[7,6,32,128]{3,2,1,0:T(8,128)S(1)} %get-tuple-element.19.groups_in, ...), custom_call_target="tpu_custom_call", output_to_operand_aliasing={{0}: (1, {})} | custom-call | tf_op jit(solution)/shard_map/enter_and_sum/pallas_call | solution.py:583
  15.8 0.5 collective-permute-start.2
  16.3 9.0 %all_to_all.15 = f32[8,7,8,128]{3,2,1,0:T(8,128)S(1)} all-to-all(f32[8,7,8,128]{3,2,1,0:T(8,128)S(1)} %bitcast.7), channel_id=1, replica_groups=mesh['gx'=2,'gy'=2,'x'=4,'yl'=2,'z'=8] {'x','yl'}, dimensions={0} | all-to-all | bytes 458752 | tf_op jit(solution)/shard_map/all_to_all | solution.py:522
  25.3 0.7 %broadcast_in_dim.4 = f32[8,7,8,128]{3,2,1,0:T(8,128)} broadcast(f32[7,8,128]{2,1,0:T(8,128)S(1)} %reduce_sum.18), dimensions={1,2,3} | broadcast | bytes 258048 | tf_op jit(solution)/shard_map/broadcast_in_dim | solution.py:523
  26.0 8.2 %all-to-all-start.1 = ((f32[8,7,8,128]{3,2,1,0:T(8,128)}), f32[8,7,8,128]{3,2,1,0:T(8,128)S(1)}, u32[]{:S(2)}, u32[]{:S(2)}) async-start(f32[8,7,8,128]{3,2,1,0:T(8,128)} %broadcast_in_dim.4), calls=%async_computation.1 | async-start | bytes 458752 | tf_op jit(solution)/shard_map/all_to_all | solution.py:523
  34.2 2.6 %collective-permute-start.3 = (f32[125,2,128]{2,1,0:T(2,128)S(1)}, f32[125,2,128]{2,1,0:T(2,128)S(1)}, u32[]{:S(2)}, u32[]{:S(2)}) collective-permute-start(f32[125,2,128]{2,1,0:T(2,128)S(1)} %get-tuple-element.22), channel_id=1, source_target_pairs={{0,128},{128,0},{1,129},{129,1},{2,130},{130,2},{3,131},{131,3},{4... | collective-permute-start | bytes 384008 | tf_op jit(solution)/shard_map/ppermute | solution.py:582
  36.8 6.3 %all-to-all-done.1 = f32[8,7,8,128]{3,2,1,0:T(8,128)S(1)} async-done(((f32[8,7,8,128]{3,2,1,0:T(8,128)}), f32[8,7,8,128]{3,2,1,0:T(8,128)S(1)}, u32[]{:S(2)}, u32[]{:S(2)}) %all-to-all-start.1) | async-done | bytes 229408 | tf_op jit(solution)/shard_map/all_to_all | solution.py:523
  43.1 0.0 collective-permute-done.3.kept_edge
  43.1 9.6 %all_to_all.16 = f32[8,7,8,128]{3,2,1,0:T(8,128)S(1)} all-to-all(f32[8,7,8,128]{3,2,1,0:T(8,128)S(1)} %broadcast_in_dim.5), channel_id=1, replica_groups=mesh['gx'=2,'gy'=2,'x'=4,'yl'=2,'z'=8] {'x','yl'}, dimensions={0} | all-to-all | bytes 458752 | tf_op jit(solution)/shard_map/all_to_all | solution.py:525
  52.7 3.7 %collective-permute-start.4 = (f32[448,128]{1,0:T(8,128)S(1)}, f32[448,128]{1,0:T(8,128)S(1)}, u32[]{:S(2)}, u32[]{:S(2)}) collective-permute-start(f32[448,128]{1,0:T(8,128)S(1)} %bitcast.3), channel_id=1, source_target_pairs={{0,64},{64,0},{1,65},{65,1},{2,66},{66,2},{3,67},{67,3},{4,68},{68... | collective-permute-start | bytes 688136 | tf_op jit(solution)/shard_map/ppermute | solution.py:600
  56.5 2.6 %collective-permute-start.5 = (f32[64,128]{1,0:T(8,128)S(1)}, f32[64,128]{1,0:T(8,128)S(1)}, u32[]{:S(2)}, u32[]{:S(2)}) collective-permute-start(f32[64,128]{1,0:T(8,128)S(1)} %slice.9), channel_id=1, source_target_pairs={{0,128},{128,0},{1,129},{129,1},{2,130},{130,2},{3,131},{131,3},{4... | collective-permute-start | bytes 98312 | tf_op jit(solution)/shard_map/ppermute | solution.py:601
  59.1 0.6 tables_own.1
  59.7 0.0 collective-permute-done.4.total.total_near
  59.7 0.5 tables_near.1
  60.2 0.0 collective-permute-done.2.kept_near
  60.2 5.9 %move_inside_two.1.moved_part = f32[125,32,128]{2,1,0:T(8,128)S(1)} custom-call(s32[1]{0:T(128)} %bitcast.place, f32[125,32,128]{2,1,0:T(8,128)S(1)} %get-tuple-element.20.kept, f32[125,32,128]{2,1,0:T(8,128)} %collective-permute-done.2.kept_near, f32[32,128]{1,0:T(8,128)S(1)} %copy-done, f32[32,128]{1,0:T(8,128)S(1)} %get-tuple-element.24.base, ...), custom_call_target="tpu_custom_call" | custom-call | flops 50000000 | bytes 6000000 | tf_op jit(solution)/shard_map/move_inside_two/pallas_call | solution.py:604
  66.1 0.0 collective-permute-done.5.total_edge
  66.1 2.4 %collide_two.1 = f32[125,32,128]{2,1,0:T(8,128)} custom-call(s32[1]{0:T(128)} %bitcast.place, f32[125,32,128]{2,1,0:T(8,128)S(1)} %move_inside_two.1.moved_part, f32[125,2,128]{2,1,0:T(2,128)S(1)} %collective-permute-done.3.kept_edge, f32[448,128]{1,0:T(8,128)S(1)} %bitcast.6, f32[448,128]{1,0:T(8,128)S(1)} %collective-permute-done.4.total.total_near, ...), custom_call_target="tpu_custom_call" | custom-call | tf_op jit(solution)/shard_map/collide_two/pallas_call | solution.py:614
  (5 shorter events, 0.1 us)
Async XLA Ops:
  0.0 7.3 %collective-permute-start = (f32[125,32,128]{2,1,0:T(8,128)}, f32[125,32,128]{2,1,0:T(8,128)}, u32[]{:S(2)}, u32[]{:S(2)}) collective-permute-start(f32[125,32,128]{2,1,0:T(8,128)} %f.3), channel_id=1, source_target_pairs={{0,64},{64,0},{1,65},{65,1},{2,66},{66,2},{3,67},{67,3},{4,68},{68... | collective-permute-start | bytes 6144008 | tf_op jit(solution)/shard_map/ppermute | solution.py:561
  4.3 9.3 %copy-start = (f32[32,128]{1,0:T(8,128)S(1)}, f32[32,128]{1,0:T(8,128)}, u32[]{:S(2)}) copy-start(f32[32,128]{1,0:T(8,128)} %rate.9) | copy-start | bytes 49156
  4.3 9.3 %collective-permute-start.1 = (f32[125,2,128]{2,1,0:T(2,128)S(1)}, f32[125,2,128]{2,1,0:T(2,128)S(1)}, u32[]{:S(2)}, u32[]{:S(2)}) collective-permute-start(f32[125,2,128]{2,1,0:T(2,128)S(1)} %send_rows.1), channel_id=1, source_target_pairs={{0,128},{128,0},{1,129},{129,1},{2,130},{130,2},{3,131},{131,3},{4... | collective-permute-start | bytes 384008 | tf_op jit(solution)/shard_map/ppermute | solution.py:560
  15.8 44.4 %collective-permute-start.2 = (f32[125,32,128]{2,1,0:T(8,128)S(1)}, f32[125,32,128]{2,1,0:T(8,128)}, u32[]{:S(2)}, u32[]{:S(2)}) collective-permute-start(f32[125,32,128]{2,1,0:T(8,128)S(1)} %get-tuple-element.20.kept), channel_id=1, source_target_pairs={{0,64},{64,0},{1,65},{65,1},{2,66},{66,2},{3,67},{67,3},{4,68},{68... | collective-permute-start | bytes 6144008 | tf_op jit(solution)/shard_map/ppermute | solution.py:598
  26.0 17.1 %all-to-all-start.1 = ((f32[8,7,8,128]{3,2,1,0:T(8,128)}), f32[8,7,8,128]{3,2,1,0:T(8,128)S(1)}, u32[]{:S(2)}, u32[]{:S(2)}) async-start(f32[8,7,8,128]{3,2,1,0:T(8,128)} %broadcast_in_dim.4), calls=%async_computation.1 | async-start | bytes 458752 | tf_op jit(solution)/shard_map/all_to_all | solution.py:523
  34.2 8.9 %collective-permute-start.3 = (f32[125,2,128]{2,1,0:T(2,128)S(1)}, f32[125,2,128]{2,1,0:T(2,128)S(1)}, u32[]{:S(2)}, u32[]{:S(2)}) collective-permute-start(f32[125,2,128]{2,1,0:T(2,128)S(1)} %get-tuple-element.22), channel_id=1, source_target_pairs={{0,128},{128,0},{1,129},{129,1},{2,130},{130,2},{3,131},{131,3},{4... | collective-permute-start | bytes 384008 | tf_op jit(solution)/shard_map/ppermute | solution.py:582
  52.7 7.0 %collective-permute-start.4 = (f32[448,128]{1,0:T(8,128)S(1)}, f32[448,128]{1,0:T(8,128)S(1)}, u32[]{:S(2)}, u32[]{:S(2)}) collective-permute-start(f32[448,128]{1,0:T(8,128)S(1)} %bitcast.3), channel_id=1, source_target_pairs={{0,64},{64,0},{1,65},{65,1},{2,66},{66,2},{3,67},{67,3},{4,68},{68... | collective-permute-start | bytes 688136 | tf_op jit(solution)/shard_map/ppermute | solution.py:600
  56.5 9.7 %collective-permute-start.5 = (f32[64,128]{1,0:T(8,128)S(1)}, f32[64,128]{1,0:T(8,128)S(1)}, u32[]{:S(2)}, u32[]{:S(2)}) collective-permute-start(f32[64,128]{1,0:T(8,128)S(1)} %slice.9), channel_id=1, source_target_pairs={{0,128},{128,0},{1,129},{129,1},{2,130},{130,2},{3,131},{131,3},{4... | collective-permute-start | bytes 98312 | tf_op jit(solution)/shard_map/ppermute | solution.py:601

commit v5 on v4

--- a/solution.py
+++ b/solution.py
@@ -103,6 +103,13 @@
     return pltpu.make_async_copy(f.at[rows], held.at[rows], sem.at[piece])
 
 
+def x_inside(center, forward):
+    row = lax.broadcasted_iota(jnp.int32, (ROWS, LANES), 0)
+    if forward:
+        return [jnp.where(row >= n, pltpu.roll(center, n, 0), 0.0) for n in (1, 2)]
+    return [jnp.where(row < ROWS - n, pltpu.roll(center, ROWS - n, 0), 0.0) for n in (1, 2)]
+
+
 def send_kernel(place, f, out, band, sem):
     def take(forward):
         copy = pltpu.make_async_copy(f.at[:, pl.ds(24 if forward else 0, 8)], band, sem)
@@ -114,7 +121,7 @@
 
 
 def inside_kernel(
-    place, f, f_near, rate, kept, kept_edge, groups, held, held_near, held_rate, buf, sem, sem_near,
+    place, f, f_near, rate, kept, kept_edge, groups, held, held_near, held_rate, sem, sem_near,
     sem_rate,
 ):
     rate_copy = pltpu.make_async_copy(rate, held_rate, sem_rate)
@@ -138,25 +145,26 @@
 
             sides = y_sides(index_y >= VG // 2)
             acc = [None] * 4
-            for t in range(CHUNK):
-                v = c * CHUNK + t
-                center = held[v]
-                x_one, x_two = x_steps(
-                    buf, t, center, jnp.zeros((2, LANES), jnp.float32), forward
-                )
-                speed_z = speed_of(index_z + t)
-                back = y_part(center, held_near[v], sides)
-                moved = upwind(
-                    center, back, x_one, x_two, even, coef_x, coef_y, DT * speed_z * side
-                )
-                left = keep * moved
-                kept[v] = left
-                kept_edge[v] = left[30:32] if forward else left[0:2]
-                power = moved
+            at = [c * CHUNK + t for t in range(CHUNK)]
+            speeds = [speed_of(index_z + t) for t in range(CHUNK)]
+            centers = [held[v] for v in at]
+            nears = [held_near[v] for v in at]
+            backs = [y_part(center, near, sides) for center, near in zip(centers, nears)]
+            moved = [
+                upwind(center, back, *x_inside(center, forward), even, coef_x, coef_y,
+                       DT * speed * side)
+                for center, back, speed in zip(centers, backs, speeds)
+            ]
+            for value, speed in zip(moved, speeds):
+                power = value
                 for k in range(4):
                     acc[k] = power if acc[k] is None else acc[k] + power
                     if k < 3:
-                        power = power * speed_z
+                        power = power * speed
+            for v, value in zip(at, moved):
+                left = keep * value
+                kept[v] = left
+                kept_edge[v] = left[30:32] if forward else left[0:2]
             for k in range(3):
                 groups[group, k] += acc[k]
                 groups[group, 3 + k] += side * acc[k + 1]
@@ -166,7 +174,9 @@
         def piece(p, carry):
             load_piece(f, held, sem, p).wait()
             load_piece(f_near, held_near, sem_near, p).wait()
-            return lax.fori_loop(p * STEP_CHUNKS, (p + 1) * STEP_CHUNKS, chunk, carry)
+            for c in range(STEP_CHUNKS):
+                chunk(p * STEP_CHUNKS + c, carry)
+            return carry
 
         lax.fori_loop(0, STEPS, piece, 0)
 
@@ -213,7 +223,12 @@
                 groups[group, 3 + k, rows] += side * acc[k + 1]
             return carry
 
-        lax.fori_loop(0, CHUNKS, chunk, 0)
+        def some(p, carry):
+            for c in range(STEP_CHUNKS):
+                chunk(p * STEP_CHUNKS + c, carry)
+            return carry
+
+        lax.fori_loop(0, STEPS, some, 0)
         store = pltpu.make_async_copy(edge, band, sem)
         store.start()
         return store
@@ -371,8 +386,10 @@
 
 
 def second_inside_kernel(
-    place, kept, kept_near, rate, base, tables, base_near, tables_near, moved_part, buf
+    place, kept, kept_near, base, tables, base_near, tables_near, moved_part, held_near, sem
 ):
+    for piece in range(STEPS):
+        load_piece(kept_near, held_near, sem, piece).start()
     device = place[0]
     first = device * VEL_LOCAL
     even = lax.rem(lane_index(), 2) == 0
@@ -386,21 +403,26 @@
             sides = y_sides(index_y >= VG // 2)
             front = base[...] * tables[0, index_x] * tables[1, index_y]
             front_near = base_near[...] * tables_near[0, index_x] * tables_near[1, index_y]
-            for t in range(CHUNK):
-                v = c * CHUNK + t
-                n = index_z + t
-                center = kept[v] + front * tables[2, n]
-                near = kept_near[v] + front_near * tables_near[2, n]
-                x_one, x_two = x_steps(
-                    buf, t, center, jnp.zeros((2, LANES), jnp.float32), forward
+            at = [c * CHUNK + t for t in range(CHUNK)]
+            centers = [kept[v] + front * tables[2, index_z + t] for t, v in enumerate(at)]
+            nears = [
+                held_near[v] + front_near * tables_near[2, index_z + t] for t, v in enumerate(at)
+            ]
+            backs = [y_part(center, near, sides) for center, near in zip(centers, nears)]
+            for t, v in enumerate(at):
+                moved_part[v] = upwind(
+                    centers[t], backs[t], *x_inside(centers[t], forward), even, coef_x, coef_y,
+                    DT * speed_of(index_z + t) * side,
                 )
-                moved_part[v] = upwind(
-                    center, y_part(center, near, sides), x_one, x_two, even, coef_x, coef_y,
-                    DT * speed_of(n) * side,
-                )
-            return carry
-
-        lax.fori_loop(0, CHUNKS, chunk, 0)
+            return carry
+
+        def piece(p, carry):
+            load_piece(kept_near, held_near, sem, p).wait()
+            for c in range(STEP_CHUNKS):
+                chunk(p * STEP_CHUNKS + c, carry)
+            return carry
+
+        lax.fori_loop(0, STEPS, piece, 0)
 
     each_sign(device >= 32, move)
 
@@ -483,7 +505,8 @@
             return carry
 
         def piece(p, carry):
-            lax.fori_loop(p * STEP_CHUNKS, (p + 1) * STEP_CHUNKS, chunk, 0)
+            for c in range(STEP_CHUNKS):
+                chunk(p * STEP_CHUNKS + c, carry)
             load_piece(done, out, sem, p).start()
             return carry
 
@@ -570,7 +593,6 @@
             pltpu.VMEM((VEL_LOCAL, ROWS, LANES), jnp.float32),
             pltpu.VMEM((VEL_LOCAL, ROWS, LANES), jnp.float32),
             pltpu.VMEM((ROWS, LANES), jnp.float32),
-            pltpu.VMEM((CHUNK, 48, LANES), jnp.float32),
             pltpu.SemaphoreType.DMA((STEPS,)),
             pltpu.SemaphoreType.DMA((STEPS,)),
             pltpu.SemaphoreType.DMA,
@@ -604,13 +626,16 @@
     moved_part = pl.pallas_call(
         second_inside_kernel,
         out_shape=f32(VEL_LOCAL, ROWS, LANES),
-        in_specs=[smem()] + [vmem()] * 7,
+        in_specs=[smem(), vmem(), hbm()] + [vmem()] * 4,
         out_specs=vmem(),
-        scratch_shapes=[pltpu.VMEM((CHUNK, 48, LANES), jnp.float32)],
+        scratch_shapes=[
+            pltpu.VMEM((VEL_LOCAL, ROWS, LANES), jnp.float32),
+            pltpu.SemaphoreType.DMA((STEPS,)),
+        ],
         compiler_params=pltpu.CompilerParams(vmem_limit_bytes=16 * 2**20),
         cost_estimate=pl.CostEstimate(flops=50000000, bytes_accessed=6000000, transcendentals=0),
         name="move_inside_two",
-    )(place, kept, kept_near, collision_rate, *own[:2], *near[:2])
+    )(place, kept, in_hbm(kept_near), *own[:2], *near[:2])
     return pl.pallas_call(
         second_kernel,
         out_shape=f32(VEL_LOCAL, ROWS, LANES),

time: 68.9 us -> 63.9 us (0.927)
  Pallas kernels: 18.9 us -> 14 us
    pallas_call x1, Pallas kernels: 5.94 us -> 3.74 us  [body(): pl.pallas_call(second_inside_kernel, out_shape=f32(VEL_LOCAL, ROWS, LANES...]
    pallas_call x1, Pallas kernels: 6.37 us -> 4.57 us  [body(): pl.pallas_call(inside_kernel, out_shape=(f32(VEL_LOCAL, ROWS, LANES), f32...]
  transfers between devices with their start and end apart: 7 -> 7, of which waited for: 2 -> 2; matrix products, arithmetic and copies ran while one was open for 1% -> 1% of each run, Pallas kernels for 21% -> 16%
where the time goes in v5:
time: 63.9 us; the launch traced here: 63.6 us
  starting transfers between devices  22.1 us (35%)
  blocking collectives  18.6 us (29%)
  Pallas kernels  14 us (22%)
  waiting for transfers between devices  7.96 us (12%)
  local copies, waits for them, and re-layouts  0.73 us (1%)
    all_to_all x1, blocking collectives, sum_over_vert(): lax.all_to_all(jnp.broadcast_to(share[None], parts.shape), PLANE, 0, 0)  9.56 us
    all_to_all x1, blocking collectives, sum_over_vert(): share = jnp.sum(lax.all_to_all(parts, PLANE, 0, 0), axis=0)  9.01 us
    all_to_all x1, starting transfers between devices, sum_over_vert(): lax.all_to_all(jnp.broadcast_to(share[None], parts.shape), 'z', 0, 0)  8.19 us
    all_to_all x1, waiting for transfers between devices, sum_over_vert(): lax.all_to_all(jnp.broadcast_to(share[None], parts.shape), 'z', 0, 0)  6.26 us
    pallas_call x1, Pallas kernels, body(): pl.pallas_call(inside_kernel, out_shape=(f32(VEL_LOCAL, ROWS, LANES), f32...  4.57 us
    pallas_call x1, Pallas kernels, body(): pl.pallas_call(second_inside_kernel, out_shape=f32(VEL_LOCAL, ROWS, LANES...  3.74 us
    ppermute x1, starting transfers between devices, body(): total_near = lax.ppermute(total, 'gy', SWAP)  3.73 us
    ppermute x1, starting transfers between devices, body(): f_near = lax.ppermute(distribution, 'gy', SWAP)  3.24 us
  transfers between devices with their start and end apart: 7, of which 2 were waited for; matrix products, arithmetic and copies ran while one was open for 1% of the time, Pallas kernels for 16%

profile of v5, /device:TPU:1, one launch (start us, length us, event | category | flops | bytes accessed | tf_op | source)
XLA Modules:
  0.0 63.6 jit_solution(3633543627951037316)
XLA Ops:
  0.0 3.2 %collective-permute-start = (f32[125,32,128]{2,1,0:T(8,128)}, f32[125,32,128]{2,1,0:T(8,128)}, u32[]{:S(2)}, u32[]{:S(2)}) collective-permute-start(f32[125,32,128]{2,1,0:T(8,128)} %f.3), channel_id=1, source_target_pairs={{0,64},{64,0},{1,65},{65,1},{2,66},{66,2},{3,67},{67,3},{4,68},{68... | collective-permute-start | bytes 6144008 | tf_op jit(solution)/shard_map/ppermute | solution.py:584
  3.2 1.1 %send_rows.1 = f32[125,2,128]{2,1,0:T(2,128)S(1)} custom-call(s32[1]{0:T(128)} %bitcast.place, f32[125,32,128]{2,1,0:T(8,128)} %f.3), custom_call_target="tpu_custom_call" | custom-call | bytes 600000 | tf_op jit(solution)/shard_map/send_rows/pallas_call | solution.py:573
  4.3 0.0 copy-start
  4.3 1.3 %collective-permute-start.1 = (f32[125,2,128]{2,1,0:T(2,128)S(1)}, f32[125,2,128]{2,1,0:T(2,128)S(1)}, u32[]{:S(2)}, u32[]{:S(2)}) collective-permute-start(f32[125,2,128]{2,1,0:T(2,128)S(1)} %send_rows.1), channel_id=1, source_target_pairs={{0,128},{128,0},{1,129},{129,1},{2,130},{130,2},{3,131},{131,3},{4... | collective-permute-start | bytes 384008 | tf_op jit(solution)/shard_map/ppermute | solution.py:583
  5.6 1.7 %collective-permute-done.f_near = f32[125,32,128]{2,1,0:T(8,128)} collective-permute-done((f32[125,32,128]{2,1,0:T(8,128)}, f32[125,32,128]{2,1,0:T(8,128)}, u32[]{:S(2)}, u32[]{:S(2)}) %collective-permute-start) | collective-permute-done | bytes 2048032 | tf_op jit(solution)/shard_map/ppermute | solution.py:584
  7.3 4.6 %move_inside.1 = (f32[125,32,128]{2,1,0:T(8,128)S(1)}, f32[125,2,128]{2,1,0:T(2,128)S(1)}, f32[7,6,32,128]{3,2,1,0:T(8,128)S(1)}) custom-call(s32[1]{0:T(128)} %bitcast.place, f32[125,32,128]{2,1,0:T(8,128)} %f.3, f32[125,32,128]{2,1,0:T(8,128)} %collective-permute-done.f_near, f32[32,128]{1,0:T(8,128)} %rate.7), custom_call_target="tpu_custom_call" | custom-call | flops 50000000 | bytes 6000000 | tf_op jit(solution)/shard_map/move_inside/pallas_call | solution.py:585
  11.9 0.0 collective-permute-done.1.f_edge
  11.9 0.0 copy-done
  11.9 1.6 %enter_and_sum.1 = (f32[125,32,128]{2,1,0:T(8,128)S(1)}, f32[448,128]{1,0:T(8,128)S(1)}) custom-call(s32[1]{0:T(128)} %bitcast.place, f32[125,32,128]{2,1,0:T(8,128)S(1)} %get-tuple-element.18.kept_in, f32[7,6,32,128]{3,2,1,0:T(8,128)S(1)} %get-tuple-element.19.groups_in, ...), custom_call_target="tpu_custom_call", output_to_operand_aliasing={{0}: (1, {})} | custom-call | tf_op jit(solution)/shard_map/enter_and_sum/pallas_call | solution.py:605
  13.5 0.5 collective-permute-start.2
  14.0 9.0 %all_to_all.15 = f32[8,7,8,128]{3,2,1,0:T(8,128)S(1)} all-to-all(f32[8,7,8,128]{3,2,1,0:T(8,128)S(1)} %bitcast.7), channel_id=1, replica_groups=mesh['gx'=2,'gy'=2,'x'=4,'yl'=2,'z'=8] {'x','yl'}, dimensions={0} | all-to-all | bytes 458752 | tf_op jit(solution)/shard_map/all_to_all | solution.py:545
  23.0 0.7 %broadcast_in_dim.4 = f32[8,7,8,128]{3,2,1,0:T(8,128)} broadcast(f32[7,8,128]{2,1,0:T(8,128)S(1)} %reduce_sum.18), dimensions={1,2,3} | broadcast | bytes 258048 | tf_op jit(solution)/shard_map/broadcast_in_dim | solution.py:546
  23.7 8.2 %all-to-all-start.1 = ((f32[8,7,8,128]{3,2,1,0:T(8,128)}), f32[8,7,8,128]{3,2,1,0:T(8,128)S(1)}, u32[]{:S(2)}, u32[]{:S(2)}) async-start(f32[8,7,8,128]{3,2,1,0:T(8,128)} %broadcast_in_dim.4), calls=%async_computation.1 | async-start | bytes 458752 | tf_op jit(solution)/shard_map/all_to_all | solution.py:546
  31.9 2.6 %collective-permute-start.3 = (f32[125,2,128]{2,1,0:T(2,128)S(1)}, f32[125,2,128]{2,1,0:T(2,128)S(1)}, u32[]{:S(2)}, u32[]{:S(2)}) collective-permute-start(f32[125,2,128]{2,1,0:T(2,128)S(1)} %get-tuple-element.22), channel_id=1, source_target_pairs={{0,128},{128,0},{1,129},{129,1},{2,130},{130,2},{3,131},{131,3},{4... | collective-permute-start | bytes 384008 | tf_op jit(solution)/shard_map/ppermute | solution.py:604
  34.5 6.3 %all-to-all-done.1 = f32[8,7,8,128]{3,2,1,0:T(8,128)S(1)} async-done(((f32[8,7,8,128]{3,2,1,0:T(8,128)}), f32[8,7,8,128]{3,2,1,0:T(8,128)S(1)}, u32[]{:S(2)}, u32[]{:S(2)}) %all-to-all-start.1) | async-done | bytes 229408 | tf_op jit(solution)/shard_map/all_to_all | solution.py:546
  40.8 0.0 collective-permute-done.3.kept_edge
  40.9 9.6 %all_to_all.16 = f32[8,7,8,128]{3,2,1,0:T(8,128)S(1)} all-to-all(f32[8,7,8,128]{3,2,1,0:T(8,128)S(1)} %broadcast_in_dim.5), channel_id=1, replica_groups=mesh['gx'=2,'gy'=2,'x'=4,'yl'=2,'z'=8] {'x','yl'}, dimensions={0} | all-to-all | bytes 458752 | tf_op jit(solution)/shard_map/all_to_all | solution.py:548
  50.4 3.7 %collective-permute-start.4 = (f32[448,128]{1,0:T(8,128)S(1)}, f32[448,128]{1,0:T(8,128)S(1)}, u32[]{:S(2)}, u32[]{:S(2)}) collective-permute-start(f32[448,128]{1,0:T(8,128)S(1)} %bitcast.3), channel_id=1, source_target_pairs={{0,64},{64,0},{1,65},{65,1},{2,66},{66,2},{3,67},{67,3},{4,68},{68... | collective-permute-start | bytes 688136 | tf_op jit(solution)/shard_map/ppermute | solution.py:622
  54.2 2.6 %collective-permute-start.5 = (f32[64,128]{1,0:T(8,128)S(1)}, f32[64,128]{1,0:T(8,128)S(1)}, u32[]{:S(2)}, u32[]{:S(2)}) collective-permute-start(f32[64,128]{1,0:T(8,128)S(1)} %slice.9), channel_id=1, source_target_pairs={{0,128},{128,0},{1,129},{129,1},{2,130},{130,2},{3,131},{131,3},{4... | collective-permute-start | bytes 98312 | tf_op jit(solution)/shard_map/ppermute | solution.py:623
  56.8 0.6 tables_own.1
  57.4 0.0 collective-permute-done.4.total.total_near
  57.4 0.5 tables_near.1
  57.9 0.0 collective-permute-done.2.kept_near
  57.9 3.7 %move_inside_two.1.moved_part = f32[125,32,128]{2,1,0:T(8,128)S(1)} custom-call(s32[1]{0:T(128)} %bitcast.place, f32[125,32,128]{2,1,0:T(8,128)S(1)} %get-tuple-element.20.kept, f32[125,32,128]{2,1,0:T(8,128)} %collective-permute-done.2.kept_near, f32[32,128]{1,0:T(8,128)S(1)} %get-tuple-element.24.base, f32[3,20,32,128]{3,2,1,0:T(8,128)S(1)} %get-tuple-element.25.tables, ...), custom_call_target="tpu_custom_call" | custom-call | flops 50000000 | bytes 6000000 | tf_op jit(solution)/shard_map/move_inside_two/pallas_call | solution.py:626
  61.6 0.0 collective-permute-done.5.total_edge
  61.7 1.9 %collide_two.1 = f32[125,32,128]{2,1,0:T(8,128)} custom-call(s32[1]{0:T(128)} %bitcast.place, f32[125,32,128]{2,1,0:T(8,128)S(1)} %move_inside_two.1.moved_part, f32[125,2,128]{2,1,0:T(2,128)S(1)} %collective-permute-done.3.kept_edge, f32[448,128]{1,0:T(8,128)S(1)} %bitcast.6, f32[448,128]{1,0:T(8,128)S(1)} %collective-permute-done.4.total.total_near, ...), custom_call_target="tpu_custom_call" | custom-call | tf_op jit(solution)/shard_map/collide_two/pallas_call | solution.py:639
  (5 shorter events, 0.1 us)
Async XLA Ops:
  0.0 7.3 %collective-permute-start = (f32[125,32,128]{2,1,0:T(8,128)}, f32[125,32,128]{2,1,0:T(8,128)}, u32[]{:S(2)}, u32[]{:S(2)}) collective-permute-start(f32[125,32,128]{2,1,0:T(8,128)} %f.3), channel_id=1, source_target_pairs={{0,64},{64,0},{1,65},{65,1},{2,66},{66,2},{3,67},{67,3},{4,68},{68... | collective-permute-start | bytes 6144008 | tf_op jit(solution)/shard_map/ppermute | solution.py:584
  4.3 7.6 %copy-start = (f32[32,128]{1,0:T(8,128)S(1)}, f32[32,128]{1,0:T(8,128)}, u32[]{:S(2)}) copy-start(f32[32,128]{1,0:T(8,128)} %rate.7) | copy-start | bytes 49156
  4.3 7.5 %collective-permute-start.1 = (f32[125,2,128]{2,1,0:T(2,128)S(1)}, f32[125,2,128]{2,1,0:T(2,128)S(1)}, u32[]{:S(2)}, u32[]{:S(2)}) collective-permute-start(f32[125,2,128]{2,1,0:T(2,128)S(1)} %send_rows.1), channel_id=1, source_target_pairs={{0,128},{128,0},{1,129},{129,1},{2,130},{130,2},{3,131},{131,3},{4... | collective-permute-start | bytes 384008 | tf_op jit(solution)/shard_map/ppermute | solution.py:583
  13.5 44.3 %collective-permute-start.2 = (f32[125,32,128]{2,1,0:T(8,128)S(1)}, f32[125,32,128]{2,1,0:T(8,128)}, u32[]{:S(2)}, u32[]{:S(2)}) collective-permute-start(f32[125,32,128]{2,1,0:T(8,128)S(1)} %get-tuple-element.20.kept), channel_id=1, source_target_pairs={{0,64},{64,0},{1,65},{65,1},{2,66},{66,2},{3,67},{67,3},{4,68},{68... | collective-permute-start | bytes 6144008 | tf_op jit(solution)/shard_map/ppermute | solution.py:620
  23.7 17.1 %all-to-all-start.1 = ((f32[8,7,8,128]{3,2,1,0:T(8,128)}), f32[8,7,8,128]{3,2,1,0:T(8,128)S(1)}, u32[]{:S(2)}, u32[]{:S(2)}) async-start(f32[8,7,8,128]{3,2,1,0:T(8,128)} %broadcast_in_dim.4), calls=%async_computation.1 | async-start | bytes 458752 | tf_op jit(solution)/shard_map/all_to_all | solution.py:546
  31.9 8.9 %collective-permute-start.3 = (f32[125,2,128]{2,1,0:T(2,128)S(1)}, f32[125,2,128]{2,1,0:T(2,128)S(1)}, u32[]{:S(2)}, u32[]{:S(2)}) collective-permute-start(f32[125,2,128]{2,1,0:T(2,128)S(1)} %get-tuple-element.22), channel_id=1, source_target_pairs={{0,128},{128,0},{1,129},{129,1},{2,130},{130,2},{3,131},{131,3},{4... | collective-permute-start | bytes 384008 | tf_op jit(solution)/shard_map/ppermute | solution.py:604
  50.4 7.0 %collective-permute-start.4 = (f32[448,128]{1,0:T(8,128)S(1)}, f32[448,128]{1,0:T(8,128)S(1)}, u32[]{:S(2)}, u32[]{:S(2)}) collective-permute-start(f32[448,128]{1,0:T(8,128)S(1)} %bitcast.3), channel_id=1, source_target_pairs={{0,64},{64,0},{1,65},{65,1},{2,66},{66,2},{3,67},{67,3},{4,68},{68... | collective-permute-start | bytes 688136 | tf_op jit(solution)/shard_map/ppermute | solution.py:622
  54.2 7.5 %collective-permute-start.5 = (f32[64,128]{1,0:T(8,128)S(1)}, f32[64,128]{1,0:T(8,128)S(1)}, u32[]{:S(2)}, u32[]{:S(2)}) collective-permute-start(f32[64,128]{1,0:T(8,128)S(1)} %slice.9), channel_id=1, source_target_pairs={{0,128},{128,0},{1,129},{129,1},{2,130},{130,2},{3,131},{131,3},{4... | collective-permute-start | bytes 98312 | tf_op jit(solution)/shard_map/ppermute | solution.py:623

commit v6 on v5

--- a/solution.py
+++ b/solution.py
@@ -30,11 +30,13 @@
 PLANE = ("x", "yl")
 
 ROW_SECOND = 5 * ROWS
-ROW_SPILL_Y = 10 * ROWS
+ROW_PACKED = 10 * ROWS
 ROW_SPILL_X = 11 * ROWS
-ROW_EDGE = 12 * ROWS
-ROW_RATE = 13 * ROWS
-ROW_COUNT = 14 * ROWS
+ROW_EDGE = ROW_SPILL_X + 20
+ROW_COUNT = 12 * ROWS
+HALF = LANES // 2
+HALF_AT = 48
+FEW = 12
 
 
 def speed_of(index):
@@ -184,7 +186,7 @@
 
 
 def edge_kernel(
-    place, kept_in, groups_in, f_edge, rate, kept, sums, groups, edge, buf, sem
+    place, kept_in, groups_in, f_edge, rate, kept, sums, groups, edge, few, buf, sem
 ):
     del kept_in
     device = place[0]
@@ -277,10 +279,10 @@
             for m, value in enumerate(five(near_x)):
                 at = ROW_SPILL_X + 4 * m + (0 if forward else 2)
                 sums[at : at + 2] += value
-            packed = sums[ROW_SPILL_Y : ROW_SPILL_Y + ROWS]
+            packed = sums[ROW_PACKED : ROW_PACKED + ROWS]
             for m, value in enumerate(five(near_y)):
                 packed = packed + (pltpu.roll(value, 8 * m, 1) if m else value)
-            sums[ROW_SPILL_Y : ROW_SPILL_Y + ROWS] = packed
+            sums[ROW_PACKED : ROW_PACKED + ROWS] = packed
 
             return carry
 
@@ -295,16 +297,25 @@
 
     each_sign(device >= 32, both)
     for m in range(5):
-        at = ROW_EDGE + 4 * m
-        sums[at : at + 2] = sums[ROWS * m + 30 : ROWS * m + 32]
-        sums[at + 2 : at + 4] = sums[ROWS * m : ROWS * m + 2]
+        target, at = (sums, ROW_EDGE + 4 * m) if m < 3 else (few, 4 * (m - 3))
+        target[at : at + 2] = sums[ROWS * m + 30 : ROWS * m + 32]
+        target[at + 2 : at + 4] = sums[ROWS * m : ROWS * m + 2]
+    few[8:16] = jnp.zeros((8, LANES), jnp.float32)
 
     @pl.when(device == 0)
     def _():
-        at = ROW_EDGE + 20
-        sums[at : at + 2] = rate[30:32]
-        sums[at + 2 : at + 4] = rate[0:2]
-        sums[ROW_RATE : ROW_RATE + ROWS] = rate[...]
+        few[8:10] = rate[30:32]
+        few[10:12] = rate[0:2]
+        lane = lane_index()
+        border = jnp.where((lane < 4) | (lane >= LANES - 4), rate[...], 0.0)
+        sums[ROW_PACKED : ROW_PACKED + ROWS] += pltpu.roll(border, 40, 1)
+
+    rest = few[...]
+    lane = lax.broadcasted_iota(jnp.int32, rest.shape, 1)
+    left = pltpu.roll(jnp.where(lane < HALF, rest, 0.0), HALF_AT, 1)
+    right = pltpu.roll(jnp.where(lane >= HALF, rest, 0.0), LANES - (HALF - HALF_AT), 1)
+    sums[ROW_PACKED : ROW_PACKED + FEW] += left[0:FEW]
+    sums[ROW_PACKED + FEW : ROW_PACKED + 2 * FEW] += right[0:FEW]
 
 
 def parameters(moments):
@@ -372,17 +383,21 @@
 
 
 def table_kernel(wanted, total, rate, base, tables, kinds):
-    def block(b, carry):
-        def rows(start):
-            return pl.ds(pl.multiple_of(start + b * 8, 8), 8)
-
+    for at in range(0, ROWS, 8):
+        rows = slice(at, at + 8)
         one_block(
-            rows(0), [total[rows(ROWS * m)] for m in range(5)], rate[rows(0)], base, tables, kinds,
-            wanted,
+            rows, [total[ROWS * m + at : ROWS * m + at + 8] for m in range(5)], rate[rows], base,
+            tables, kinds, wanted,
         )
-        return carry
-
-    lax.fori_loop(0, ROWS // 8, block, 0)
+
+
+def near_kernel(wanted, total, base, tables, kinds):
+    for at in range(0, ROWS, 8):
+        rate = pltpu.roll(total[ROW_PACKED + at : ROW_PACKED + at + 8], LANES - 40, 1)
+        one_block(
+            slice(at, at + 8), [total[ROWS * m + at : ROWS * m + at + 8] for m in range(5)], rate,
+            base, tables, kinds, wanted,
+        )
 
 
 def second_inside_kernel(
@@ -429,32 +444,38 @@
 
 def second_kernel(
     place, moved_part, kept_edge, total, total_near, total_edge, rate, kinds, kinds_near,
-    out, base_edge, tables_edge, kinds_edge, table_two, done, buf, sem,
+    out, base_edge, tables_edge, kinds_edge, table_two, done, few, buf, sem,
 ):
     device = place[0]
     first = device * VEL_LOCAL
     even = lax.rem(lane_index(), 2) == 0
     keep = 1.0 - rate[...]
 
-    def edge(row):
-        rows = total_edge[row : row + 4]
+    left = pltpu.roll(total_edge[0:16], LANES - HALF_AT, 1)
+    right = pltpu.roll(total_edge[FEW : FEW + 16], HALF - HALF_AT, 1)
+    few[...] = jnp.where(lax.broadcasted_iota(jnp.int32, left.shape, 1) < HALF, left, right)
+
+    def edge(source, row):
+        rows = source[row : row + 4]
         return jnp.concatenate([rows, rows], axis=0)
 
     one_block(
-        slice(0, 8), [edge(ROWS + 4 * m) for m in range(5)], edge(ROWS + 20), base_edge,
+        slice(0, 8),
+        [edge(total_edge, ROWS + 20 + 4 * m) for m in range(3)] + [edge(few, 0), edge(few, 4)],
+        edge(few, 8), base_edge,
         tables_edge, kinds_edge, "x",
     )
-    spill_y = total_near[ROW_SPILL_Y : ROW_SPILL_Y + ROWS]
+    spill_y = total_near[ROW_PACKED : ROW_PACKED + ROWS]
     moments = []
     for m in range(5):
         result = total[ROW_SECOND + ROWS * m : ROW_SECOND + ROWS * (m + 1)] + kinds[5, m]
         x_one, x_two = x_steps(
             buf, 0, kinds[0, m],
-            kinds_edge[0, m, 0:2] + (1.0 / DT) * total_edge[4 * m : 4 * m + 2], True,
+            kinds_edge[0, m, 0:2] + (1.0 / DT) * total_edge[ROWS + 4 * m : ROWS + 4 * m + 2], True,
         )
         x_low, x_lower = x_steps(
             buf, 1, kinds[1, m],
-            kinds_edge[1, m, 2:4] + (1.0 / DT) * total_edge[4 * m + 2 : 4 * m + 4], False,
+            kinds_edge[1, m, 2:4] + (1.0 / DT) * total_edge[ROWS + 4 * m + 2 : ROWS + 4 * m + 4], False,
         )
         spill = pltpu.roll(spill_y, LANES - 8 * m, 1) if m else spill_y
         spill = (1.0 / DT) * spill
@@ -553,18 +574,18 @@
     return jax.ShapeDtypeStruct(shape, jnp.float32)
 
 
-def tables_of(total, rate, wanted, name):
+def tables_of(kernel, wanted, name, *operands):
     return pl.pallas_call(
-        functools.partial(table_kernel, wanted),
+        functools.partial(kernel, wanted),
         out_shape=(
             f32(ROWS, LANES), f32(3, VG, ROWS, LANES), f32(6, 5, ROWS, LANES)
         ),
-        in_specs=[vmem(), vmem()],
+        in_specs=[vmem()] * len(operands),
         out_specs=(vmem(), vmem(), vmem()),
         compiler_params=pltpu.CompilerParams(vmem_limit_bytes=16 * 2**20),
         cost_estimate=pl.CostEstimate(flops=8000000, bytes_accessed=3000000, transcendentals=250000),
         name=name,
-    )(total, rate)
+    )(*operands)
 
 
 def body(distribution, collision_rate):
@@ -610,6 +631,7 @@
         scratch_shapes=[
             pltpu.VMEM((GROUPS, 6, ROWS, LANES), jnp.float32),
             pltpu.VMEM((VEL_LOCAL, 8, LANES), jnp.float32),
+            pltpu.VMEM((16, LANES), jnp.float32),
             pltpu.VMEM((CHUNK, 48, LANES), jnp.float32),
             pltpu.SemaphoreType.DMA,
         ],
@@ -620,9 +642,9 @@
     kept_near = lax.ppermute(kept, "gy", SWAP)
     total, kept_edge = sum_over_vert(partial, kept_edge)
     total_near = lax.ppermute(total, "gy", SWAP)
-    total_edge = lax.ppermute(total[ROW_SPILL_X : ROW_EDGE + ROWS], "gx", SWAP)
-    own = tables_of(total, collision_rate, "xyz", "tables_own")
-    near = tables_of(total_near, total_near[ROW_RATE : ROW_RATE + ROWS], "y", "tables_near")
+    total_edge = lax.ppermute(total[ROW_PACKED:], "gx", SWAP)
+    own = tables_of(table_kernel, "xyz", "tables_own", total, collision_rate)
+    near = tables_of(near_kernel, "y", "tables_near", total_near)
     moved_part = pl.pallas_call(
         second_inside_kernel,
         out_shape=f32(VEL_LOCAL, ROWS, LANES),
@@ -647,6 +669,7 @@
             pltpu.VMEM((2, 5, 8, LANES), jnp.float32),
             pltpu.VMEM((VG + 4, ROWS, LANES), jnp.float32),
             pltpu.VMEM((VEL_LOCAL, ROWS, LANES), jnp.float32),
+            pltpu.VMEM((16, LANES), jnp.float32),
             pltpu.VMEM((CHUNK, 48, LANES), jnp.float32),
             pltpu.SemaphoreType.DMA((STEPS,)),
         ],

time: 63.9 us -> 62.6 us (0.980)
  blocking collectives: 18.6 us -> 17 us
    all_to_all x1, blocking collectives: 9.56 us -> 8.18 us  [sum_over_vert(): lax.all_to_all(jnp.broadcast_to(share[None], parts.shape), PLANE, 0, 0)]
  transfers between devices with their start and end apart: 7 -> 7, of which waited for: 2 -> 2; matrix products, arithmetic and copies ran while one was open for 1% -> 1% of each run, Pallas kernels for 16% -> 17%
where the time goes in v6:
time: 62.6 us; the launch traced here: 62.3 us
  starting transfers between devices  22.5 us (36%)
  blocking collectives  17 us (27%)
  Pallas kernels  14.1 us (23%)
  waiting for transfers between devices  7.81 us (12%)
  local copies, waits for them, and re-layouts  0.71 us (1%)
    all_to_all x1, blocking collectives, sum_over_vert(): share = jnp.sum(lax.all_to_all(parts, PLANE, 0, 0), axis=0)  8.78 us
    all_to_all x1, starting transfers between devices, sum_over_vert(): lax.all_to_all(jnp.broadcast_to(share[None], parts.shape), 'z', 0, 0)  8.19 us
    all_to_all x1, blocking collectives, sum_over_vert(): lax.all_to_all(jnp.broadcast_to(share[None], parts.shape), PLANE, 0, 0)  8.18 us
    all_to_all x1, waiting for transfers between devices, sum_over_vert(): lax.all_to_all(jnp.broadcast_to(share[None], parts.shape), 'z', 0, 0)  6.11 us
    pallas_call x1, Pallas kernels, body(): pl.pallas_call(inside_kernel, out_shape=(f32(VEL_LOCAL, ROWS, LANES), f32...  4.57 us
    ppermute x1, starting transfers between devices, body(): total_near = lax.ppermute(total, 'gy', SWAP)  4.14 us
    pallas_call x1, Pallas kernels, body(): pl.pallas_call(second_inside_kernel, out_shape=f32(VEL_LOCAL, ROWS, LANES...  3.74 us
    ppermute x1, starting transfers between devices, body(): f_near = lax.ppermute(distribution, 'gy', SWAP)  3.24 us
  transfers between devices with their start and end apart: 7, of which 2 were waited for; matrix products, arithmetic and copies ran while one was open for 1% of the time, Pallas kernels for 17%

profile of v6, /device:TPU:1, one launch (start us, length us, event | category | flops | bytes accessed | tf_op | source)
XLA Modules:
  0.0 62.3 jit_solution(8770911641945390958)
XLA Ops:
  0.0 3.2 %collective-permute-start = (f32[125,32,128]{2,1,0:T(8,128)}, f32[125,32,128]{2,1,0:T(8,128)}, u32[]{:S(2)}, u32[]{:S(2)}) collective-permute-start(f32[125,32,128]{2,1,0:T(8,128)} %f.3), channel_id=1, source_target_pairs={{0,64},{64,0},{1,65},{65,1},{2,66},{66,2},{3,67},{67,3},{4,68},{68... | collective-permute-start | bytes 6144008 | tf_op jit(solution)/shard_map/ppermute | solution.py:605
  3.2 1.1 %send_rows.1 = f32[125,2,128]{2,1,0:T(2,128)S(1)} custom-call(s32[1]{0:T(128)} %bitcast.place, f32[125,32,128]{2,1,0:T(8,128)} %f.3), custom_call_target="tpu_custom_call" | custom-call | bytes 600000 | tf_op jit(solution)/shard_map/send_rows/pallas_call | solution.py:594
  4.3 0.0 copy-start
  4.3 1.3 %collective-permute-start.1 = (f32[125,2,128]{2,1,0:T(2,128)S(1)}, f32[125,2,128]{2,1,0:T(2,128)S(1)}, u32[]{:S(2)}, u32[]{:S(2)}) collective-permute-start(f32[125,2,128]{2,1,0:T(2,128)S(1)} %send_rows.1), channel_id=1, source_target_pairs={{0,128},{128,0},{1,129},{129,1},{2,130},{130,2},{3,131},{131,3},{4... | collective-permute-start | bytes 384008 | tf_op jit(solution)/shard_map/ppermute | solution.py:604
  5.6 1.7 %collective-permute-done.f_near = f32[125,32,128]{2,1,0:T(8,128)} collective-permute-done((f32[125,32,128]{2,1,0:T(8,128)}, f32[125,32,128]{2,1,0:T(8,128)}, u32[]{:S(2)}, u32[]{:S(2)}) %collective-permute-start) | collective-permute-done | bytes 2048032 | tf_op jit(solution)/shard_map/ppermute | solution.py:605
  7.3 4.6 %move_inside.1 = (f32[125,32,128]{2,1,0:T(8,128)S(1)}, f32[125,2,128]{2,1,0:T(2,128)S(1)}, f32[7,6,32,128]{3,2,1,0:T(8,128)S(1)}) custom-call(s32[1]{0:T(128)} %bitcast.place, f32[125,32,128]{2,1,0:T(8,128)} %f.3, f32[125,32,128]{2,1,0:T(8,128)} %collective-permute-done.f_near, f32[32,128]{1,0:T(8,128)} %rate.7), custom_call_target="tpu_custom_call" | custom-call | flops 50000000 | bytes 6000000 | tf_op jit(solution)/shard_map/move_inside/pallas_call | solution.py:606
  11.9 0.0 collective-permute-done.1.f_edge
  11.9 0.0 copy-done
  11.9 1.8 %enter_and_sum.1 = (f32[125,32,128]{2,1,0:T(8,128)S(1)}, f32[384,128]{1,0:T(8,128)S(1)}) custom-call(s32[1]{0:T(128)} %bitcast.place, f32[125,32,128]{2,1,0:T(8,128)S(1)} %get-tuple-element.18.kept_in, f32[7,6,32,128]{3,2,1,0:T(8,128)S(1)} %get-tuple-element.19.groups_in, ...), custom_call_target="tpu_custom_call", output_to_operand_aliasing={{0}: (1, {})} | custom-call | tf_op jit(solution)/shard_map/enter_and_sum/pallas_call | solution.py:626
  13.7 0.5 collective-permute-start.2
  14.1 8.8 %all_to_all.15 = f32[8,6,8,128]{3,2,1,0:T(8,128)S(1)} all-to-all(f32[8,6,8,128]{3,2,1,0:T(8,128)S(1)} %bitcast.7), channel_id=1, replica_groups=mesh['gx'=2,'gy'=2,'x'=4,'yl'=2,'z'=8] {'x','yl'}, dimensions={0} | all-to-all | bytes 393216 | tf_op jit(solution)/shard_map/all_to_all | solution.py:566
  22.9 0.7 %broadcast_in_dim.4 = f32[8,6,8,128]{3,2,1,0:T(8,128)} broadcast(f32[6,8,128]{2,1,0:T(8,128)S(1)} %reduce_sum.18), dimensions={1,2,3} | broadcast | bytes 221184 | tf_op jit(solution)/shard_map/broadcast_in_dim | solution.py:567
  23.6 8.2 %all-to-all-start.1 = ((f32[8,6,8,128]{3,2,1,0:T(8,128)}), f32[8,6,8,128]{3,2,1,0:T(8,128)S(1)}, u32[]{:S(2)}, u32[]{:S(2)}) async-start(f32[8,6,8,128]{3,2,1,0:T(8,128)} %broadcast_in_dim.4), calls=%async_computation.1 | async-start | bytes 393216 | tf_op jit(solution)/shard_map/all_to_all | solution.py:567
  31.8 2.6 %collective-permute-start.3 = (f32[125,2,128]{2,1,0:T(2,128)S(1)}, f32[125,2,128]{2,1,0:T(2,128)S(1)}, u32[]{:S(2)}, u32[]{:S(2)}) collective-permute-start(f32[125,2,128]{2,1,0:T(2,128)S(1)} %get-tuple-element.22), channel_id=1, source_target_pairs={{0,128},{128,0},{1,129},{129,1},{2,130},{130,2},{3,131},{131,3},{4... | collective-permute-start | bytes 384008 | tf_op jit(solution)/shard_map/ppermute | solution.py:625
  34.4 6.1 %all-to-all-done.1 = f32[8,6,8,128]{3,2,1,0:T(8,128)S(1)} async-done(((f32[8,6,8,128]{3,2,1,0:T(8,128)}), f32[8,6,8,128]{3,2,1,0:T(8,128)S(1)}, u32[]{:S(2)}, u32[]{:S(2)}) %all-to-all-start.1) | async-done | bytes 196640 | tf_op jit(solution)/shard_map/all_to_all | solution.py:567
  40.6 0.0 collective-permute-done.3.kept_edge
  40.6 8.2 %all_to_all.16 = f32[8,6,8,128]{3,2,1,0:T(8,128)S(1)} all-to-all(f32[8,6,8,128]{3,2,1,0:T(8,128)S(1)} %broadcast_in_dim.5), channel_id=1, replica_groups=mesh['gx'=2,'gy'=2,'x'=4,'yl'=2,'z'=8] {'x','yl'}, dimensions={0} | all-to-all | bytes 393216 | tf_op jit(solution)/shard_map/all_to_all | solution.py:569
  48.8 4.1 %collective-permute-start.4 = (f32[384,128]{1,0:T(8,128)S(1)}, f32[384,128]{1,0:T(8,128)S(1)}, u32[]{:S(2)}, u32[]{:S(2)}) collective-permute-start(f32[384,128]{1,0:T(8,128)S(1)} %bitcast.3), channel_id=1, source_target_pairs={{0,64},{64,0},{1,65},{65,1},{2,66},{66,2},{3,67},{67,3},{4,68},{68... | collective-permute-start | bytes 589832 | tf_op jit(solution)/shard_map/ppermute | solution.py:644
  52.9 2.6 %collective-permute-start.5 = (f32[64,128]{1,0:T(8,128)S(1)}, f32[64,128]{1,0:T(8,128)S(1)}, u32[]{:S(2)}, u32[]{:S(2)}) collective-permute-start(f32[64,128]{1,0:T(8,128)S(1)} %slice.4), channel_id=1, source_target_pairs={{0,128},{128,0},{1,129},{129,1},{2,130},{130,2},{3,131},{131,3},{4... | collective-permute-start | bytes 98312 | tf_op jit(solution)/shard_map/ppermute | solution.py:645
  55.6 0.5 tables_own.1
  56.1 0.0 collective-permute-done.4.total.total_near
  56.1 0.4 tables_near.1
  56.5 0.0 collective-permute-done.2.kept_near
  56.5 3.7 %move_inside_two.1.moved_part = f32[125,32,128]{2,1,0:T(8,128)S(1)} custom-call(s32[1]{0:T(128)} %bitcast.place, f32[125,32,128]{2,1,0:T(8,128)S(1)} %get-tuple-element.20.kept, f32[125,32,128]{2,1,0:T(8,128)} %collective-permute-done.2.kept_near, f32[32,128]{1,0:T(8,128)S(1)} %get-tuple-element.24.base, f32[3,20,32,128]{3,2,1,0:T(8,128)S(1)} %get-tuple-element.25.tables, ...), custom_call_target="tpu_custom_call" | custom-call | flops 50000000 | bytes 6000000 | tf_op jit(solution)/shard_map/move_inside_two/pallas_call | solution.py:648
  60.3 0.0 collective-permute-done.5.total_edge
  60.3 2.0 %collide_two.1 = f32[125,32,128]{2,1,0:T(8,128)} custom-call(s32[1]{0:T(128)} %bitcast.place, f32[125,32,128]{2,1,0:T(8,128)S(1)} %move_inside_two.1.moved_part, f32[125,2,128]{2,1,0:T(2,128)S(1)} %collective-permute-done.3.kept_edge, f32[384,128]{1,0:T(8,128)S(1)} %bitcast.6, f32[384,128]{1,0:T(8,128)S(1)} %collective-permute-done.4.total.total_near, ...), custom_call_target="tpu_custom_call" | custom-call | tf_op jit(solution)/shard_map/collide_two/pallas_call | solution.py:661
  (4 shorter events, 0.0 us)
Async XLA Ops:
  0.0 7.3 %collective-permute-start = (f32[125,32,128]{2,1,0:T(8,128)}, f32[125,32,128]{2,1,0:T(8,128)}, u32[]{:S(2)}, u32[]{:S(2)}) collective-permute-start(f32[125,32,128]{2,1,0:T(8,128)} %f.3), channel_id=1, source_target_pairs={{0,64},{64,0},{1,65},{65,1},{2,66},{66,2},{3,67},{67,3},{4,68},{68... | collective-permute-start | bytes 6144008 | tf_op jit(solution)/shard_map/ppermute | solution.py:605
  4.3 7.6 %copy-start = (f32[32,128]{1,0:T(8,128)S(1)}, f32[32,128]{1,0:T(8,128)}, u32[]{:S(2)}) copy-start(f32[32,128]{1,0:T(8,128)} %rate.7) | copy-start | bytes 49156
  4.3 7.5 %collective-permute-start.1 = (f32[125,2,128]{2,1,0:T(2,128)S(1)}, f32[125,2,128]{2,1,0:T(2,128)S(1)}, u32[]{:S(2)}, u32[]{:S(2)}) collective-permute-start(f32[125,2,128]{2,1,0:T(2,128)S(1)} %send_rows.1), channel_id=1, source_target_pairs={{0,128},{128,0},{1,129},{129,1},{2,130},{130,2},{3,131},{131,3},{4... | collective-permute-start | bytes 384008 | tf_op jit(solution)/shard_map/ppermute | solution.py:604
  13.7 42.9 %collective-permute-start.2 = (f32[125,32,128]{2,1,0:T(8,128)S(1)}, f32[125,32,128]{2,1,0:T(8,128)}, u32[]{:S(2)}, u32[]{:S(2)}) collective-permute-start(f32[125,32,128]{2,1,0:T(8,128)S(1)} %get-tuple-element.20.kept), channel_id=1, source_target_pairs={{0,64},{64,0},{1,65},{65,1},{2,66},{66,2},{3,67},{67,3},{4,68},{68... | collective-permute-start | bytes 6144008 | tf_op jit(solution)/shard_map/ppermute | solution.py:642
  23.6 16.9 %all-to-all-start.1 = ((f32[8,6,8,128]{3,2,1,0:T(8,128)}), f32[8,6,8,128]{3,2,1,0:T(8,128)S(1)}, u32[]{:S(2)}, u32[]{:S(2)}) async-start(f32[8,6,8,128]{3,2,1,0:T(8,128)} %broadcast_in_dim.4), calls=%async_computation.1 | async-start | bytes 393216 | tf_op jit(solution)/shard_map/all_to_all | solution.py:567
  31.8 8.8 %collective-permute-start.3 = (f32[125,2,128]{2,1,0:T(2,128)S(1)}, f32[125,2,128]{2,1,0:T(2,128)S(1)}, u32[]{:S(2)}, u32[]{:S(2)}) collective-permute-start(f32[125,2,128]{2,1,0:T(2,128)S(1)} %get-tuple-element.22), channel_id=1, source_target_pairs={{0,128},{128,0},{1,129},{129,1},{2,130},{130,2},{3,131},{131,3},{4... | collective-permute-start | bytes 384008 | tf_op jit(solution)/shard_map/ppermute | solution.py:625
  48.8 7.3 %collective-permute-start.4 = (f32[384,128]{1,0:T(8,128)S(1)}, f32[384,128]{1,0:T(8,128)S(1)}, u32[]{:S(2)}, u32[]{:S(2)}) collective-permute-start(f32[384,128]{1,0:T(8,128)S(1)} %bitcast.3), channel_id=1, source_target_pairs={{0,64},{64,0},{1,65},{65,1},{2,66},{66,2},{3,67},{67,3},{4,68},{68... | collective-permute-start | bytes 589832 | tf_op jit(solution)/shard_map/ppermute | solution.py:644
  52.9 7.4 %collective-permute-start.5 = (f32[64,128]{1,0:T(8,128)S(1)}, f32[64,128]{1,0:T(8,128)S(1)}, u32[]{:S(2)}, u32[]{:S(2)}) collective-permute-start(f32[64,128]{1,0:T(8,128)S(1)} %slice.4), channel_id=1, source_target_pairs={{0,128},{128,0},{1,129},{129,1},{2,130},{130,2},{3,131},{131,3},{4... | collective-permute-start | bytes 98312 | tf_op jit(solution)/shard_map/ppermute | solution.py:645

commit v7 on v6

--- a/solution.py
+++ b/solution.py
@@ -122,14 +122,19 @@
     each_sign(place[0] >= 32, take)
 
 
+def hold_kernel(f, after, held, sem):
+    del after
+    copy = pltpu.make_async_copy(f, held, sem)
+    copy.start()
+    copy.wait()
+
+
 def inside_kernel(
-    place, f, f_near, rate, kept, kept_edge, groups, held, held_near, held_rate, sem, sem_near,
-    sem_rate,
+    place, held, f_near, rate, kept, kept_edge, groups, held_near, held_rate, sem_near, sem_rate
 ):
     rate_copy = pltpu.make_async_copy(rate, held_rate, sem_rate)
     rate_copy.start()
     for piece in range(STEPS):
-        load_piece(f, held, sem, piece).start()
         load_piece(f_near, held_near, sem_near, piece).start()
     rate_copy.wait()
     device = place[0]
@@ -174,7 +179,6 @@
             return carry
 
         def piece(p, carry):
-            load_piece(f, held, sem, p).wait()
             load_piece(f_near, held_near, sem_near, p).wait()
             for c in range(STEP_CHUNKS):
                 chunk(p * STEP_CHUNKS + c, carry)
@@ -591,7 +595,7 @@
 def body(distribution, collision_rate):
     device = lax.axis_index(VERT)
     place = device.astype(jnp.int32).reshape(1)
-    f_edge = pl.pallas_call(
+    rows = pl.pallas_call(
         send_kernel,
         out_shape=f32(VEL_LOCAL, 2, LANES),
         in_specs=[smem(), hbm()],
@@ -601,27 +605,35 @@
         cost_estimate=pl.CostEstimate(flops=0, bytes_accessed=600000, transcendentals=0),
         name="send_rows",
     )(place, in_hbm(distribution))
-    f_edge = lax.ppermute(f_edge, "gx", SWAP)
+    f_edge = lax.ppermute(rows, "gx", SWAP)
+    held = pl.pallas_call(
+        hold_kernel,
+        out_shape=f32(VEL_LOCAL, ROWS, LANES),
+        in_specs=[hbm(), anywhere()],
+        out_specs=vmem(),
+        scratch_shapes=[pltpu.SemaphoreType.DMA],
+        compiler_params=pltpu.CompilerParams(vmem_limit_bytes=16 * 2**20),
+        cost_estimate=pl.CostEstimate(flops=0, bytes_accessed=4000000, transcendentals=0),
+        name="hold",
+    )(in_hbm(distribution), rows)
     f_near = lax.ppermute(distribution, "gy", SWAP)
     kept, kept_edge, groups = pl.pallas_call(
         inside_kernel,
         out_shape=(
             f32(VEL_LOCAL, ROWS, LANES), f32(VEL_LOCAL, 2, LANES), f32(GROUPS, 6, ROWS, LANES)
         ),
-        in_specs=[smem(), hbm(), hbm(), hbm()],
+        in_specs=[smem(), vmem(), hbm(), hbm()],
         out_specs=(vmem(), vmem(), vmem()),
         scratch_shapes=[
             pltpu.VMEM((VEL_LOCAL, ROWS, LANES), jnp.float32),
-            pltpu.VMEM((VEL_LOCAL, ROWS, LANES), jnp.float32),
             pltpu.VMEM((ROWS, LANES), jnp.float32),
-            pltpu.SemaphoreType.DMA((STEPS,)),
             pltpu.SemaphoreType.DMA((STEPS,)),
             pltpu.SemaphoreType.DMA,
         ],
         compiler_params=pltpu.CompilerParams(vmem_limit_bytes=16 * 2**20),
         cost_estimate=pl.CostEstimate(flops=50000000, bytes_accessed=6000000, transcendentals=0),
         name="move_inside",
-    )(place, in_hbm(distribution), in_hbm(f_near), in_hbm(collision_rate))
+    )(place, held, in_hbm(f_near), in_hbm(collision_rate))
     kept_edge = lax.ppermute(kept_edge, "gx", SWAP)
     kept, partial = pl.pallas_call(
         edge_kernel,

time: 62.6 us -> 62.3 us (level)
  Pallas kernels: 14.1 us -> 15.3 us
  starting transfers between devices: 22.5 us -> 21.4 us
  waiting for transfers between devices: 7.81 us -> 6.89 us
    ppermute x1, waiting for transfers between devices: 1.68 us -> 0.1 us  [body(): f_near = lax.ppermute(distribution, 'gy', SWAP)]
    pallas_call x0 -> x1, Pallas kernels: none -> 1.58 us  [body(): pl.pallas_call(hold_kernel, out_shape=f32(VEL_LOCAL, ROWS, LANES), in_spe...]
    all_to_all x1, blocking collectives: 8.78 us -> 9.47 us  [sum_over_vert(): share = jnp.sum(lax.all_to_all(parts, PLANE, 0, 0), axis=0)]
    ppermute x1, starting transfers between devices: 2.62 us -> 1.95 us  [body(): kept_edge = lax.ppermute(kept_edge, 'gx', SWAP)]
    all_to_all x1, waiting for transfers between devices: 6.11 us -> 6.78 us  [sum_over_vert(): lax.all_to_all(jnp.broadcast_to(share[None], parts.shape), 'z', 0, 0)]
  transfers between devices with their start and end apart: 7 -> 7, of which waited for: 2 -> 2; matrix products, arithmetic and copies ran while one was open for 1% -> 1% of each run, Pallas kernels for 17% -> 19%
where the time goes in v7:
time: 62.3 us; the launch traced here: 62 us
  starting transfers between devices  21.4 us (34%)
  blocking collectives  17.4 us (28%)
  Pallas kernels  15.3 us (25%)
  waiting for transfers between devices  6.89 us (11%)
  local copies, waits for them, and re-layouts  0.71 us (1%)
    all_to_all x1, blocking collectives, sum_over_vert(): share = jnp.sum(lax.all_to_all(parts, PLANE, 0, 0), axis=0)  9.47 us
    all_to_all x1, starting transfers between devices, sum_over_vert(): lax.all_to_all(jnp.broadcast_to(share[None], parts.shape), 'z', 0, 0)  8.19 us
    all_to_all x1, blocking collectives, sum_over_vert(): lax.all_to_all(jnp.broadcast_to(share[None], parts.shape), PLANE, 0, 0)  7.93 us
    all_to_all x1, waiting for transfers between devices, sum_over_vert(): lax.all_to_all(jnp.broadcast_to(share[None], parts.shape), 'z', 0, 0)  6.78 us
    ppermute x1, starting transfers between devices, body(): total_near = lax.ppermute(total, 'gy', SWAP)  4.34 us
    pallas_call x1, Pallas kernels, body(): pl.pallas_call(inside_kernel, out_shape=(f32(VEL_LOCAL, ROWS, LANES), f32...  4.18 us
    pallas_call x1, Pallas kernels, body(): pl.pallas_call(second_inside_kernel, out_shape=f32(VEL_LOCAL, ROWS, LANES...  3.74 us
    ppermute x1, starting transfers between devices, body(): f_near = lax.ppermute(distribution, 'gy', SWAP)  3.24 us
  transfers between devices with their start and end apart: 7, of which 2 were waited for; matrix products, arithmetic and copies ran while one was open for 1% of the time, Pallas kernels for 19%

profile of v7, /device:TPU:1, one launch (start us, length us, event | category | flops | bytes accessed | tf_op | source)
XLA Modules:
  0.0 62.0 jit_solution(8134416149819363353)
XLA Ops:
  0.0 3.2 %collective-permute-start = (f32[125,32,128]{2,1,0:T(8,128)}, f32[125,32,128]{2,1,0:T(8,128)}, u32[]{:S(2)}, u32[]{:S(2)}) collective-permute-start(f32[125,32,128]{2,1,0:T(8,128)} %f.3), channel_id=1, source_target_pairs={{0,64},{64,0},{1,65},{65,1},{2,66},{66,2},{3,67},{67,3},{4,68},{68... | collective-permute-start | bytes 6144008 | tf_op jit(solution)/shard_map/ppermute | solution.py:619
  3.2 1.1 %send_rows.1.after = f32[125,2,128]{2,1,0:T(2,128)S(1)} custom-call(s32[1]{0:T(128)} %bitcast.place, f32[125,32,128]{2,1,0:T(8,128)} %f.3), custom_call_target="tpu_custom_call" | custom-call | bytes 600000 | tf_op jit(solution)/shard_map/send_rows/pallas_call | solution.py:598
  4.3 1.3 %collective-permute-start.1 = (f32[125,2,128]{2,1,0:T(2,128)S(1)}, f32[125,2,128]{2,1,0:T(2,128)S(1)}, u32[]{:S(2)}, u32[]{:S(2)}) collective-permute-start(f32[125,2,128]{2,1,0:T(2,128)S(1)} %send_rows.1.after), channel_id=1, source_target_pairs={{0,128},{128,0},{1,129},{129,1},{2,130},{130,2},{3,131},{131,3},{4... | collective-permute-start | bytes 384008 | tf_op jit(solution)/shard_map/ppermute | solution.py:608
  5.6 1.6 %hold.1.held = f32[125,32,128]{2,1,0:T(8,128)S(1)} custom-call(f32[125,32,128]{2,1,0:T(8,128)} %f.3, f32[125,2,128]{2,1,0:T(2,128)S(1)} %send_rows.1.after), custom_call_target="tpu_custom_call" | custom-call | bytes 4000000 | tf_op jit(solution)/shard_map/hold/pallas_call | solution.py:609
  7.2 0.0 copy-start
  7.2 0.1 collective-permute-done.f_near
  7.3 4.2 %move_inside.1 = (f32[125,32,128]{2,1,0:T(8,128)S(1)}, f32[125,2,128]{2,1,0:T(2,128)S(1)}, f32[7,6,32,128]{3,2,1,0:T(8,128)S(1)}) custom-call(s32[1]{0:T(128)} %bitcast.place, f32[125,32,128]{2,1,0:T(8,128)S(1)} %hold.1.held, f32[125,32,128]{2,1,0:T(8,128)} %collective-permute-done.f_near, f32[32,128]{1,0:T(8,128)} %rate.7), custom_call_target="tpu_custom_call" | custom-call | flops 50000000 | bytes 6000000 | tf_op jit(solution)/shard_map/move_inside/pallas_call | solution.py:620
  11.5 0.0 collective-permute-done.1.f_edge
  11.5 0.0 copy-done
  11.5 1.8 %enter_and_sum.1 = (f32[125,32,128]{2,1,0:T(8,128)S(1)}, f32[384,128]{1,0:T(8,128)S(1)}) custom-call(s32[1]{0:T(128)} %bitcast.place, f32[125,32,128]{2,1,0:T(8,128)S(1)} %get-tuple-element.18.kept_in, f32[7,6,32,128]{3,2,1,0:T(8,128)S(1)} %get-tuple-element.19.groups_in, ...), custom_call_target="tpu_custom_call", output_to_operand_aliasing={{0}: (1, {})} | custom-call | tf_op jit(solution)/shard_map/enter_and_sum/pallas_call | solution.py:638
  13.3 0.5 collective-permute-start.2
  13.8 9.5 %all_to_all.15 = f32[8,6,8,128]{3,2,1,0:T(8,128)S(1)} all-to-all(f32[8,6,8,128]{3,2,1,0:T(8,128)S(1)} %bitcast.7), channel_id=1, replica_groups=mesh['gx'=2,'gy'=2,'x'=4,'yl'=2,'z'=8] {'x','yl'}, dimensions={0} | all-to-all | bytes 393216 | tf_op jit(solution)/shard_map/all_to_all | solution.py:570
  23.2 0.7 %broadcast_in_dim.4 = f32[8,6,8,128]{3,2,1,0:T(8,128)} broadcast(f32[6,8,128]{2,1,0:T(8,128)S(1)} %reduce_sum.18), dimensions={1,2,3} | broadcast | bytes 221184 | tf_op jit(solution)/shard_map/broadcast_in_dim | solution.py:571
  23.9 8.2 %all-to-all-start.1 = ((f32[8,6,8,128]{3,2,1,0:T(8,128)}), f32[8,6,8,128]{3,2,1,0:T(8,128)S(1)}, u32[]{:S(2)}, u32[]{:S(2)}) async-start(f32[8,6,8,128]{3,2,1,0:T(8,128)} %broadcast_in_dim.4), calls=%async_computation.1 | async-start | bytes 393216 | tf_op jit(solution)/shard_map/all_to_all | solution.py:571
  32.1 2.0 %collective-permute-start.3 = (f32[125,2,128]{2,1,0:T(2,128)S(1)}, f32[125,2,128]{2,1,0:T(2,128)S(1)}, u32[]{:S(2)}, u32[]{:S(2)}) collective-permute-start(f32[125,2,128]{2,1,0:T(2,128)S(1)} %get-tuple-element.22), channel_id=1, source_target_pairs={{0,128},{128,0},{1,129},{129,1},{2,130},{130,2},{3,131},{131,3},{4... | collective-permute-start | bytes 384008 | tf_op jit(solution)/shard_map/ppermute | solution.py:637
  34.1 6.8 %all-to-all-done.1 = f32[8,6,8,128]{3,2,1,0:T(8,128)S(1)} async-done(((f32[8,6,8,128]{3,2,1,0:T(8,128)}), f32[8,6,8,128]{3,2,1,0:T(8,128)S(1)}, u32[]{:S(2)}, u32[]{:S(2)}) %all-to-all-start.1) | async-done | bytes 196640 | tf_op jit(solution)/shard_map/all_to_all | solution.py:571
  40.9 0.0 collective-permute-done.3.kept_edge
  40.9 7.9 %all_to_all.16 = f32[8,6,8,128]{3,2,1,0:T(8,128)S(1)} all-to-all(f32[8,6,8,128]{3,2,1,0:T(8,128)S(1)} %broadcast_in_dim.5), channel_id=1, replica_groups=mesh['gx'=2,'gy'=2,'x'=4,'yl'=2,'z'=8] {'x','yl'}, dimensions={0} | all-to-all | bytes 393216 | tf_op jit(solution)/shard_map/all_to_all | solution.py:573
  48.8 4.3 %collective-permute-start.4 = (f32[384,128]{1,0:T(8,128)S(1)}, f32[384,128]{1,0:T(8,128)S(1)}, u32[]{:S(2)}, u32[]{:S(2)}) collective-permute-start(f32[384,128]{1,0:T(8,128)S(1)} %bitcast.3), channel_id=1, source_target_pairs={{0,64},{64,0},{1,65},{65,1},{2,66},{66,2},{3,67},{67,3},{4,68},{68... | collective-permute-start | bytes 589832 | tf_op jit(solution)/shard_map/ppermute | solution.py:656
  53.2 2.0 %collective-permute-start.5 = (f32[64,128]{1,0:T(8,128)S(1)}, f32[64,128]{1,0:T(8,128)S(1)}, u32[]{:S(2)}, u32[]{:S(2)}) collective-permute-start(f32[64,128]{1,0:T(8,128)S(1)} %slice.4), channel_id=1, source_target_pairs={{0,128},{128,0},{1,129},{129,1},{2,130},{130,2},{3,131},{131,3},{4... | collective-permute-start | bytes 98312 | tf_op jit(solution)/shard_map/ppermute | solution.py:657
  55.2 0.5 tables_own.1
  55.7 0.0 collective-permute-done.4.total.total_near
  55.8 0.4 tables_near.1
  56.2 0.0 collective-permute-done.2.kept_near
  56.2 3.7 %move_inside_two.1.moved_part = f32[125,32,128]{2,1,0:T(8,128)S(1)} custom-call(s32[1]{0:T(128)} %bitcast.place, f32[125,32,128]{2,1,0:T(8,128)S(1)} %get-tuple-element.20.kept, f32[125,32,128]{2,1,0:T(8,128)} %collective-permute-done.2.kept_near, f32[32,128]{1,0:T(8,128)S(1)} %get-tuple-element.24.base, f32[3,20,32,128]{3,2,1,0:T(8,128)S(1)} %get-tuple-element.25.tables, ...), custom_call_target="tpu_custom_call" | custom-call | flops 50000000 | bytes 6000000 | tf_op jit(solution)/shard_map/move_inside_two/pallas_call | solution.py:660
  59.9 0.0 collective-permute-done.5.total_edge
  59.9 2.0 %collide_two.1 = f32[125,32,128]{2,1,0:T(8,128)} custom-call(s32[1]{0:T(128)} %bitcast.place, f32[125,32,128]{2,1,0:T(8,128)S(1)} %move_inside_two.1.moved_part, f32[125,2,128]{2,1,0:T(2,128)S(1)} %collective-permute-done.3.kept_edge, f32[384,128]{1,0:T(8,128)S(1)} %bitcast.6, f32[384,128]{1,0:T(8,128)S(1)} %collective-permute-done.4.total.total_near, ...), custom_call_target="tpu_custom_call" | custom-call | tf_op jit(solution)/shard_map/collide_two/pallas_call | solution.py:673
  (4 shorter events, 0.0 us)
Async XLA Ops:
  0.0 7.3 %collective-permute-start = (f32[125,32,128]{2,1,0:T(8,128)}, f32[125,32,128]{2,1,0:T(8,128)}, u32[]{:S(2)}, u32[]{:S(2)}) collective-permute-start(f32[125,32,128]{2,1,0:T(8,128)} %f.3), channel_id=1, source_target_pairs={{0,64},{64,0},{1,65},{65,1},{2,66},{66,2},{3,67},{67,3},{4,68},{68... | collective-permute-start | bytes 6144008 | tf_op jit(solution)/shard_map/ppermute | solution.py:619
  4.3 7.2 %collective-permute-start.1 = (f32[125,2,128]{2,1,0:T(2,128)S(1)}, f32[125,2,128]{2,1,0:T(2,128)S(1)}, u32[]{:S(2)}, u32[]{:S(2)}) collective-permute-start(f32[125,2,128]{2,1,0:T(2,128)S(1)} %send_rows.1.after), channel_id=1, source_target_pairs={{0,128},{128,0},{1,129},{129,1},{2,130},{130,2},{3,131},{131,3},{4... | collective-permute-start | bytes 384008 | tf_op jit(solution)/shard_map/ppermute | solution.py:608
  7.2 4.3 %copy-start = (f32[32,128]{1,0:T(8,128)S(1)}, f32[32,128]{1,0:T(8,128)}, u32[]{:S(2)}) copy-start(f32[32,128]{1,0:T(8,128)} %rate.7) | copy-start | bytes 49156
  13.3 42.9 %collective-permute-start.2 = (f32[125,32,128]{2,1,0:T(8,128)S(1)}, f32[125,32,128]{2,1,0:T(8,128)}, u32[]{:S(2)}, u32[]{:S(2)}) collective-permute-start(f32[125,32,128]{2,1,0:T(8,128)S(1)} %get-tuple-element.20.kept), channel_id=1, source_target_pairs={{0,64},{64,0},{1,65},{65,1},{2,66},{66,2},{3,67},{67,3},{4,68},{68... | collective-permute-start | bytes 6144008 | tf_op jit(solution)/shard_map/ppermute | solution.py:654
  23.9 16.9 %all-to-all-start.1 = ((f32[8,6,8,128]{3,2,1,0:T(8,128)}), f32[8,6,8,128]{3,2,1,0:T(8,128)S(1)}, u32[]{:S(2)}, u32[]{:S(2)}) async-start(f32[8,6,8,128]{3,2,1,0:T(8,128)} %broadcast_in_dim.4), calls=%async_computation.1 | async-start | bytes 393216 | tf_op jit(solution)/shard_map/all_to_all | solution.py:571
  32.1 8.8 %collective-permute-start.3 = (f32[125,2,128]{2,1,0:T(2,128)S(1)}, f32[125,2,128]{2,1,0:T(2,128)S(1)}, u32[]{:S(2)}, u32[]{:S(2)}) collective-permute-start(f32[125,2,128]{2,1,0:T(2,128)S(1)} %get-tuple-element.22), channel_id=1, source_target_pairs={{0,128},{128,0},{1,129},{129,1},{2,130},{130,2},{3,131},{131,3},{4... | collective-permute-start | bytes 384008 | tf_op jit(solution)/shard_map/ppermute | solution.py:637
  48.8 6.9 %collective-permute-start.4 = (f32[384,128]{1,0:T(8,128)S(1)}, f32[384,128]{1,0:T(8,128)S(1)}, u32[]{:S(2)}, u32[]{:S(2)}) collective-permute-start(f32[384,128]{1,0:T(8,128)S(1)} %bitcast.3), channel_id=1, source_target_pairs={{0,64},{64,0},{1,65},{65,1},{2,66},{66,2},{3,67},{67,3},{4,68},{68... | collective-permute-start | bytes 589832 | tf_op jit(solution)/shard_map/ppermute | solution.py:656
  53.2 6.7 %collective-permute-start.5 = (f32[64,128]{1,0:T(8,128)S(1)}, f32[64,128]{1,0:T(8,128)S(1)}, u32[]{:S(2)}, u32[]{:S(2)}) collective-permute-start(f32[64,128]{1,0:T(8,128)S(1)} %slice.4), channel_id=1, source_target_pairs={{0,128},{128,0},{1,129},{129,1},{2,130},{130,2},{3,131},{131,3},{4... | collective-permute-start | bytes 98312 | tf_op jit(solution)/shard_map/ppermute | solution.py:657

commit v8 on v7

--- a/solution.py
+++ b/solution.py
@@ -195,7 +195,6 @@
     del kept_in
     device = place[0]
     first = device * VEL_LOCAL
-    groups[...] = groups_in[...]
     even = lax.rem(lane_index(), 2) == 0
     keep = 1.0 - rate[...]
 
@@ -206,6 +205,7 @@
         band = kept.at[:, pl.ds(0 if forward else 24, 8)]
         load = pltpu.make_async_copy(band, edge, sem)
         load.start()
+        groups[...] = groups_in[...]
         load.wait()
 
         def chunk(c, carry):

time: 62.3 us -> 62.3 us (level)
  no operation moved by 1% of the time
where the time goes in v8:
time: 62.3 us; the launch traced here: 62 us
  starting transfers between devices  21.4 us (34%)
  blocking collectives  17.4 us (28%)
  Pallas kernels  15.3 us (25%)
  waiting for transfers between devices  6.89 us (11%)
  local copies, waits for them, and re-layouts  0.71 us (1%)
    all_to_all x1, blocking collectives, sum_over_vert(): share = jnp.sum(lax.all_to_all(parts, PLANE, 0, 0), axis=0)  9.47 us
    all_to_all x1, starting transfers between devices, sum_over_vert(): lax.all_to_all(jnp.broadcast_to(share[None], parts.shape), 'z', 0, 0)  8.19 us
    all_to_all x1, blocking collectives, sum_over_vert(): lax.all_to_all(jnp.broadcast_to(share[None], parts.shape), PLANE, 0, 0)  7.93 us
    all_to_all x1, waiting for transfers between devices, sum_over_vert(): lax.all_to_all(jnp.broadcast_to(share[None], parts.shape), 'z', 0, 0)  6.78 us
    ppermute x1, starting transfers between devices, body(): total_near = lax.ppermute(total, 'gy', SWAP)  4.34 us
    pallas_call x1, Pallas kernels, body(): pl.pallas_call(inside_kernel, out_shape=(f32(VEL_LOCAL, ROWS, LANES), f32...  4.18 us
    pallas_call x1, Pallas kernels, body(): pl.pallas_call(second_inside_kernel, out_shape=f32(VEL_LOCAL, ROWS, LANES...  3.74 us
    ppermute x1, starting transfers between devices, body(): f_near = lax.ppermute(distribution, 'gy', SWAP)  3.24 us
  transfers between devices with their start and end apart: 7, of which 2 were waited for; matrix products, arithmetic and copies ran while one was open for 1% of the time, Pallas kernels for 19%

profile of v8, /device:TPU:1, one launch (start us, length us, event | category | flops | bytes accessed | tf_op | source)
XLA Modules:
  0.0 62.0 jit_solution(10243832969707616160)
XLA Ops:
  0.0 3.2 %collective-permute-start = (f32[125,32,128]{2,1,0:T(8,128)}, f32[125,32,128]{2,1,0:T(8,128)}, u32[]{:S(2)}, u32[]{:S(2)}) collective-permute-start(f32[125,32,128]{2,1,0:T(8,128)} %f.3), channel_id=1, source_target_pairs={{0,64},{64,0},{1,65},{65,1},{2,66},{66,2},{3,67},{67,3},{4,68},{68... | collective-permute-start | bytes 6144008 | tf_op jit(solution)/shard_map/ppermute | solution.py:619
  3.2 1.1 %send_rows.1.after = f32[125,2,128]{2,1,0:T(2,128)S(1)} custom-call(s32[1]{0:T(128)} %bitcast.place, f32[125,32,128]{2,1,0:T(8,128)} %f.3), custom_call_target="tpu_custom_call" | custom-call | bytes 600000 | tf_op jit(solution)/shard_map/send_rows/pallas_call | solution.py:598
  4.3 1.3 %collective-permute-start.1 = (f32[125,2,128]{2,1,0:T(2,128)S(1)}, f32[125,2,128]{2,1,0:T(2,128)S(1)}, u32[]{:S(2)}, u32[]{:S(2)}) collective-permute-start(f32[125,2,128]{2,1,0:T(2,128)S(1)} %send_rows.1.after), channel_id=1, source_target_pairs={{0,128},{128,0},{1,129},{129,1},{2,130},{130,2},{3,131},{131,3},{4... | collective-permute-start | bytes 384008 | tf_op jit(solution)/shard_map/ppermute | solution.py:608
  5.6 1.6 %hold.1.held = f32[125,32,128]{2,1,0:T(8,128)S(1)} custom-call(f32[125,32,128]{2,1,0:T(8,128)} %f.3, f32[125,2,128]{2,1,0:T(2,128)S(1)} %send_rows.1.after), custom_call_target="tpu_custom_call" | custom-call | bytes 4000000 | tf_op jit(solution)/shard_map/hold/pallas_call | solution.py:609
  7.2 0.0 copy-start
  7.2 0.1 collective-permute-done.f_near
  7.3 4.2 %move_inside.1 = (f32[125,32,128]{2,1,0:T(8,128)S(1)}, f32[125,2,128]{2,1,0:T(2,128)S(1)}, f32[7,6,32,128]{3,2,1,0:T(8,128)S(1)}) custom-call(s32[1]{0:T(128)} %bitcast.place, f32[125,32,128]{2,1,0:T(8,128)S(1)} %hold.1.held, f32[125,32,128]{2,1,0:T(8,128)} %collective-permute-done.f_near, f32[32,128]{1,0:T(8,128)} %rate.7), custom_call_target="tpu_custom_call" | custom-call | flops 50000000 | bytes 6000000 | tf_op jit(solution)/shard_map/move_inside/pallas_call | solution.py:620
  11.5 0.0 collective-permute-done.1.f_edge
  11.5 0.0 copy-done
  11.5 1.8 %enter_and_sum.1 = (f32[125,32,128]{2,1,0:T(8,128)S(1)}, f32[384,128]{1,0:T(8,128)S(1)}) custom-call(s32[1]{0:T(128)} %bitcast.place, f32[125,32,128]{2,1,0:T(8,128)S(1)} %get-tuple-element.18.kept_in, f32[7,6,32,128]{3,2,1,0:T(8,128)S(1)} %get-tuple-element.19.groups_in, ...), custom_call_target="tpu_custom_call", output_to_operand_aliasing={{0}: (1, {})} | custom-call | tf_op jit(solution)/shard_map/enter_and_sum/pallas_call | solution.py:638
  13.3 0.5 collective-permute-start.2
  13.8 9.5 %all_to_all.15 = f32[8,6,8,128]{3,2,1,0:T(8,128)S(1)} all-to-all(f32[8,6,8,128]{3,2,1,0:T(8,128)S(1)} %bitcast.7), channel_id=1, replica_groups=mesh['gx'=2,'gy'=2,'x'=4,'yl'=2,'z'=8] {'x','yl'}, dimensions={0} | all-to-all | bytes 393216 | tf_op jit(solution)/shard_map/all_to_all | solution.py:570
  23.2 0.7 %broadcast_in_dim.4 = f32[8,6,8,128]{3,2,1,0:T(8,128)} broadcast(f32[6,8,128]{2,1,0:T(8,128)S(1)} %reduce_sum.18), dimensions={1,2,3} | broadcast | bytes 221184 | tf_op jit(solution)/shard_map/broadcast_in_dim | solution.py:571
  23.9 8.2 %all-to-all-start.1 = ((f32[8,6,8,128]{3,2,1,0:T(8,128)}), f32[8,6,8,128]{3,2,1,0:T(8,128)S(1)}, u32[]{:S(2)}, u32[]{:S(2)}) async-start(f32[8,6,8,128]{3,2,1,0:T(8,128)} %broadcast_in_dim.4), calls=%async_computation.1 | async-start | bytes 393216 | tf_op jit(solution)/shard_map/all_to_all | solution.py:571
  32.1 2.0 %collective-permute-start.3 = (f32[125,2,128]{2,1,0:T(2,128)S(1)}, f32[125,2,128]{2,1,0:T(2,128)S(1)}, u32[]{:S(2)}, u32[]{:S(2)}) collective-permute-start(f32[125,2,128]{2,1,0:T(2,128)S(1)} %get-tuple-element.22), channel_id=1, source_target_pairs={{0,128},{128,0},{1,129},{129,1},{2,130},{130,2},{3,131},{131,3},{4... | collective-permute-start | bytes 384008 | tf_op jit(solution)/shard_map/ppermute | solution.py:637
  34.1 6.8 %all-to-all-done.1 = f32[8,6,8,128]{3,2,1,0:T(8,128)S(1)} async-done(((f32[8,6,8,128]{3,2,1,0:T(8,128)}), f32[8,6,8,128]{3,2,1,0:T(8,128)S(1)}, u32[]{:S(2)}, u32[]{:S(2)}) %all-to-all-start.1) | async-done | bytes 196640 | tf_op jit(solution)/shard_map/all_to_all | solution.py:571
  40.9 0.0 collective-permute-done.3.kept_edge
  40.9 7.9 %all_to_all.16 = f32[8,6,8,128]{3,2,1,0:T(8,128)S(1)} all-to-all(f32[8,6,8,128]{3,2,1,0:T(8,128)S(1)} %broadcast_in_dim.5), channel_id=1, replica_groups=mesh['gx'=2,'gy'=2,'x'=4,'yl'=2,'z'=8] {'x','yl'}, dimensions={0} | all-to-all | bytes 393216 | tf_op jit(solution)/shard_map/all_to_all | solution.py:573
  48.8 4.3 %collective-permute-start.4 = (f32[384,128]{1,0:T(8,128)S(1)}, f32[384,128]{1,0:T(8,128)S(1)}, u32[]{:S(2)}, u32[]{:S(2)}) collective-permute-start(f32[384,128]{1,0:T(8,128)S(1)} %bitcast.3), channel_id=1, source_target_pairs={{0,64},{64,0},{1,65},{65,1},{2,66},{66,2},{3,67},{67,3},{4,68},{68... | collective-permute-start | bytes 589832 | tf_op jit(solution)/shard_map/ppermute | solution.py:656
  53.2 2.0 %collective-permute-start.5 = (f32[64,128]{1,0:T(8,128)S(1)}, f32[64,128]{1,0:T(8,128)S(1)}, u32[]{:S(2)}, u32[]{:S(2)}) collective-permute-start(f32[64,128]{1,0:T(8,128)S(1)} %slice.4), channel_id=1, source_target_pairs={{0,128},{128,0},{1,129},{129,1},{2,130},{130,2},{3,131},{131,3},{4... | collective-permute-start | bytes 98312 | tf_op jit(solution)/shard_map/ppermute | solution.py:657
  55.2 0.5 tables_own.1
  55.7 0.0 collective-permute-done.4.total.total_near
  55.8 0.4 tables_near.1
  56.2 0.0 collective-permute-done.2.kept_near
  56.2 3.7 %move_inside_two.1.moved_part = f32[125,32,128]{2,1,0:T(8,128)S(1)} custom-call(s32[1]{0:T(128)} %bitcast.place, f32[125,32,128]{2,1,0:T(8,128)S(1)} %get-tuple-element.20.kept, f32[125,32,128]{2,1,0:T(8,128)} %collective-permute-done.2.kept_near, f32[32,128]{1,0:T(8,128)S(1)} %get-tuple-element.24.base, f32[3,20,32,128]{3,2,1,0:T(8,128)S(1)} %get-tuple-element.25.tables, ...), custom_call_target="tpu_custom_call" | custom-call | flops 50000000 | bytes 6000000 | tf_op jit(solution)/shard_map/move_inside_two/pallas_call | solution.py:660
  59.9 0.0 collective-permute-done.5.total_edge
  59.9 2.0 %collide_two.1 = f32[125,32,128]{2,1,0:T(8,128)} custom-call(s32[1]{0:T(128)} %bitcast.place, f32[125,32,128]{2,1,0:T(8,128)S(1)} %move_inside_two.1.moved_part, f32[125,2,128]{2,1,0:T(2,128)S(1)} %collective-permute-done.3.kept_edge, f32[384,128]{1,0:T(8,128)S(1)} %bitcast.6, f32[384,128]{1,0:T(8,128)S(1)} %collective-permute-done.4.total.total_near, ...), custom_call_target="tpu_custom_call" | custom-call | tf_op jit(solution)/shard_map/collide_two/pallas_call | solution.py:673
  (4 shorter events, 0.0 us)
Async XLA Ops:
  0.0 7.3 %collective-permute-start = (f32[125,32,128]{2,1,0:T(8,128)}, f32[125,32,128]{2,1,0:T(8,128)}, u32[]{:S(2)}, u32[]{:S(2)}) collective-permute-start(f32[125,32,128]{2,1,0:T(8,128)} %f.3), channel_id=1, source_target_pairs={{0,64},{64,0},{1,65},{65,1},{2,66},{66,2},{3,67},{67,3},{4,68},{68... | collective-permute-start | bytes 6144008 | tf_op jit(solution)/shard_map/ppermute | solution.py:619
  4.3 7.2 %collective-permute-start.1 = (f32[125,2,128]{2,1,0:T(2,128)S(1)}, f32[125,2,128]{2,1,0:T(2,128)S(1)}, u32[]{:S(2)}, u32[]{:S(2)}) collective-permute-start(f32[125,2,128]{2,1,0:T(2,128)S(1)} %send_rows.1.after), channel_id=1, source_target_pairs={{0,128},{128,0},{1,129},{129,1},{2,130},{130,2},{3,131},{131,3},{4... | collective-permute-start | bytes 384008 | tf_op jit(solution)/shard_map/ppermute | solution.py:608
  7.2 4.3 %copy-start = (f32[32,128]{1,0:T(8,128)S(1)}, f32[32,128]{1,0:T(8,128)}, u32[]{:S(2)}) copy-start(f32[32,128]{1,0:T(8,128)} %rate.7) | copy-start | bytes 49156
  13.3 42.9 %collective-permute-start.2 = (f32[125,32,128]{2,1,0:T(8,128)S(1)}, f32[125,32,128]{2,1,0:T(8,128)}, u32[]{:S(2)}, u32[]{:S(2)}) collective-permute-start(f32[125,32,128]{2,1,0:T(8,128)S(1)} %get-tuple-element.20.kept), channel_id=1, source_target_pairs={{0,64},{64,0},{1,65},{65,1},{2,66},{66,2},{3,67},{67,3},{4,68},{68... | collective-permute-start | bytes 6144008 | tf_op jit(solution)/shard_map/ppermute | solution.py:654
  23.9 16.9 %all-to-all-start.1 = ((f32[8,6,8,128]{3,2,1,0:T(8,128)}), f32[8,6,8,128]{3,2,1,0:T(8,128)S(1)}, u32[]{:S(2)}, u32[]{:S(2)}) async-start(f32[8,6,8,128]{3,2,1,0:T(8,128)} %broadcast_in_dim.4), calls=%async_computation.1 | async-start | bytes 393216 | tf_op jit(solution)/shard_map/all_to_all | solution.py:571
  32.1 8.8 %collective-permute-start.3 = (f32[125,2,128]{2,1,0:T(2,128)S(1)}, f32[125,2,128]{2,1,0:T(2,128)S(1)}, u32[]{:S(2)}, u32[]{:S(2)}) collective-permute-start(f32[125,2,128]{2,1,0:T(2,128)S(1)} %get-tuple-element.22), channel_id=1, source_target_pairs={{0,128},{128,0},{1,129},{129,1},{2,130},{130,2},{3,131},{131,3},{4... | collective-permute-start | bytes 384008 | tf_op jit(solution)/shard_map/ppermute | solution.py:637
  48.8 6.9 %collective-permute-start.4 = (f32[384,128]{1,0:T(8,128)S(1)}, f32[384,128]{1,0:T(8,128)S(1)}, u32[]{:S(2)}, u32[]{:S(2)}) collective-permute-start(f32[384,128]{1,0:T(8,128)S(1)} %bitcast.3), channel_id=1, source_target_pairs={{0,64},{64,0},{1,65},{65,1},{2,66},{66,2},{3,67},{67,3},{4,68},{68... | collective-permute-start | bytes 589832 | tf_op jit(solution)/shard_map/ppermute | solution.py:656
  53.2 6.7 %collective-permute-start.5 = (f32[64,128]{1,0:T(8,128)S(1)}, f32[64,128]{1,0:T(8,128)S(1)}, u32[]{:S(2)}, u32[]{:S(2)}) collective-permute-start(f32[64,128]{1,0:T(8,128)S(1)} %slice.4), channel_id=1, source_target_pairs={{0,128},{128,0},{1,129},{129,1},{2,130},{130,2},{3,131},{131,3},{4... | collective-permute-start | bytes 98312 | tf_op jit(solution)/shard_map/ppermute | solution.py:657
